TPU v7x, 128 devices: a whole 4x4x4 slice. The times are simulated.
128 devices in a mesh: space: 16 (over y_hi, z, core), member: 8 (over x, y_lo).
Axes of the slice: x: 4, y: 4 (y_hi: 2, y_lo: 2; y = y_hi * 2 + y_lo), z: 4, core: 2. Of those that a mesh axis runs over, the one named last changes fastest.
Arguments:
- tokens: bfloat16 [16, 32, 256, 1536], P('member', 'space'), may hold values from -6 to 6
- gain: float32 [1536], replicated, may hold values from 0.5 to 1.5
- weight: bfloat16 [1536, 1120], P(('space', 'member')), may hold values from -0.15625 to 0.15625
- bias: float32 [1120], replicated, may hold values from -3 to 3
- target: bfloat16 [70, 128, 1024], P(None, 'space'), may hold values from -6 to 6
- channel_weight: float32 [70], replicated, may hold values from 0.5 to 2
Outputs:
- token_gradient: bfloat16 [16, 32, 256, 1536], P('member', 'space')
- gain_gradient: float32 [1536], replicated
- grad_weight: float32 [1536, 1120], P(('space', 'member'))
- grad_bias: float32 [1120], replicated
All inputs are finite; a program needn't handle non-finite values.
Results may differ from a plain program's by a relative error of at most 0.023.
Values may be sent and summed in bfloat16 or wider, within the bound.
No kernel may reach another device: no remote copies, remote signals or barrier semaphores. Data moves between devices by JAX's collectives and lax.ppermute only.
A program may use at most 192 MiB of HBM per device.

v0:
```python
import jax
import jax.numpy as jnp
from jax import lax
from jax.sharding import PartitionSpec as P

ALPHA = 0.95
DELTA = 0.1
EPS = 1e-05


def latitude_weights(rows):
    index = jnp.arange(rows, dtype=jnp.float32)
    angle = (60.0 - 0.25 * (index + 0.5)) * (jnp.pi / 180.0)
    cosine = jnp.cos(angle)
    return cosine / jnp.mean(cosine)


def token_layout(target):
    chans, grid_rows, grid_cols = target.shape
    shaped = target.reshape(chans, grid_rows // 4, 4, grid_cols // 4, 4)
    shaped = jnp.transpose(shaped, (1, 3, 0, 2, 4))
    return shaped.reshape(grid_rows // 4, grid_cols // 4, chans * 16)


def slope(value):
    return value * lax.rsqrt(value * value + DELTA * DELTA)


def on_device(tokens, gain, weight, bias, target, channel_weight):
    members_here = tokens.shape[0]
    lat_rows = tokens.shape[1]
    n_member = lax.axis_size("member")
    n_space = lax.axis_size("space")
    count = members_here * n_member
    eps_fair = (1.0 - ALPHA) / count
    coef = (1.0 - eps_fair) / (count * (count - 1))
    chans = channel_weight.shape[0]
    wide = tokens.astype(jnp.float32)
    feature_mean = jnp.mean(wide, -1, keepdims=True)
    centred_input = wide - feature_mean
    variance = jnp.mean(centred_input * centred_input, -1, keepdims=True)
    inverse_deviation = lax.rsqrt(variance + EPS)
    standardized_input = centred_input * inverse_deviation
    normed_tokens = (standardized_input * gain).astype(jnp.bfloat16)
    full_weight = lax.all_gather(weight, ("space", "member"), axis=0, tiled=True)
    field = (
        jnp.einsum("mtld,do->mtlo", normed_tokens, full_weight, preferred_element_type=jnp.float32)
        + bias
    ).astype(jnp.bfloat16)
    truth = token_layout(target).astype(jnp.float32)
    all_rows = latitude_weights(4 * lat_rows * n_space)
    latw = lax.dynamic_slice_in_dim(
        all_rows, lax.axis_index("space") * (4 * lat_rows), 4 * lat_rows, 0
    ).reshape(lat_rows, 4)
    table = jnp.broadcast_to(
        channel_weight[None, :, None, None] * latw[:, None, :, None], (lat_rows, chans, 4, 4)
    )
    weights = table.reshape(lat_rows, 1, chans * 16)
    mine = field.astype(jnp.float32)
    others = lax.all_gather(field, "member", axis=0, tiled=True).astype(jnp.float32)
    pairs = jnp.sum(slope(mine[:, None] - others[None]), axis=1)
    dfield = (weights * (slope(mine - truth) / count - coef * pairs)).astype(jnp.bfloat16)
    grad_weight = lax.psum_scatter(
        jnp.einsum("mtld,mtlo->do", normed_tokens, dfield, preferred_element_type=jnp.float32),
        ("space", "member"),
        scatter_dimension=0,
        tiled=True,
    )
    normed_gradient = jnp.einsum(
        "mtlo,do->mtld", dfield, full_weight, preferred_element_type=jnp.float32
    )
    bias_part = jnp.sum(dfield.astype(jnp.float32), axis=(0, 1, 2))
    gain_portion = jnp.sum(normed_gradient * standardized_input, axis=(0, 1, 2))
    grad_bias, gain_gradient = lax.psum((bias_part, gain_portion), ("space", "member"))
    scaled_tokens = normed_gradient * gain
    token_gradient = inverse_deviation * (
        scaled_tokens
        - jnp.mean(scaled_tokens, -1, keepdims=True)
        - standardized_input * jnp.mean(scaled_tokens * standardized_input, -1, keepdims=True)
    )
    return (token_gradient.astype(jnp.bfloat16), gain_gradient, grad_weight, grad_bias)


def solution(mesh):
    return jax.shard_map(
        on_device,
        mesh=mesh,
        in_specs=(
            P("member", "space", None, None),
            P(),
            P(("space", "member"), None),
            P(),
            P(None, "space", None),
            P(),
        ),
        out_specs=(P("member", "space", None, None), P(), P(("space", "member"), None), P()),
        check_vma=False,
    )
```

profile of v0, /device:TPU:0, one launch (start us, length us, event | category | flops | bytes accessed | tf_op | source)
XLA Modules:
  0.0 1317.3 jit_solution(17572682270306615580)
XLA Ops:
  8.0 2.5 convert_reduce_fusion
  11.5 308.0 %all-gather.6.cloned.1.call-done = bf16[128,12,1120]{2,1,0:T(8,128)(2,1)} async-done(((bf16[1,12,1120]{2,1,0:T(8,128)(2,1)}), bf16[128,12,1120]{2,1,0:T(8,128)(2,1)}) %all-gather.6.cloned.1.call-update) | async-done | bytes 3440656 | tf_op jit(solution)/shard_map/all_gather | solution.py:45
  319.5 7.1 reshape.55
  326.6 8.3 fusion.23
  336.9 4.0 copy.38
  340.9 7.0 copy.39
  347.9 3.3 copy.40
  351.2 341.3 %all-gather.4.cloned.1.call-done = bf16[16,2,256,1120]{2,3,1,0:T(8,128)(2,1)} async-done(((bf16[2,2,256,1120]{2,3,1,0:T(8,128)(2,1)}), bf16[16,2,256,1120]{2,3,1,0:T(8,128)(2,1)}) %all-gather.4.cloned.1.call-update) | async-done | bytes 18350096 | tf_op jit(solution)/shard_map/all_gather | solution.py:60
  692.5 20.1 %convert_element_type.48 = f32[16,2,256,1120]{2,3,1,0:T(8,128)} convert(bf16[16,2,256,1120]{2,3,1,0:T(8,128)(2,1)} %all-gather.4.cloned.1.call-done) | non-fusion elementwise | flops 9175040 | bytes 55050240 | tf_op jit(solution)/shard_map/convert_element_type | solution.py:60
  712.6 22.1 %fusion.3 = f32[2,2,256,1120]{2,3,1,0:T(8,128)} fusion(f32[16,2,256,1120]{2,3,1,0:T(8,128)} %convert_element_type.48, f32[2,2,256,1120]{2,3,1,0:T(8,128)} %get-tuple-element.11), kind=kLoop, calls=%fused_computation.4 | loop fusion | flops 90603520 | bytes 45875200 | tf_op jit(solution)/shard_map/reduce_sum | solution.py:61
  734.7 4.6 convert_reduce_fusion.1
  740.7 7.2 convolution_bitcast_fusion
  748.0 372.2 %fusion = f32[16,1120]{1,0:T(8,128)S(1)} fusion(f32[1536,1120]{1,0:T(8,128)} %convolution_bitcast_fusion), kind=kCustom, calls=%all-reduce-scatter | all-reduce-scatter fusion | flops 2293761 | bytes 6952960
  1120.1 2.6 collective-permute-start
  1133.2 7.2 collective-permute-start.16
  1140.4 8.7 collective-permute-start.17
  1149.2 6.1 collective-permute-start.18
  1155.3 4.9 collective-permute-start.19
  1160.3 2.8 collective-permute-start.2
  1163.1 2.1 collective-permute-start.20
  1165.2 2.2 collective-permute-start.21
  1170.9 2.2 collective-permute-start.24
  1177.0 2.8 collective-permute-start.27
  1179.8 8.6 fusion.15
  1192.1 5.1 collective-permute-start.3
  1199.1 4.5 collective-permute-start.4
  1205.7 2.2 collective-permute-start.6
  1209.8 3.6 collective-permute-start.8
  1213.4 2.3 collective-permute-start.9
  1215.7 3.1 fusion.14
  1218.9 63.2 %all-reduce.2 = (f32[1536]{0:T(1024)}, f32[1120]{0:T(1024)}) all-reduce(f32[1536]{0:T(1024)S(1)} %get-tuple-element.4, f32[1120]{0:T(1024)S(1)} %get-tuple-element.9), channel_id=1, replica_groups=mesh['space'=16,'member'=8] {'space','member'}, use_global_device_ids=true, to_apply=%region_7.0 | all-reduce | flops 2656 | bytes 21248 | tf_op jit(solution)/shard_map/psum | solution.py:74
  1282.2 27.6 %concatenate = f32[524,1120]{1,0:T(8,128)S(1)} concatenate(f32[12,1120]{1,0:T(8,128)S(1)} %collective-permute-done.31, f32[16,1120]{1,0:T(8,128)} %copy-done.18, f32[16,1120]{1,0:T(8,128)} %copy-done.16, f32[16,1120]{1,0:T(8,128)} %copy-done.15, f32[16,1120]{1,0:T(8,128)} %copy-done.14, f32[16,1120]{1,0:T(8,128)} %copy-done.13, f32[16,1120]{1,0:T(8,128)} %copy-done.12, ...), dimensions={0} | concatenate | bytes 4695040
  (112 shorter events, 32.2 us)
Async XLA Ops:
  7.2 312.3 %all-gather.6.cloned.1.call-start = ((), (), s32[]{:S(2)}) async-start(), calls=%async_computation.1 | async-start | bytes 4755456 | tf_op jit(solution)/shard_map/all_gather | solution.py:45
  7.9 684.6 %all-gather.4.cloned.1.call-start = ((), (), s32[]{:S(2)}) async-start(), calls=%async_computation | async-start | bytes 20643840 | tf_op jit(solution)/shard_map/all_gather | solution.py:60
  1120.1 9.2 collective-permute-start
  1125.4 6.5 collective-permute-start.10
  1126.7 6.6 collective-permute-start.11
  1128.0 12.4 collective-permute-start.12
  1129.3 19.9 %collective-permute-start.13 = (f32[16,1120]{1,0:T(8,128)S(1)}, f32[16,1120]{1,0:T(8,128)S(1)}, u32[]{:S(2)}, u32[]{:S(2)}) collective-permute-start(f32[16,1120]{1,0:T(8,128)S(1)} %fusion), channel_id=1, source_target_pairs={{0,14},{1,15},{2,16},{3,17},{4,18},{5,19},{6,20},{7,21},{8,22},{9,... | collective-permute-start | bytes 215048
  1130.6 24.7 %collective-permute-start.14 = (f32[16,1120]{1,0:T(8,128)S(1)}, f32[16,1120]{1,0:T(8,128)S(1)}, u32[]{:S(2)}, u32[]{:S(2)}) collective-permute-start(f32[16,1120]{1,0:T(8,128)S(1)} %fusion), channel_id=1, source_target_pairs={{0,15},{1,16},{2,17},{3,18},{4,19},{5,20},{6,21},{7,22},{8,23},{9,... | collective-permute-start | bytes 215048
  1131.9 28.3 %collective-permute-start.15 = (f32[16,1120]{1,0:T(8,128)S(1)}, f32[16,1120]{1,0:T(8,128)S(1)}, u32[]{:S(2)}, u32[]{:S(2)}) collective-permute-start(f32[16,1120]{1,0:T(8,128)S(1)} %fusion), channel_id=1, source_target_pairs={{0,16},{1,17},{2,18},{3,19},{4,20},{5,21},{6,22},{7,23},{8,24},{9,... | collective-permute-start | bytes 215048
  1133.2 29.8 %collective-permute-start.16 = (f32[16,1120]{1,0:T(8,128)S(1)}, f32[16,1120]{1,0:T(8,128)S(1)}, u32[]{:S(2)}, u32[]{:S(2)}) collective-permute-start(f32[16,1120]{1,0:T(8,128)S(1)} %fusion), channel_id=1, source_target_pairs={{0,17},{1,18},{2,19},{3,20},{4,21},{5,22},{6,23},{7,24},{8,25},{9,... | collective-permute-start | bytes 215048
  1140.4 24.8 %collective-permute-start.17 = (f32[16,1120]{1,0:T(8,128)S(1)}, f32[16,1120]{1,0:T(8,128)S(1)}, u32[]{:S(2)}, u32[]{:S(2)}) collective-permute-start(f32[16,1120]{1,0:T(8,128)S(1)} %fusion), channel_id=1, source_target_pairs={{0,18},{1,19},{2,20},{3,21},{4,22},{5,23},{6,24},{7,25},{8,26},{9,... | collective-permute-start | bytes 215048
  1149.2 18.3 %collective-permute-start.18 = (f32[16,1120]{1,0:T(8,128)S(1)}, f32[16,1120]{1,0:T(8,128)S(1)}, u32[]{:S(2)}, u32[]{:S(2)}) collective-permute-start(f32[16,1120]{1,0:T(8,128)S(1)} %fusion), channel_id=1, source_target_pairs={{0,19},{1,20},{2,21},{3,22},{4,23},{5,24},{6,25},{7,26},{8,27},{9,... | collective-permute-start | bytes 215048
  1155.3 14.1 %collective-permute-start.19 = (f32[16,1120]{1,0:T(8,128)S(1)}, f32[16,1120]{1,0:T(8,128)}, u32[]{:S(2)}, u32[]{:S(2)}) collective-permute-start(f32[16,1120]{1,0:T(8,128)S(1)} %fusion), channel_id=1, source_target_pairs={{0,20},{1,21},{2,22},{3,23},{4,24},{5,25},{6,26},{7,27},{8,28},{9,... | collective-permute-start | bytes 215048
  1160.3 10.6 collective-permute-start.2
  1163.1 10.0 collective-permute-start.20
  1165.2 9.8 collective-permute-start.21
  1167.5 9.5 collective-permute-start.22
  1169.4 19.0 %collective-permute-start.23 = (f32[16,1120]{1,0:T(8,128)S(1)}, f32[16,1120]{1,0:T(8,128)S(1)}, u32[]{:S(2)}, u32[]{:S(2)}) collective-permute-start(f32[16,1120]{1,0:T(8,128)S(1)} %fusion), channel_id=1, source_target_pairs={{0,24},{1,25},{2,26},{3,27},{4,28},{5,29},{6,30},{7,31},{8,32},{9,... | collective-permute-start | bytes 215048
  1170.9 19.5 %collective-permute-start.24 = (f32[16,1120]{1,0:T(8,128)S(1)}, f32[16,1120]{1,0:T(8,128)S(1)}, u32[]{:S(2)}, u32[]{:S(2)}) collective-permute-start(f32[16,1120]{1,0:T(8,128)S(1)} %fusion), channel_id=1, source_target_pairs={{0,25},{1,26},{2,27},{3,28},{4,29},{5,30},{6,31},{7,32},{8,33},{9,... | collective-permute-start | bytes 215048
  1173.1 18.9 %collective-permute-start.25 = (f32[16,1120]{1,0:T(8,128)S(1)}, f32[16,1120]{1,0:T(8,128)S(1)}, u32[]{:S(2)}, u32[]{:S(2)}) collective-permute-start(f32[16,1120]{1,0:T(8,128)S(1)} %fusion), channel_id=1, source_target_pairs={{0,26},{1,27},{2,28},{3,29},{4,30},{5,31},{6,32},{7,33},{8,34},{9,... | collective-permute-start | bytes 215048
  1175.0 22.2 %collective-permute-start.26 = (f32[16,1120]{1,0:T(8,128)S(1)}, f32[16,1120]{1,0:T(8,128)S(1)}, u32[]{:S(2)}, u32[]{:S(2)}) collective-permute-start(f32[16,1120]{1,0:T(8,128)S(1)} %fusion), channel_id=1, source_target_pairs={{0,27},{1,28},{2,29},{3,30},{4,31},{5,32},{6,33},{7,34},{8,35},{9,... | collective-permute-start | bytes 215048
  1177.0 22.1 %collective-permute-start.27 = (f32[16,1120]{1,0:T(8,128)S(1)}, f32[16,1120]{1,0:T(8,128)S(1)}, u32[]{:S(2)}, u32[]{:S(2)}) collective-permute-start(f32[16,1120]{1,0:T(8,128)S(1)} %fusion), channel_id=1, source_target_pairs={{0,28},{1,29},{2,30},{3,31},{4,32},{5,33},{6,34},{7,35},{8,36},{9,... | collective-permute-start | bytes 215048
  1188.4 15.2 %collective-permute-start.28 = (f32[16,1120]{1,0:T(8,128)S(1)}, f32[16,1120]{1,0:T(8,128)S(1)}, u32[]{:S(2)}, u32[]{:S(2)}) collective-permute-start(f32[16,1120]{1,0:T(8,128)S(1)} %fusion), channel_id=1, source_target_pairs={{0,29},{1,30},{2,31},{3,32},{4,33},{5,34},{6,35},{7,36},{8,37},{9,... | collective-permute-start | bytes 215048
  1190.4 15.3 %collective-permute-start.29 = (f32[16,1120]{1,0:T(8,128)S(1)}, f32[16,1120]{1,0:T(8,128)S(1)}, u32[]{:S(2)}, u32[]{:S(2)}) collective-permute-start(f32[16,1120]{1,0:T(8,128)S(1)} %fusion), channel_id=1, source_target_pairs={{0,30},{1,31},{2,32},{3,33},{4,34},{5,35},{6,36},{7,37},{8,38},{9,... | collective-permute-start | bytes 215048
  1192.1 15.8 %collective-permute-start.3 = (f32[16,1120]{1,0:T(8,128)S(1)}, f32[16,1120]{1,0:T(8,128)S(1)}, u32[]{:S(2)}, u32[]{:S(2)}) collective-permute-start(f32[16,1120]{1,0:T(8,128)S(1)} %fusion), channel_id=1, source_target_pairs={{0,4},{1,5},{2,6},{3,7},{4,8},{5,9},{6,10},{7,11},{8,12},{9,13},{1... | collective-permute-start | bytes 215048
  1197.2 12.6 collective-permute-start.30
  1199.1 14.3 %collective-permute-start.4 = (f32[16,1120]{1,0:T(8,128)S(1)}, f32[16,1120]{1,0:T(8,128)S(1)}, u32[]{:S(2)}, u32[]{:S(2)}) collective-permute-start(f32[16,1120]{1,0:T(8,128)S(1)} %fusion), channel_id=1, source_target_pairs={{0,5},{1,6},{2,7},{3,8},{4,9},{5,10},{6,11},{7,12},{8,13},{9,14},{... | collective-permute-start | bytes 215048
  1203.7 78.5 %collective-permute-start.5 = (f32[16,1120]{1,0:T(8,128)S(1)}, f32[16,1120]{1,0:T(8,128)}, u32[]{:S(2)}, u32[]{:S(2)}) collective-permute-start(f32[16,1120]{1,0:T(8,128)S(1)} %fusion), channel_id=1, source_target_pairs={{0,6},{1,7},{2,8},{3,9},{4,10},{5,11},{6,12},{7,13},{8,14},{9,15},... | collective-permute-start | bytes 215048
  1205.7 76.5 %collective-permute-start.6 = (f32[16,1120]{1,0:T(8,128)S(1)}, f32[16,1120]{1,0:T(8,128)}, u32[]{:S(2)}, u32[]{:S(2)}) collective-permute-start(f32[16,1120]{1,0:T(8,128)S(1)} %fusion), channel_id=1, source_target_pairs={{0,7},{1,8},{2,9},{3,10},{4,11},{5,12},{6,13},{7,14},{8,15},{9,16}... | collective-permute-start | bytes 215048
  1207.9 74.3 %collective-permute-start.7 = (f32[16,1120]{1,0:T(8,128)S(1)}, f32[16,1120]{1,0:T(8,128)}, u32[]{:S(2)}, u32[]{:S(2)}) collective-permute-start(f32[16,1120]{1,0:T(8,128)S(1)} %fusion), channel_id=1, source_target_pairs={{0,8},{1,9},{2,10},{3,11},{4,12},{5,13},{6,14},{7,15},{8,16},{9,17... | collective-permute-start | bytes 215048
  1209.8 72.4 %collective-permute-start.8 = (f32[16,1120]{1,0:T(8,128)S(1)}, f32[16,1120]{1,0:T(8,128)}, u32[]{:S(2)}, u32[]{:S(2)}) collective-permute-start(f32[16,1120]{1,0:T(8,128)S(1)} %fusion), channel_id=1, source_target_pairs={{0,9},{1,10},{2,11},{3,12},{4,13},{5,14},{6,15},{7,16},{8,17},{9,1... | collective-permute-start | bytes 215048
  1213.4 68.8 %collective-permute-start.9 = (f32[16,1120]{1,0:T(8,128)S(1)}, f32[16,1120]{1,0:T(8,128)}, u32[]{:S(2)}, u32[]{:S(2)}) collective-permute-start(f32[16,1120]{1,0:T(8,128)S(1)} %fusion), channel_id=1, source_target_pairs={{0,10},{1,11},{2,12},{3,13},{4,14},{5,15},{6,16},{7,17},{8,18},{9,... | collective-permute-start | bytes 215048
  (25 other events, 956.7 us)
Sparse Core Ops, SparseCore 0:
  9.7 309.7 all-gather.5
  335.0 357.4 all-gather.3
where the time goes:
time: 1320 us
  waiting for transfers between devices  650 us (49%)
  blocking collectives  435 us (33%)
  starting transfers between devices  86.5 us (7%)
  other arithmetic  54.2 us (4%)
  local copies, waits for them, and re-layouts  51.7 us (4%)
  matrix products  24.1 us (2%)
  between operations  15.3 us (1%)
    unnamed x1, blocking collectives  372 us
    all_gather x1, waiting for transfers between devices, on_device(): lax.all_gather(field, 'member', axis=0, tiled=True).astype(jnp.float32)  341 us
    all_gather x1, waiting for transfers between devices, on_device(): lax.all_gather(weight, ('space', 'member'), axis=0, tiled=True)  308 us
    unnamed x32, starting transfers between devices  86.4 us
    psum x1, blocking collectives, on_device(): lax.psum((bias_part, gain_portion), ('space', 'member'))  63.2 us
    unnamed x50, local copies, waits for them, and re-layouts  36.8 us
  transfers between devices with their start and end apart: 34, of which 2 were waited for; matrix products, arithmetic and copies ran while one was open for 2% of the time, Pallas kernels for 0%

commit v1 on v0

v1 whole, which is shorter than its diff:
```python
import functools

import jax
import jax.numpy as jnp
import numpy as np
from jax import lax
from jax.experimental import pallas as pl
from jax.experimental.pallas import tpu as pltpu
from jax.sharding import Mesh
from jax.sharding import PartitionSpec as P

ALPHA = 0.95
DELTA = 0.1
EPS = 1e-05
SIZE = dict(yh=2, z=4, core=2, x=4, yl=2)
SPACE = ("yh", "z", "core")
MEMBER = ("x", "yl")
CHUNKS = ((0, 640), (640, 480))
BF16 = jnp.bfloat16
F32 = jnp.float32
PARAMS = pltpu.CompilerParams(vmem_limit_bytes=56 * 1024 * 1024)


def latitude_weights(rows):
    index = np.arange(rows, dtype=np.float64)
    cosine = np.cos((60.0 - 0.25 * (index + 0.5)) * (np.pi / 180.0))
    return (cosine / cosine.mean()).astype(np.float32)


def swap(value, axis, step):
    return lax.ppermute(value, axis, [(i, i ^ step) for i in range(SIZE[axis])])


def swap_member(value, step):
    return lax.ppermute(value, MEMBER, [(i, i ^ step) for i in range(8)])


def vmem(count):
    return [pl.BlockSpec(memory_space=pltpu.VMEM)] * count


def truth_kernel(image_ref, out_ref):
    image = image_ref[...]
    chan_rows, cols = image.shape
    cells = cols // 4
    outs = chan_rows * 4
    total = jnp.zeros((cells, outs), F32)
    for q in range(4):
        pick = (
            lax.broadcasted_iota(jnp.int32, (cells, cols), 1)
            == 4 * lax.broadcasted_iota(jnp.int32, (cells, cols), 0) + q
        ).astype(BF16)
        part = lax.dot_general(
            pick, image, (((1,), (1,)), ((), ())), preferred_element_type=F32
        ).astype(BF16)
        place = (
            lax.broadcasted_iota(jnp.int32, (chan_rows, outs), 1)
            == 4 * lax.broadcasted_iota(jnp.int32, (chan_rows, outs), 0) + q
        ).astype(BF16)
        total = total + jnp.dot(part, place, preferred_element_type=F32)
    out_ref[...] = total


def norm_kernel(tokens_ref, gain_ref, normed_ref):
    wide = tokens_ref[...].astype(F32)
    mean = jnp.mean(wide, -1, keepdims=True)
    centred = wide - mean
    variance = jnp.mean(centred * centred, -1, keepdims=True)
    normed_ref[...] = (centred * lax.rsqrt(variance + EPS) * gain_ref[...]).astype(BF16)


def weight_kernel(place_ref, a_ref, b_ref, c_ref, d_ref, out_ref):
    for core, yh, ref in ((0, 0, a_ref), (0, 1, b_ref), (1, 0, c_ref), (1, 1, d_ref)):
        for step in range(4):
            block = (
                (place_ref[0] ^ yh) * 8 + (place_ref[1] ^ step) * 2 + (place_ref[2] ^ core)
            )
            out_ref[pl.ds(pl.multiple_of(block * 96, 96), 96), :] = ref[step]


def slope(value):
    return value * lax.rsqrt(value * value + DELTA * DELTA)


def middle_kernel(
    place_ref, normed_ref, weight_ref, bias_ref, truth_ref, wt_ref,
    dfield_ref, bias_out_ref, keep_ref, send_ref, field, grad, sums,
):
    width = weight_ref.shape[1]
    padded = field.shape[2]
    count = 16
    coef = (1.0 - (1.0 - ALPHA) / count) / (count * (count - 1))

    def project(step, carry):
        row = pl.multiple_of(step * 256, 256)
        part = jnp.dot(
            normed_ref[pl.ds(row, 256), :], weight_ref[...], preferred_element_type=F32
        ) + bias_ref[...]
        part = part.astype(BF16).astype(F32).reshape(4, 64, width)
        field[pl.ds(step * 4, 4), :, 0:width] = part
        return carry

    lax.fori_loop(0, 4, project, 0)
    sums[...] = jnp.zeros_like(sums)

    def pairs(step, carry):
        row = pl.multiple_of((step // (padded // 128)) * 8, 8)
        lane = pl.multiple_of((step % (padded // 128)) * 128, 128)
        here = (pl.ds(row, 8), pl.ds(lane, 128))
        values = [field[m, here[0], here[1]] for m in range(count)]
        total = [None] * count
        for m in range(count):
            for k in range(m + 1, count):
                s = slope(values[m] - values[k])
                total[m] = s if total[m] is None else total[m] + s
                total[k] = -s if total[k] is None else total[k] - s
        true = truth_ref[here[0], here[1]]
        scale = wt_ref[0:1, pl.ds(lane, 128)]
        column = None
        for m in range(count):
            value = scale * (slope(values[m] - true) * (1.0 / count) - coef * total[m])
            value = value.astype(BF16).astype(F32)
            field[m, here[0], here[1]] = value
            column = value if column is None else column + value
        sums[:, pl.ds(lane, 128)] += column
        return carry

    lax.fori_loop(0, 8 * (padded // 128), pairs, 0)
    bias_out_ref[...] = sums[:, 0:width]

    def store(step, carry):
        row = pl.multiple_of(step * 64, 64)
        dfield_ref[pl.ds(row, 64), :] = field[step, :, 0:width].astype(BF16)
        return carry

    lax.fori_loop(0, count, store, 0)

    def weight_grad(step, carry):
        lane = pl.multiple_of(step * 256, 256)
        grad[pl.ds(lane, 256), :] = lax.dot_general(
            normed_ref[:, pl.ds(lane, 256)],
            dfield_ref[...],
            (((0,), (0,)), ((), ())),
            preferred_element_type=F32,
        )
        return carry

    lax.fori_loop(0, 6, weight_grad, 0)
    for yh in range(2):
        for step in range(4):
            base = (place_ref[0] ^ yh) * 8 + (place_ref[1] ^ step) * 2
            mine = pl.multiple_of((base + place_ref[2]) * 96, 96)
            other = pl.multiple_of((base + (place_ref[2] ^ 1)) * 96, 96)
            keep_ref[yh, step] = grad[pl.ds(mine, 96), :]
            send_ref[yh, step] = grad[pl.ds(other, 96), :].astype(BF16)


def backward_kernel(tokens_ref, gain_ref, *refs):
    count = len(CHUNKS)
    dfields, weights = refs[:count], refs[count : 2 * count]
    out_ref, gain_out_ref = refs[2 * count :]
    step = pl.program_id(0)
    wide = tokens_ref[...].astype(F32)
    mean = jnp.mean(wide, -1, keepdims=True)
    centred = wide - mean
    variance = jnp.mean(centred * centred, -1, keepdims=True)
    inverse = lax.rsqrt(variance + EPS)
    xhat = centred * inverse
    grad = None
    for d_ref, w_ref in zip(dfields, weights):
        part = lax.dot_general(
            d_ref[...], w_ref[...], (((1,), (1,)), ((), ())), preferred_element_type=F32
        )
        grad = part if grad is None else grad + part

    @pl.when(step == 0)
    def _():
        gain_out_ref[...] = jnp.zeros_like(gain_out_ref)

    rows = grad.shape[0]
    gain_out_ref[...] += jnp.sum((grad * xhat).reshape(rows // 8, 8, -1), axis=0)
    scaled = grad * gain_ref[...]
    out = inverse * (
        scaled
        - jnp.mean(scaled, -1, keepdims=True)
        - xhat * jnp.mean(scaled * xhat, -1, keepdims=True)
    )
    out_ref[...] = out.astype(BF16)


def gather_weight(weight, where):
    pieces = [weight] + [swap(weight, "x", k) for k in (1, 2, 3)]
    near = jnp.stack(pieces)
    both = jnp.stack([near, swap(near, "yl", 1)], axis=1)
    rows, width = weight.shape
    members = 8 * rows
    index = jnp.arange(members)
    block, inside = index // rows, index % rows
    source = (((block // 2) ^ where["x"]) * 2 + ((block % 2) ^ where["yl"])) * rows + inside
    pick = (source[:, None] == jnp.arange(members)[None, :]).astype(BF16)
    block = jnp.dot(
        pick, both.reshape(members, width), preferred_element_type=F32
    ).astype(BF16)
    pair = [block, swap(block, "yh", 1)]
    pair = jnp.stack(pair)
    quad = [pair] + [swap(pair, "z", k) for k in (1, 2, 3)]
    quad = jnp.stack(quad, axis=1)
    other = swap(quad, "core", 1)
    place = jnp.stack([where["yh"], where["z"], where["core"]]).astype(jnp.int32)
    full = pl.pallas_call(
        weight_kernel,
        out_shape=jax.ShapeDtypeStruct((16 * members, width), BF16),
        in_specs=[pl.BlockSpec(memory_space=pltpu.SMEM)] + vmem(4),
        out_specs=pl.BlockSpec(memory_space=pltpu.VMEM),
        compiler_params=PARAMS,
        name="weight_rows",
    )(place, quad[0], quad[1], other[0], other[1])
    return full, place


def scatter_grad(keep, send, where):
    width = keep.shape[-1]
    total = keep + swap(send, "core", 1).astype(F32)
    low = total.astype(BF16)
    total = sum([swap(low[:, k], "z", k).astype(F32) for k in (1, 2, 3)], total[:, 0])
    total = total[0] + swap(total[1].astype(BF16), "yh", 1).astype(F32)
    total = total.reshape(4, 2, 12, width)

    def part(value, index):
        return lax.dynamic_index_in_dim(value, index, 0, keepdims=False)

    mine = part(total, where["x"])
    for k in (1, 2, 3):
        mine = mine + swap(part(total, where["x"] ^ k).astype(BF16), "x", k).astype(F32)
    return part(mine, where["yl"]) + swap(
        part(mine, where["yl"] ^ 1).astype(BF16), "yl", 1
    ).astype(F32)


def all_sum(value):
    for axis in ("core", "z", "yh", "x", "yl"):
        value = sum([swap(value, axis, k) for k in range(1, SIZE[axis])], value)
    return value


def on_device(tokens, gain, weight, bias, target, channel_weight):
    where = {axis: lax.axis_index(axis) for axis in SIZE}
    member = where["x"] * 2 + where["yl"]
    space = (where["yh"] * 4 + where["z"]) * 2 + where["core"]
    features = tokens.shape[-1]
    outs = weight.shape[1]

    full, place = gather_weight(weight, where)
    pieces = tokens.reshape(2, 8, 64, features)
    received = []
    for k in range(8):
        piece = lax.dynamic_index_in_dim(pieces, member ^ k, 1, keepdims=False)
        received.append(swap_member(piece, k) if k else piece)
    gathered = jnp.concatenate([r.reshape(128, features) for r in received])

    t_here, l_here = member // 4, member % 4
    image = lax.dynamic_slice(
        target, (0, 4 * t_here, 256 * l_here), (target.shape[0], 4, 256)
    ).reshape(-1, 256)
    truth = pl.pallas_call(
        truth_kernel,
        out_shape=jax.ShapeDtypeStruct((64, outs), F32),
        in_specs=vmem(1),
        out_specs=vmem(1)[0],
        compiler_params=PARAMS,
        name="truth",
    )(image)
    table = jnp.asarray(latitude_weights(128).reshape(32, 4))
    latw = lax.dynamic_index_in_dim(table, space * 2 + t_here, 0, keepdims=False)
    wt = jnp.broadcast_to(
        channel_weight[:, None, None] * latw[None, :, None], (channel_weight.shape[0], 4, 4)
    ).reshape(1, outs)

    gain_row = gain.reshape(1, features)
    bias_row = bias.reshape(1, outs)
    normed = pl.pallas_call(
        norm_kernel,
        grid=(4,),
        out_shape=jax.ShapeDtypeStruct((1024, features), BF16),
        in_specs=[
            pl.BlockSpec((256, features), lambda i: (i, 0)),
            pl.BlockSpec((1, features), lambda i: (0, 0)),
        ],
        out_specs=pl.BlockSpec((256, features), lambda i: (i, 0)),
        compiler_params=PARAMS,
        name="norm",
    )(gathered, gain_row)

    dfields, weights, bias_parts, shares = [], [], [], []
    for start, width in CHUNKS:
        padded = -(-width // 128) * 128
        cut = slice(start, start + width)
        chunk = full[:, cut]
        pad = ((0, 0), (0, padded - width))
        dfield, bias_part, keep, send = pl.pallas_call(
            middle_kernel,
            out_shape=(
                jax.ShapeDtypeStruct((1024, width), BF16),
                jax.ShapeDtypeStruct((8, width), F32),
                jax.ShapeDtypeStruct((2, 4, 96, width), F32),
                jax.ShapeDtypeStruct((2, 4, 96, width), BF16),
            ),
            in_specs=[pl.BlockSpec(memory_space=pltpu.SMEM)] + vmem(5),
            out_specs=tuple(vmem(4)),
            scratch_shapes=[
                pltpu.VMEM((16, 64, padded), F32),
                pltpu.VMEM((features, width), F32),
                pltpu.VMEM((8, padded), F32),
            ],
            compiler_params=PARAMS,
            name="middle",
        )(
            place, normed, chunk, bias_row[:, cut],
            jnp.pad(truth[:, cut], pad), jnp.pad(wt[:, cut], pad),
        )
        dfields.append(dfield)
        weights.append(chunk)
        bias_parts.append(bias_part)
        shares.append(scatter_grad(keep, send, where))

    token_part, gain_part = pl.pallas_call(
        backward_kernel,
        grid=(8,),
        out_shape=(
            jax.ShapeDtypeStruct((1024, features), BF16),
            jax.ShapeDtypeStruct((8, features), F32),
        ),
        in_specs=[
            pl.BlockSpec((128, features), lambda i: (i, 0)),
            pl.BlockSpec((1, features), lambda i: (0, 0)),
        ]
        + [pl.BlockSpec((128, w), lambda i: (i, 0)) for _, w in CHUNKS]
        + [pl.BlockSpec((features, w), lambda i: (0, 0)) for _, w in CHUNKS],
        out_specs=(
            pl.BlockSpec((128, features), lambda i: (i, 0)),
            pl.BlockSpec((8, features), lambda i: (0, 0)),
        ),
        compiler_params=PARAMS,
        name="backward",
    )(gathered, gain_row, *dfields, *weights)

    small = jnp.concatenate(
        [jnp.sum(gain_part, axis=0)] + [jnp.sum(part, axis=0) for part in bias_parts]
    )
    small = jnp.pad(small, (0, 3072 - small.shape[0])).reshape(24, 128)
    small = all_sum(small).reshape(-1)

    back = token_part.reshape(8, 2, 64, features)
    result = jnp.zeros((2, 8, 64, features), BF16)
    for k in range(8):
        piece = swap_member(back[k], k) if k else back[k]
        result = lax.dynamic_update_slice(result, piece[:, None], (0, member ^ k, 0, 0))
    return (
        result.reshape(tokens.shape),
        small[:features],
        jnp.concatenate(shares, axis=1),
        small[features : features + outs],
    )


def solution(mesh):
    fine = Mesh(
        mesh.devices.reshape(2, 4, 2, 4, 2), ("yh", "z", "core", "x", "yl")
    )
    both = SPACE + MEMBER
    return jax.shard_map(
        on_device,
        mesh=fine,
        in_specs=(
            P(MEMBER, SPACE, None, None),
            P(),
            P(both, None),
            P(),
            P(None, SPACE, None),
            P(),
        ),
        out_specs=(P(MEMBER, SPACE, None, None), P(), P(both, None), P()),
        check_vma=False,
    )
```

time: 1320 us -> 302 us (0.23)
  waiting for transfers between devices: 650 us -> 126 us
  blocking collectives: 435 us -> 0 us
  Pallas kernels: 0 us -> 61.8 us
  other arithmetic: 54.2 us -> 7.91 us
  matrix products: 24.1 us -> 0.25 us
  local copies, waits for them, and re-layouts: 51.7 us -> 34.7 us
  starting transfers between devices: 86.5 us -> 69.9 us
  between operations: 15.3 us -> 1.16 us
    all_gather x2 -> x0, waiting for transfers between devices: 649 us -> none  [the longest x1 341 us: on_device(): lax.all_gather(field, 'member', axis=0, tiled=True).astype(jnp.float32)]
    unnamed x1 -> x0, blocking collectives: 372 us -> none
    ppermute x0 -> x50, waiting for transfers between devices: none -> 126 us  [the longest x36 77.7 us: swap(): return lax.ppermute(value, axis, [(i, i ^ step) for i in range(SIZE[axis])])]
    unnamed x32 -> x0, starting transfers between devices: 86.4 us -> none
    ppermute x0 -> x50, starting transfers between devices: none -> 69.9 us  [the longest x36 51.3 us: swap(): return lax.ppermute(value, axis, [(i, i ^ step) for i in range(SIZE[axis])])]
    psum x1 -> x0, blocking collectives: 63.2 us -> none  [on_device(): lax.psum((bias_part, gain_portion), ('space', 'member'))]
    pallas_call x0 -> x6, Pallas kernels: none -> 61.8 us  [the longest x2 33 us: on_device(): pl.pallas_call(middle_kernel, out_shape=(jax.ShapeDtypeStruct((1024, widt...]
    unnamed x50 -> x31, local copies, waits for them, and re-layouts: 36.8 us -> 4.64 us
  transfers between devices with their start and end apart: 34 -> 50, of which waited for: 2 -> 20; matrix products, arithmetic and copies ran while one was open for 2% -> 10% of each run, Pallas kernels for 0% -> 3%
where the time goes in v1:
time: 302 us; the launch traced here: 301 us
  waiting for transfers between devices  126 us (42%)
  starting transfers between devices  69.9 us (23%)
  Pallas kernels  61.8 us (20%)
  local copies, waits for them, and re-layouts  34.7 us (11%)
  other arithmetic  7.91 us (3%)
    ppermute x36, waiting for transfers between devices, swap(): return lax.ppermute(value, axis, [(i, i ^ step) for i in range(SIZE[axis])])  77.7 us
    ppermute x36, starting transfers between devices, swap(): return lax.ppermute(value, axis, [(i, i ^ step) for i in range(SIZE[axis])])  51.3 us
    ppermute x14, waiting for transfers between devices, swap_member(): return lax.ppermute(value, MEMBER, [(i, i ^ step) for i in range(8)])  47.8 us
    pallas_call x2, Pallas kernels, on_device(): pl.pallas_call(middle_kernel, out_shape=(jax.ShapeDtypeStruct((1024, widt...  33 us
    ppermute x14, starting transfers between devices, swap_member(): return lax.ppermute(value, MEMBER, [(i, i ^ step) for i in range(8)])  18.6 us
    pallas_call x1, Pallas kernels, on_device(): pl.pallas_call(backward_kernel, grid=(8,), out_shape=(jax.ShapeDtypeStruc...  16.7 us
  transfers between devices with their start and end apart: 50, of which 20 were waited for; matrix products, arithmetic and copies ran while one was open for 10% of the time, Pallas kernels for 3%

profile of v1, /device:TPU:0, one launch (start us, length us, event | category | flops | bytes accessed | tf_op | source)
XLA Modules:
  0.0 301.2 jit_solution(4796586817471526197)
XLA Ops:
  5.0 3.5 %dynamic-slice_bitcast_fusion = (bf16[2,64,1536]{2,1,0:T(8,128)(2,1)}, bf16[2,64,1536]{2,1,0:T(8,128)(2,1)}, bf16[2,64,1536]{2,1,0:T(8,128)(2,1)}, bf16[2,64,153...) fusion(bf16[2,8,64,1536]{3,2,1,0:T(8,128)(2,1)} %bitcast.190, ...), kind=kLoop, calls=%fused_computation.24 | loop fusion | bytes 6291488 | tf_op jit(solution)/shard_map/jit(dynamic_index_in_dim)/squeeze | solution.py:257
  8.5 3.6 %collective-permute-start.6 = (bf16[2,64,1536]{2,1,0:T(8,128)(2,1)}, bf16[2,64,1536]{2,1,0:T(8,128)(2,1)}, u32[]{:S(2)}, u32[]{:S(2)}) collective-permute-start(bf16[2,64,1536]{2,1,0:T(8,128)(2,1)} %get-tuple-element.36), channel_id=1, source_target_pairs={{0,7},{1,6},{2,5},{3,4},{4,3},{5,2},{6,1},{7,0},{8,15},{9,14},{10,... | collective-permute-start | bytes 1179656 | tf_op jit(solution)/shard_map/ppermute | solution.py:35
  16.2 16.5 %collective-permute-done.10 = bf16[4,12,1120]{2,1,0:T(8,128)(2,1)S(1)} collective-permute-done((bf16[4,12,1120]{2,1,0:T(8,128)(2,1)S(1)}, bf16[4,12,1120]{2,1,0:T(8,128)(2,1)S(1)}, u32[]{:S(2)}, u32[]{:S(2)}) %collective-permute-start.10) | collective-permute-done | bytes 107552 | tf_op jit(solution)/shard_map/ppermute | solution.py:31
  33.1 3.3 %collective-permute-start.11 = (bf16[96,1120]{1,0:T(8,128)(2,1)S(1)}, bf16[96,1120]{1,0:T(8,128)(2,1)}, u32[]{:S(2)}, u32[]{:S(2)}) collective-permute-start(bf16[96,1120]{1,0:T(8,128)(2,1)S(1)} %convolution_convert_fusion), channel_id=1, source_target_pairs={{0,64},{64,0},{1,65},{65,1},{2,66},{66,2},{3,67},{67,3},{4,68},{68... | collective-permute-start | bytes 645128 | tf_op jit(solution)/shard_map/ppermute | solution.py:31
  41.8 2.9 truth.1
  50.7 4.0 %collective-permute-start.13 = (bf16[2,96,1120]{2,1,0:T(8,128)(2,1)S(1)}, bf16[2,96,1120]{2,1,0:T(8,128)(2,1)S(1)}, u32[]{:S(2)}, u32[]{:S(2)}) collective-permute-start(bf16[2,96,1120]{2,1,0:T(8,128)(2,1)S(1)} %get-tuple-element.55), channel_id=1, source_target_pairs={{0,32},{16,48},{32,0},{48,16},{1,33},{17,49},{33,1},{49,17},{2,34}... | collective-permute-start | bytes 1290248 | tf_op jit(solution)/shard_map/ppermute | solution.py:31
  57.8 7.9 %collective-permute-done.13 = bf16[2,96,1120]{2,1,0:T(8,128)(2,1)S(1)} collective-permute-done((bf16[2,96,1120]{2,1,0:T(8,128)(2,1)S(1)}, bf16[2,96,1120]{2,1,0:T(8,128)(2,1)S(1)}, u32[]{:S(2)}, u32[]{:S(2)}) %collective-permute-start.13) | collective-permute-done | bytes 430112 | tf_op jit(solution)/shard_map/ppermute | solution.py:31
  68.1 6.9 %collective-permute-done.12 = bf16[2,96,1120]{2,1,0:T(8,128)(2,1)S(1)} collective-permute-done((bf16[2,96,1120]{2,1,0:T(8,128)(2,1)S(1)}, bf16[2,96,1120]{2,1,0:T(8,128)(2,1)S(1)}, u32[]{:S(2)}, u32[]{:S(2)}) %collective-permute-start.12) | collective-permute-done | bytes 430112 | tf_op jit(solution)/shard_map/ppermute | solution.py:31
  79.3 15.9 %collective-permute-done.3 = bf16[2,64,1536]{2,1,0:T(8,128)(2,1)S(1)} collective-permute-done((bf16[2,64,1536]{2,1,0:T(8,128)(2,1)}, bf16[2,64,1536]{2,1,0:T(8,128)(2,1)S(1)}, u32[]{:S(2)}, u32[]{:S(2)}) %collective-permute-start.3) | collective-permute-done | bytes 393248 | tf_op jit(solution)/shard_map/ppermute | solution.py:35
  97.9 5.1 %norm.1.normed_ref = bf16[1024,1536]{1,0:T(8,128)(2,1)} custom-call(bf16[1024,1536]{1,0:T(8,128)(2,1)} %copy-done.3, f32[1,1536]{1,0:T(1,128)} %reshape.188.gain_ref), custom_call_target="tpu_custom_call" | custom-call | tf_op jit(solution)/shard_map/norm/pallas_call | solution.py:281
  105.7 4.1 %weight_rows.1 = bf16[1536,1120]{1,0:T(8,128)(2,1)} custom-call(s32[3]{0:T(128)} %pad_add_fusion.place_ref, bf16[4,96,1120]{2,1,0:T(8,128)(2,1)} %get-tuple-element.47.a_ref, bf16[4,96,1120]{2,1,0:T(8,128)(2,1)} %get-tuple-element.46.b_ref, bf16[4,96,1120]{2,1,0:T(8,128)(2,1)} %get-tuple-element.45.c_ref, bf16[4,96,1120]{2,1,0:T(8,128)(2,1)} %get-tuple-element.44.d_ref), custom_call_target="tpu_custom_call" | custom-call | tf_op jit(solution)/shard_map/weight_rows/pallas_call | solution.py:210
  109.8 2.7 slice.158.weight_ref.refs_3_
  112.6 3.0 slice.154.weight_ref.refs_2_
  115.5 14.7 %middle.3 = (bf16[1024,480]{1,0:T(8,128)(2,1)}, f32[8,480]{1,0:T(8,128)}, f32[2,4,96,480]{3,2,1,0:T(8,128)}, bf16[2,4,96,480]{3,2,1,0:T(8,128)(2,1)}) custom-call(s32[3]{0:T(128)} %pad_add_fusion.place_ref, bf16[1024,1536]{1,0:T(8,128)(2,1)} %norm.1.normed_ref, bf16[1536,480]{1,0:T(8,128)(2,1)} %slice.158.weight_ref.refs_3_, f32[1,480]{1,0:T(1,128)} %slice.159.bias_ref, ...), custom_call_target="tpu_custom_call" | custom-call | tf_op jit(solution)/shard_map/middle/pallas_call | solution.py:300
  130.9 18.4 %middle.2 = (bf16[1024,640]{1,0:T(8,128)(2,1)}, f32[8,640]{1,0:T(8,128)}, f32[2,4,96,640]{3,2,1,0:T(8,128)}, bf16[2,4,96,640]{3,2,1,0:T(8,128)(2,1)}) custom-call(s32[3]{0:T(128)} %pad_add_fusion.place_ref, bf16[1024,1536]{1,0:T(8,128)(2,1)} %norm.1.normed_ref, bf16[1536,640]{1,0:T(8,128)(2,1)} %slice.154.weight_ref.refs_2_, f32[1,640]{1,0:T(1,128)} %slice.155.bias_ref, ...), custom_call_target="tpu_custom_call" | custom-call | tf_op jit(solution)/shard_map/middle/pallas_call | solution.py:300
  150.1 16.7 %backward.1 = (bf16[1024,1536]{1,0:T(8,128)(2,1)}, f32[8,1536]{1,0:T(8,128)}) custom-call(bf16[1024,1536]{1,0:T(8,128)(2,1)} %copy-done.3, f32[1,1536]{1,0:T(1,128)} %reshape.188.gain_ref, bf16[1024,640]{1,0:T(8,128)(2,1)} %get-tuple-element.14.refs_0_, bf16[1024,480]{1,0:T(8,128)(2,1)} %get-tuple-element.15.refs_1_, ...), custom_call_target="tpu_custom_call" | custom-call | tf_op jit(solution)/shard_map/backward/pallas_call | solution.py:326
  177.6 3.3 %collective-permute-done.27 = f32[24,128]{1,0:T(8,128)S(1)} collective-permute-done((f32[24,128]{1,0:T(8,128)S(1)}, f32[24,128]{1,0:T(8,128)S(1)}, u32[]{:S(2)}, u32[]{:S(2)}) %collective-permute-start.27) | collective-permute-done | bytes 12320 | tf_op jit(solution)/shard_map/ppermute | solution.py:31
  187.2 2.4 collective-permute-start.21
  193.7 17.6 %collective-permute-done.31 = f32[24,128]{1,0:T(8,128)S(1)} collective-permute-done((f32[24,128]{1,0:T(8,128)S(1)}, f32[24,128]{1,0:T(8,128)S(1)}, u32[]{:S(2)}, u32[]{:S(2)}) %collective-permute-start.31) | collective-permute-done | bytes 12320 | tf_op jit(solution)/shard_map/ppermute | solution.py:31
  216.0 14.1 %collective-permute-done.17 = bf16[2,64,1536]{2,1,0:T(8,128)(2,1)S(1)} collective-permute-done((bf16[2,64,1536]{2,1,0:T(8,128)(2,1)S(1)}, bf16[2,64,1536]{2,1,0:T(8,128)(2,1)S(1)}, u32[]{:S(2)}, u32[]{:S(2)}) %collective-permute-start.17) | collective-permute-done | bytes 393248 | tf_op jit(solution)/shard_map/ppermute | solution.py:35
  230.1 8.6 %collective-permute-done.18 = bf16[2,64,1536]{2,1,0:T(8,128)(2,1)S(1)} collective-permute-done((bf16[2,64,1536]{2,1,0:T(8,128)(2,1)S(1)}, bf16[2,64,1536]{2,1,0:T(8,128)(2,1)S(1)}, u32[]{:S(2)}, u32[]{:S(2)}) %collective-permute-start.18) | collective-permute-done | bytes 393248 | tf_op jit(solution)/shard_map/ppermute | solution.py:35
  238.7 9.2 %collective-permute-done.19 = bf16[2,64,1536]{2,1,0:T(8,128)(2,1)S(1)} collective-permute-done((bf16[2,64,1536]{2,1,0:T(8,128)(2,1)S(1)}, bf16[2,64,1536]{2,1,0:T(8,128)(2,1)S(1)}, u32[]{:S(2)}, u32[]{:S(2)}) %collective-permute-start.19) | collective-permute-done | bytes 393248 | tf_op jit(solution)/shard_map/ppermute | solution.py:35
  252.8 3.6 %collective-permute-done.42 = bf16[2,96,480]{2,1,0:T(8,128)(2,1)S(1)} collective-permute-done((bf16[2,96,480]{2,1,0:T(8,128)(2,1)S(1)}, bf16[2,96,480]{2,1,0:T(8,128)(2,1)S(1)}, u32[]{:S(2)}, u32[]{:S(2)}) %collective-permute-start.42) | collective-permute-done | bytes 184352 | tf_op jit(solution)/shard_map/ppermute | solution.py:31
  256.3 5.7 %collective-permute-done.44 = bf16[2,96,480]{2,1,0:T(8,128)(2,1)S(1)} collective-permute-done((bf16[2,96,480]{2,1,0:T(8,128)(2,1)S(1)}, bf16[2,96,480]{2,1,0:T(8,128)(2,1)S(1)}, u32[]{:S(2)}, u32[]{:S(2)}) %collective-permute-start.44) | collective-permute-done | bytes 184352 | tf_op jit(solution)/shard_map/ppermute | solution.py:31
  266.6 2.9 collective-permute-start.34
  272.9 2.5 collective-permute-start.48
  275.4 2.7 collective-permute-start.47
  282.6 4.3 %collective-permute-done.36 = bf16[96,640]{1,0:T(8,128)(2,1)S(1)} collective-permute-done((bf16[96,640]{1,0:T(8,128)(2,1)S(1)}, bf16[96,640]{1,0:T(8,128)(2,1)S(1)}, u32[]{:S(2)}, u32[]{:S(2)}) %collective-permute-start.36) | collective-permute-done | bytes 122912 | tf_op jit(solution)/shard_map/ppermute | solution.py:31
  288.7 2.5 collective-permute-start.39
  291.2 2.5 collective-permute-start.49
  293.9 2.7 collective-permute-done.38
  296.9 3.7 %collective-permute-done.40 = bf16[12,640]{1,0:T(8,128)(2,1)S(1)} collective-permute-done((bf16[12,640]{1,0:T(8,128)(2,1)S(1)}, bf16[12,640]{1,0:T(8,128)(2,1)S(1)}, u32[]{:S(2)}, u32[]{:S(2)}) %collective-permute-start.40) | collective-permute-done | bytes 15392 | tf_op jit(solution)/shard_map/ppermute | solution.py:31
  (178 shorter events, 82.6 us)
Async XLA Ops:
  0.6 13.3 %collective-permute-start.7 = (bf16[12,1120]{1,0:T(8,128)(2,1)}, bf16[12,1120]{1,0:T(8,128)(2,1)S(1)}, u32[]{:S(2)}, u32[]{:S(2)}) collective-permute-start(bf16[12,1120]{1,0:T(8,128)(2,1)} %param.9), channel_id=1, source_target_pairs={{0,2},{2,0},{4,6},{6,4},{1,3},{3,1},{5,7},{7,5},{8,10},{10,8},{12,... | collective-permute-start | bytes 80648 | tf_op jit(solution)/shard_map/ppermute | solution.py:31
  2.3 12.1 %collective-permute-start.9 = (bf16[12,1120]{1,0:T(8,128)(2,1)}, bf16[12,1120]{1,0:T(8,128)(2,1)S(1)}, u32[]{:S(2)}, u32[]{:S(2)}) collective-permute-start(bf16[12,1120]{1,0:T(8,128)(2,1)} %param.9), channel_id=1, source_target_pairs={{0,6},{2,4},{4,2},{6,0},{1,7},{3,5},{5,3},{7,1},{8,14},{10,12},{12... | collective-permute-start | bytes 80648 | tf_op jit(solution)/shard_map/ppermute | solution.py:31
  4.4 10.1 %collective-permute-start.8 = (bf16[12,1120]{1,0:T(8,128)(2,1)}, bf16[12,1120]{1,0:T(8,128)(2,1)S(1)}, u32[]{:S(2)}, u32[]{:S(2)}) collective-permute-start(bf16[12,1120]{1,0:T(8,128)(2,1)} %param.9), channel_id=1, source_target_pairs={{0,4},{2,6},{4,0},{6,2},{1,5},{3,7},{5,1},{7,3},{8,12},{10,14},{12... | collective-permute-start | bytes 80648 | tf_op jit(solution)/shard_map/ppermute | solution.py:31
  8.5 86.7 %collective-permute-start.6 = (bf16[2,64,1536]{2,1,0:T(8,128)(2,1)}, bf16[2,64,1536]{2,1,0:T(8,128)(2,1)}, u32[]{:S(2)}, u32[]{:S(2)}) collective-permute-start(bf16[2,64,1536]{2,1,0:T(8,128)(2,1)} %get-tuple-element.36), channel_id=1, source_target_pairs={{0,7},{1,6},{2,5},{3,4},{4,3},{5,2},{6,1},{7,0},{8,15},{9,14},{10,... | collective-permute-start | bytes 1179656 | tf_op jit(solution)/shard_map/ppermute | solution.py:35
  12.1 44.6 %collective-permute-start.1 = (bf16[2,64,1536]{2,1,0:T(8,128)(2,1)}, bf16[2,64,1536]{2,1,0:T(8,128)(2,1)}, u32[]{:S(2)}, u32[]{:S(2)}) collective-permute-start(bf16[2,64,1536]{2,1,0:T(8,128)(2,1)} %get-tuple-element.41), channel_id=1, source_target_pairs={{0,2},{1,3},{2,0},{3,1},{4,6},{5,7},{6,4},{7,5},{8,10},{9,11},{10,... | collective-permute-start | bytes 1179656 | tf_op jit(solution)/shard_map/ppermute | solution.py:35
  13.9 41.8 %collective-permute-start = (bf16[2,64,1536]{2,1,0:T(8,128)(2,1)}, bf16[2,64,1536]{2,1,0:T(8,128)(2,1)}, u32[]{:S(2)}, u32[]{:S(2)}) collective-permute-start(bf16[2,64,1536]{2,1,0:T(8,128)(2,1)} %get-tuple-element.42), channel_id=1, source_target_pairs={{0,1},{1,0},{2,3},{3,2},{4,5},{5,4},{6,7},{7,6},{8,9},{9,8},{10,11... | collective-permute-start | bytes 1179656 | tf_op jit(solution)/shard_map/ppermute | solution.py:35
  14.5 18.2 %collective-permute-start.10 = (bf16[4,12,1120]{2,1,0:T(8,128)(2,1)S(1)}, bf16[4,12,1120]{2,1,0:T(8,128)(2,1)S(1)}, u32[]{:S(2)}, u32[]{:S(2)}) collective-permute-start(bf16[4,12,1120]{2,1,0:T(8,128)(2,1)S(1)} %get-tuple-element.63), channel_id=1, source_target_pairs={{0,1},{1,0},{2,3},{3,2},{4,5},{5,4},{6,7},{7,6},{8,9},{9,8},{10,11... | collective-permute-start | bytes 322568 | tf_op jit(solution)/shard_map/ppermute | solution.py:31
  33.1 16.5 %collective-permute-start.11 = (bf16[96,1120]{1,0:T(8,128)(2,1)S(1)}, bf16[96,1120]{1,0:T(8,128)(2,1)}, u32[]{:S(2)}, u32[]{:S(2)}) collective-permute-start(bf16[96,1120]{1,0:T(8,128)(2,1)S(1)} %convolution_convert_fusion), channel_id=1, source_target_pairs={{0,64},{64,0},{1,65},{65,1},{2,66},{66,2},{3,67},{67,3},{4,68},{68... | collective-permute-start | bytes 645128 | tf_op jit(solution)/shard_map/ppermute | solution.py:31
  50.7 15.0 %collective-permute-start.13 = (bf16[2,96,1120]{2,1,0:T(8,128)(2,1)S(1)}, bf16[2,96,1120]{2,1,0:T(8,128)(2,1)S(1)}, u32[]{:S(2)}, u32[]{:S(2)}) collective-permute-start(bf16[2,96,1120]{2,1,0:T(8,128)(2,1)S(1)} %get-tuple-element.55), channel_id=1, source_target_pairs={{0,32},{16,48},{32,0},{48,16},{1,33},{17,49},{33,1},{49,17},{2,34}... | collective-permute-start | bytes 1290248 | tf_op jit(solution)/shard_map/ppermute | solution.py:31
  54.7 20.3 %collective-permute-start.12 = (bf16[2,96,1120]{2,1,0:T(8,128)(2,1)S(1)}, bf16[2,96,1120]{2,1,0:T(8,128)(2,1)S(1)}, u32[]{:S(2)}, u32[]{:S(2)}) collective-permute-start(bf16[2,96,1120]{2,1,0:T(8,128)(2,1)S(1)} %get-tuple-element.55), channel_id=1, source_target_pairs={{0,16},{16,0},{32,48},{48,32},{1,17},{17,1},{33,49},{49,33},{2,18}... | collective-permute-start | bytes 1290248 | tf_op jit(solution)/shard_map/ppermute | solution.py:31
  55.7 20.8 %collective-permute-start.14 = (bf16[2,96,1120]{2,1,0:T(8,128)(2,1)S(1)}, bf16[2,96,1120]{2,1,0:T(8,128)(2,1)S(1)}, u32[]{:S(2)}, u32[]{:S(2)}) collective-permute-start(bf16[2,96,1120]{2,1,0:T(8,128)(2,1)S(1)} %get-tuple-element.55), channel_id=1, source_target_pairs={{0,48},{16,32},{32,16},{48,0},{1,49},{17,33},{33,17},{49,1},{2,50}... | collective-permute-start | bytes 1290248 | tf_op jit(solution)/shard_map/ppermute | solution.py:31
  56.7 22.2 %collective-permute-start.2 = (bf16[2,64,1536]{2,1,0:T(8,128)(2,1)}, bf16[2,64,1536]{2,1,0:T(8,128)(2,1)S(1)}, u32[]{:S(2)}, u32[]{:S(2)}) collective-permute-start(bf16[2,64,1536]{2,1,0:T(8,128)(2,1)} %get-tuple-element.40), channel_id=1, source_target_pairs={{0,3},{1,2},{2,1},{3,0},{4,7},{5,6},{6,5},{7,4},{8,11},{9,10},{10,... | collective-permute-start | bytes 1179656 | tf_op jit(solution)/shard_map/ppermute | solution.py:35
  65.7 29.5 %collective-permute-start.5 = (bf16[2,64,1536]{2,1,0:T(8,128)(2,1)}, bf16[2,64,1536]{2,1,0:T(8,128)(2,1)S(1)}, u32[]{:S(2)}, u32[]{:S(2)}) collective-permute-start(bf16[2,64,1536]{2,1,0:T(8,128)(2,1)} %get-tuple-element.37), channel_id=1, source_target_pairs={{0,6},{1,7},{2,4},{3,5},{4,2},{5,3},{6,0},{7,1},{8,14},{9,15},{10,... | collective-permute-start | bytes 1179656 | tf_op jit(solution)/shard_map/ppermute | solution.py:35
  75.0 20.1 %collective-permute-start.4 = (bf16[2,64,1536]{2,1,0:T(8,128)(2,1)}, bf16[2,64,1536]{2,1,0:T(8,128)(2,1)S(1)}, u32[]{:S(2)}, u32[]{:S(2)}) collective-permute-start(bf16[2,64,1536]{2,1,0:T(8,128)(2,1)} %get-tuple-element.38), channel_id=1, source_target_pairs={{0,5},{1,4},{2,7},{3,6},{4,1},{5,0},{6,3},{7,2},{8,13},{9,12},{10,... | collective-permute-start | bytes 1179656 | tf_op jit(solution)/shard_map/ppermute | solution.py:35
  76.5 18.6 %collective-permute-start.3 = (bf16[2,64,1536]{2,1,0:T(8,128)(2,1)}, bf16[2,64,1536]{2,1,0:T(8,128)(2,1)S(1)}, u32[]{:S(2)}, u32[]{:S(2)}) collective-permute-start(bf16[2,64,1536]{2,1,0:T(8,128)(2,1)} %get-tuple-element.39), channel_id=1, source_target_pairs={{0,4},{1,5},{2,6},{3,7},{4,0},{5,1},{6,2},{7,3},{8,12},{9,13},{10,... | collective-permute-start | bytes 1179656 | tf_op jit(solution)/shard_map/ppermute | solution.py:35
  78.9 25.4 %collective-permute-start.15 = (bf16[2,4,96,1120]{3,2,1,0:T(8,128)(2,1)S(1)}, bf16[2,4,96,1120]{3,2,1,0:T(8,128)(2,1)S(1)}, u32[]{:S(2)}, u32[]{:S(2)}) collective-permute-start(bf16[2,4,96,1120]{3,2,1,0:T(8,128)(2,1)S(1)} %pad_maximum_fusion), channel_id=1, source_target_pairs={{0,8},{8,0},{1,9},{9,1},{2,10},{10,2},{3,11},{11,3},{4,12},{12,4},... | collective-permute-start | bytes 5160968 | tf_op jit(solution)/shard_map/ppermute | solution.py:31
  177.5 70.6 %collective-permute-start.41 = (bf16[2,4,96,480]{3,2,1,0:T(8,128)(2,1)S(1)}, bf16[2,4,96,480]{3,2,1,0:T(8,128)(2,1)S(1)}, u32[]{:S(2)}, u32[]{:S(2)}) collective-permute-start(bf16[2,4,96,480]{3,2,1,0:T(8,128)(2,1)S(1)} %copy-done.11), channel_id=1, source_target_pairs={{0,8},{8,0},{1,9},{9,1},{2,10},{10,2},{3,11},{11,3},{4,12},{12,4},... | collective-permute-start | bytes 2211848 | tf_op jit(solution)/shard_map/ppermute | solution.py:31
  187.2 60.9 %collective-permute-start.21 = (bf16[2,64,1536]{2,1,0:T(8,128)(2,1)S(1)}, bf16[2,64,1536]{2,1,0:T(8,128)(2,1)S(1)}, u32[]{:S(2)}, u32[]{:S(2)}) collective-permute-start(bf16[2,64,1536]{2,1,0:T(8,128)(2,1)S(1)} %bitcast.198), channel_id=1, source_target_pairs={{0,6},{1,7},{2,4},{3,5},{4,2},{5,3},{6,0},{7,1},{8,14},{9,15},{10,... | collective-permute-start | bytes 1179656 | tf_op jit(solution)/shard_map/ppermute | solution.py:35
  189.6 63.1 %collective-permute-start.22 = (bf16[2,64,1536]{2,1,0:T(8,128)(2,1)S(1)}, bf16[2,64,1536]{2,1,0:T(8,128)(2,1)S(1)}, u32[]{:S(2)}, u32[]{:S(2)}) collective-permute-start(bf16[2,64,1536]{2,1,0:T(8,128)(2,1)S(1)} %bitcast.197), channel_id=1, source_target_pairs={{0,7},{1,6},{2,5},{3,4},{4,3},{5,2},{6,1},{7,0},{8,15},{9,14},{10,... | collective-permute-start | bytes 1179656 | tf_op jit(solution)/shard_map/ppermute | solution.py:35
  191.3 22.3 %collective-permute-start.16 = (bf16[2,64,1536]{2,1,0:T(8,128)(2,1)S(1)}, bf16[2,64,1536]{2,1,0:T(8,128)(2,1)S(1)}, u32[]{:S(2)}, u32[]{:S(2)}) collective-permute-start(bf16[2,64,1536]{2,1,0:T(8,128)(2,1)S(1)} %bitcast.203), channel_id=1, source_target_pairs={{0,1},{1,0},{2,3},{3,2},{4,5},{5,4},{6,7},{7,6},{8,9},{9,8},{10,11... | collective-permute-start | bytes 1179656 | tf_op jit(solution)/shard_map/ppermute | solution.py:35
  192.0 19.4 %collective-permute-start.31 = (f32[24,128]{1,0:T(8,128)S(1)}, f32[24,128]{1,0:T(8,128)S(1)}, u32[]{:S(2)}, u32[]{:S(2)}) collective-permute-start(f32[24,128]{1,0:T(8,128)S(1)} %add_add_fusion), channel_id=1, source_target_pairs={{0,1},{1,0},{2,3},{3,2},{4,5},{5,4},{6,7},{7,6},{8,9},{9,8},{10,11... | collective-permute-start | bytes 36872 | tf_op jit(solution)/shard_map/ppermute | solution.py:31
  211.4 36.6 %collective-permute-start.20 = (bf16[2,64,1536]{2,1,0:T(8,128)(2,1)S(1)}, bf16[2,64,1536]{2,1,0:T(8,128)(2,1)S(1)}, u32[]{:S(2)}, u32[]{:S(2)}) collective-permute-start(bf16[2,64,1536]{2,1,0:T(8,128)(2,1)S(1)} %bitcast.199), channel_id=1, source_target_pairs={{0,5},{1,4},{2,7},{3,6},{4,1},{5,0},{6,3},{7,2},{8,13},{9,12},{10,... | collective-permute-start | bytes 1179656 | tf_op jit(solution)/shard_map/ppermute | solution.py:35
  213.6 16.4 %collective-permute-start.17 = (bf16[2,64,1536]{2,1,0:T(8,128)(2,1)S(1)}, bf16[2,64,1536]{2,1,0:T(8,128)(2,1)S(1)}, u32[]{:S(2)}, u32[]{:S(2)}) collective-permute-start(bf16[2,64,1536]{2,1,0:T(8,128)(2,1)S(1)} %bitcast.202), channel_id=1, source_target_pairs={{0,2},{1,3},{2,0},{3,1},{4,6},{5,7},{6,4},{7,5},{8,10},{9,11},{10,... | collective-permute-start | bytes 1179656 | tf_op jit(solution)/shard_map/ppermute | solution.py:35
  238.7 9.3 %collective-permute-start.19 = (bf16[2,64,1536]{2,1,0:T(8,128)(2,1)S(1)}, bf16[2,64,1536]{2,1,0:T(8,128)(2,1)S(1)}, u32[]{:S(2)}, u32[]{:S(2)}) collective-permute-start(bf16[2,64,1536]{2,1,0:T(8,128)(2,1)S(1)} %bitcast.200), channel_id=1, source_target_pairs={{0,4},{1,5},{2,6},{3,7},{4,0},{5,1},{6,2},{7,3},{8,12},{9,13},{10,... | collective-permute-start | bytes 1179656 | tf_op jit(solution)/shard_map/ppermute | solution.py:35
  248.0 16.2 %collective-permute-start.32 = (bf16[2,4,96,640]{3,2,1,0:T(8,128)(2,1)S(1)}, bf16[2,4,96,640]{3,2,1,0:T(8,128)(2,1)S(1)}, u32[]{:S(2)}, u32[]{:S(2)}) collective-permute-start(bf16[2,4,96,640]{3,2,1,0:T(8,128)(2,1)S(1)} %copy-done.10), channel_id=1, source_target_pairs={{0,8},{8,0},{1,9},{9,1},{2,10},{10,2},{3,11},{11,3},{4,12},{12,4},... | collective-permute-start | bytes 2949128 | tf_op jit(solution)/shard_map/ppermute | solution.py:31
  249.6 12.5 %collective-permute-start.44 = (bf16[2,96,480]{2,1,0:T(8,128)(2,1)S(1)}, bf16[2,96,480]{2,1,0:T(8,128)(2,1)S(1)}, u32[]{:S(2)}, u32[]{:S(2)}) collective-permute-start(bf16[2,96,480]{2,1,0:T(8,128)(2,1)S(1)} %get-tuple-element.52), channel_id=1, source_target_pairs={{0,48},{16,32},{32,16},{48,0},{1,49},{17,33},{33,17},{49,1},{2,50}... | collective-permute-start | bytes 552968 | tf_op jit(solution)/shard_map/ppermute | solution.py:31
  250.8 11.3 %collective-permute-start.43 = (bf16[2,96,480]{2,1,0:T(8,128)(2,1)S(1)}, bf16[2,96,480]{2,1,0:T(8,128)(2,1)S(1)}, u32[]{:S(2)}, u32[]{:S(2)}) collective-permute-start(bf16[2,96,480]{2,1,0:T(8,128)(2,1)S(1)} %get-tuple-element.53), channel_id=1, source_target_pairs={{0,32},{16,48},{32,0},{48,16},{1,33},{17,49},{33,1},{49,17},{2,34}... | collective-permute-start | bytes 552968 | tf_op jit(solution)/shard_map/ppermute | solution.py:31
  265.5 9.9 %collective-permute-start.33 = (bf16[2,96,640]{2,1,0:T(8,128)(2,1)}, bf16[2,96,640]{2,1,0:T(8,128)(2,1)S(1)}, u32[]{:S(2)}, u32[]{:S(2)}) collective-permute-start(bf16[2,96,640]{2,1,0:T(8,128)(2,1)} %get-tuple-element.48), channel_id=1, source_target_pairs={{0,16},{16,0},{32,48},{48,32},{1,17},{17,1},{33,49},{49,33},{2,18}... | collective-permute-start | bytes 737288 | tf_op jit(solution)/shard_map/ppermute | solution.py:31
  265.5 13.8 %collective-permute-start.35 = (bf16[2,96,640]{2,1,0:T(8,128)(2,1)}, bf16[2,96,640]{2,1,0:T(8,128)(2,1)}, u32[]{:S(2)}, u32[]{:S(2)}) collective-permute-start(bf16[2,96,640]{2,1,0:T(8,128)(2,1)} %get-tuple-element.49), channel_id=1, source_target_pairs={{0,48},{16,32},{32,16},{48,0},{1,49},{17,33},{33,17},{49,1},{2,50}... | collective-permute-start | bytes 737288 | tf_op jit(solution)/shard_map/ppermute | solution.py:31
  266.6 12.6 %collective-permute-start.34 = (bf16[2,96,640]{2,1,0:T(8,128)(2,1)}, bf16[2,96,640]{2,1,0:T(8,128)(2,1)}, u32[]{:S(2)}, u32[]{:S(2)}) collective-permute-start(bf16[2,96,640]{2,1,0:T(8,128)(2,1)} %get-tuple-element.50), channel_id=1, source_target_pairs={{0,32},{16,48},{32,0},{48,16},{1,33},{17,49},{33,1},{49,17},{2,34}... | collective-permute-start | bytes 737288 | tf_op jit(solution)/shard_map/ppermute | solution.py:31
  271.2 10.5 %collective-permute-start.46 = (bf16[2,12,480]{2,1,0:T(8,128)(2,1)S(1)}, bf16[2,12,480]{2,1,0:T(8,128)(2,1)S(1)}, u32[]{:S(2)}, u32[]{:S(2)}) collective-permute-start(bf16[2,12,480]{2,1,0:T(8,128)(2,1)S(1)} %get-tuple-element.59), channel_id=1, source_target_pairs={{0,2},{2,0},{4,6},{6,4},{1,3},{3,1},{5,7},{7,5},{8,10},{10,8},{12,... | collective-permute-start | bytes 69128 | tf_op jit(solution)/shard_map/ppermute | solution.py:31
  272.9 8.8 %collective-permute-start.48 = (bf16[2,12,480]{2,1,0:T(8,128)(2,1)S(1)}, bf16[2,12,480]{2,1,0:T(8,128)(2,1)S(1)}, u32[]{:S(2)}, u32[]{:S(2)}) collective-permute-start(bf16[2,12,480]{2,1,0:T(8,128)(2,1)S(1)} %get-tuple-element.60), channel_id=1, source_target_pairs={{0,6},{2,4},{4,2},{6,0},{1,7},{3,5},{5,3},{7,1},{8,14},{10,12},{12... | collective-permute-start | bytes 69128 | tf_op jit(solution)/shard_map/ppermute | solution.py:31
  (30 other events, 423.8 us)

commit v2 on v0

v2 whole, which is shorter than its diff:
```python
import functools

import jax
import jax.numpy as jnp
import numpy as np
from jax import lax
from jax.experimental import pallas as pl
from jax.experimental.pallas import tpu as pltpu
from jax.sharding import Mesh
from jax.sharding import PartitionSpec as P

ALPHA = 0.95
DELTA = 0.1
EPS = 1e-05
SIZE = dict(yh=2, z=4, core=2, x=4, yl=2)
SPACE = ("yh", "z", "core")
MEMBER = ("x", "yl")
BF16 = jnp.bfloat16
F32 = jnp.float32


def params(mebibytes):
    return pltpu.CompilerParams(vmem_limit_bytes=mebibytes * 1024 * 1024)


def cost(flops, bytes_accessed):
    return pl.CostEstimate(flops=flops, bytes_accessed=bytes_accessed, transcendentals=0)


def after(values, *done):
    out = lax.optimization_barrier((*values, *done))
    return out[: len(values)], out[len(values) :]


def latitude_weights(rows):
    index = np.arange(rows, dtype=np.float64)
    cosine = np.cos((60.0 - 0.25 * (index + 0.5)) * (np.pi / 180.0))
    return (cosine / cosine.mean()).astype(np.float32)


def swap(value, axis, step):
    return lax.ppermute(value, axis, [(i, i ^ step) for i in range(SIZE[axis])])


def swap_y(value, step):
    return lax.ppermute(value, ("yh", "yl"), [(i, i ^ step) for i in range(4)])


def swap_member(value, step):
    return lax.ppermute(value, MEMBER, [(i, i ^ step) for i in range(8)])


def vmem(count):
    return [pl.BlockSpec(memory_space=pltpu.VMEM)] * count


def truth_kernel(image_ref, out_ref):
    image = image_ref[...]
    chan_rows, cols = image.shape
    cells = cols // 4
    total = jnp.zeros(out_ref.shape, F32)
    for q in range(4):
        pick = (
            lax.broadcasted_iota(jnp.int32, (cells, cols), 1)
            == 4 * lax.broadcasted_iota(jnp.int32, (cells, cols), 0) + q
        ).astype(BF16)
        part = lax.dot_general(
            pick, image, (((1,), (1,)), ((), ())), preferred_element_type=F32
        ).astype(BF16)
        place = (
            lax.broadcasted_iota(jnp.int32, (chan_rows, total.shape[1]), 1)
            == 4 * lax.broadcasted_iota(jnp.int32, (chan_rows, total.shape[1]), 0) + q
        ).astype(BF16)
        total = total + jnp.dot(part, place, preferred_element_type=F32)
    out_ref[...] = total


def norm_kernel(tokens_ref, gain_ref, normed_ref, flipped_ref):
    wide = tokens_ref[...].astype(F32)
    mean = jnp.mean(wide, -1, keepdims=True)
    centred = wide - mean
    variance = jnp.mean(centred * centred, -1, keepdims=True)
    normed = (centred * lax.rsqrt(variance + EPS) * gain_ref[...]).astype(BF16)
    normed_ref[...] = normed
    flipped_ref[...] = normed.T


def norm_piece(piece, gain_row):
    features = piece.shape[-1]
    return pl.pallas_call(
        norm_kernel,
        out_shape=(
            jax.ShapeDtypeStruct((128, features), BF16),
            jax.ShapeDtypeStruct((features, 128), BF16),
        ),
        in_specs=vmem(2),
        out_specs=tuple(vmem(2)),
        compiler_params=params(8),
        cost_estimate=cost(2000000000, 8000000),
        name="norm",
    )(piece.reshape(128, features), gain_row)


def slope(value):
    return value * lax.rsqrt(value * value + DELTA * DELTA)


def pairs_kernel(
    place_ref, quad_ref, other_ref, bias_ref, truth_ref, wt_ref, *refs
):
    pieces = refs[:8]
    full_ref, dfield_ref, bias_out_ref, normed_ref, field, sums = refs[8:]
    for k in range(8):
        normed_ref[pl.ds(128 * k, 128), :] = pieces[k][...]
    width = full_ref.shape[1]
    padded = field.shape[2]
    count = 16
    coef = (1.0 - (1.0 - ALPHA) / count) / (count * (count - 1))
    for core, ref in ((0, quad_ref), (1, other_ref)):
        for yh, step in [(yh, step) for yh in range(2) for step in range(4)]:
            block = (
                (place_ref[0] ^ yh) * 8 + (place_ref[1] ^ step) * 2 + (place_ref[2] ^ core)
            )
            full_ref[pl.ds(pl.multiple_of(block * 96, 96), 96), :] = ref[step, yh]

    def project(step, carry):
        row = pl.multiple_of(step * 256, 256)
        part = jnp.dot(
            normed_ref[pl.ds(row, 256), :], full_ref[...], preferred_element_type=F32
        ) + bias_ref[...]
        part = part.astype(BF16).astype(F32).reshape(4, 64, width)
        field[pl.ds(step * 4, 4), :, 0:width] = part
        return carry

    lax.fori_loop(0, 4, project, 0)
    sums[...] = jnp.zeros_like(sums)
    tiles = padded // 128

    def pairs(step, carry):
        row = pl.multiple_of((step // tiles) * 8, 8)
        lane = pl.multiple_of((step % tiles) * 128, 128)
        here = (pl.ds(row, 8), pl.ds(lane, 128))
        values = [field[m, here[0], here[1]] for m in range(count)]
        total = [None] * count
        for m in range(count):
            for k in range(m + 1, count):
                s = slope(values[m] - values[k])
                total[m] = s if total[m] is None else total[m] + s
                total[k] = -s if total[k] is None else total[k] - s
        true = truth_ref[here[0], here[1]]
        scale = wt_ref[0:1, pl.ds(lane, 128)]
        column = None
        for m in range(count):
            value = scale * (slope(values[m] - true) * (1.0 / count) - coef * total[m])
            value = value.astype(BF16).astype(F32)
            field[m, here[0], here[1]] = value
            column = value if column is None else column + value
        sums[:, pl.ds(lane, 128)] += column
        return carry

    lax.fori_loop(0, 8 * tiles, pairs, 0)
    bias_out_ref[...] = jnp.sum(sums[...], axis=0, keepdims=True)

    def store(step, carry):
        dfield_ref[step] = field[pl.ds(step * 2, 2), :, 0:width].astype(BF16)
        return carry

    lax.fori_loop(0, count // 2, store, 0)


def grad_kernel(place_ref, dfield_ref, full_ref, bias_part_ref, gain_ref, *refs):
    pieces = refs[:8]
    keep_ref, send_ref, small_ref, flipped_ref, grad, rows = refs[8:]
    for k in range(8):
        flipped_ref[:, pl.ds(128 * k, 128)] = pieces[k][...]
    width = full_ref.shape[1]
    features = full_ref.shape[0]

    def weight_grad(step, carry):
        row = pl.multiple_of(step * 512, 512)
        grad[pl.ds(row, 512), :] = jnp.dot(
            flipped_ref[pl.ds(row, 512), :], dfield_ref[...], preferred_element_type=F32
        )
        return carry

    lax.fori_loop(0, features // 512, weight_grad, 0)

    def gain_part(step, carry):
        row = pl.multiple_of(step * 128, 128)
        part = jnp.sum(
            grad[pl.ds(row, 128), :] * full_ref[pl.ds(row, 128), :].astype(F32),
            axis=1, keepdims=True,
        )
        rows[:, pl.ds(row, 128)] = jnp.broadcast_to(part, (128, 128)).T[0:8]
        return carry

    lax.fori_loop(0, features // 128, gain_part, 0)
    small_ref[...] = jnp.zeros_like(small_ref)
    for n in range(3):
        cut = slice(512 * n, 512 * (n + 1))
        small_ref[n : n + 1, :] = rows[0:1, cut] / gain_ref[:, cut]
        stop = min(512 * (n + 1), width)
        small_ref[3 + n : 4 + n, 0 : stop - 512 * n] = bias_part_ref[:, 512 * n : stop]
    small = small_ref[...]
    high = small.astype(BF16)
    low = (small - high.astype(F32)).astype(BF16)
    send_ref[0:16, :] = jnp.zeros((16, width), BF16)
    send_ref[0:16, 0:512] = jnp.concatenate([high, low], axis=0)
    for yh in range(2):
        for step in range(4):
            base = (place_ref[0] ^ yh) * 8 + (place_ref[1] ^ step) * 2
            mine = pl.multiple_of((base + place_ref[2]) * 96, 96)
            other = pl.multiple_of((base + (place_ref[2] ^ 1)) * 96, 96)
            keep_ref[yh, step] = grad[pl.ds(mine, 96), :]
            start = 16 + 96 * (yh * 4 + step)
            send_ref[start : start + 96, :] = grad[pl.ds(other, 96), :].astype(BF16)


def backward_kernel(place_ref, tokens_ref, gain_ref, full_ref, *refs):
    pieces, out_ref, dfield, grad = refs[:8], refs[8], refs[9], refs[10]
    features = full_ref.shape[0]
    for k in range(8):
        dfield[pl.ds(128 * k, 128), :] = pieces[k][...].reshape(128, -1)

    def matmul(step, carry):
        lane = pl.multiple_of(step * 256, 256)
        grad[:, pl.ds(lane, 256)] = lax.dot_general(
            dfield[...], full_ref[pl.ds(lane, 256), :], (((1,), (1,)), ((), ())),
            preferred_element_type=F32,
        )
        return carry

    lax.fori_loop(0, features // 256, matmul, 0)

    def rows(step, carry):
        k, m = step // 2, step % 2
        j = place_ref[3] ^ k
        wide = tokens_ref[m, j].astype(F32)
        mean = jnp.mean(wide, -1, keepdims=True)
        centred = wide - mean
        variance = jnp.mean(centred * centred, -1, keepdims=True)
        inverse = lax.rsqrt(variance + EPS)
        xhat = centred * inverse
        scaled = grad[pl.ds(pl.multiple_of(step * 64, 64), 64), :] * gain_ref[...]
        out = inverse * (
            scaled
            - jnp.mean(scaled, -1, keepdims=True)
            - xhat * jnp.mean(scaled * xhat, -1, keepdims=True)
        )
        out_ref[m, j] = out.astype(BF16)
        return carry

    lax.fori_loop(0, 16, rows, 0)


def member_rows(parts, where):
    _, _, rows, width = parts.shape
    members = 8 * rows
    index = jnp.arange(members)
    block, inside = index // rows, index % rows
    source = (((block % 2) ^ where["yl"]) * 4 + ((block // 2) ^ where["x"])) * rows + inside
    pick = (source[:, None] == jnp.arange(members)[None, :]).astype(BF16)
    return jnp.dot(
        pick, parts.reshape(members, width), preferred_element_type=F32
    ).astype(BF16)


def pack(small, width):
    high = lax.reduce_precision(small, 8, 7)
    both = jnp.concatenate([high, small - high], axis=0).astype(BF16)
    return jnp.pad(both, ((0, 0), (0, width - both.shape[1])))


def unpack(rows):
    rows = rows[:, :512].astype(F32)
    return rows[:8] + rows[8:16]


def on_device(tokens, gain, weight, bias, target, channel_weight):
    where = {axis: lax.axis_index(axis) for axis in SIZE}
    member = where["x"] * 2 + where["yl"]
    space = (where["yh"] * 4 + where["z"]) * 2 + where["core"]
    place = jnp.stack([where["yh"], where["z"], where["core"], member]).astype(jnp.int32)
    smem = pl.BlockSpec(memory_space=pltpu.SMEM)
    features = tokens.shape[-1]
    outs = weight.shape[1]
    padded = -(-outs // 128) * 128
    gain_row = gain.reshape(1, features)

    pieces = tokens.reshape(2, 8, 64, features)
    sources = [
        lax.dynamic_index_in_dim(pieces, member ^ k, 1, keepdims=False) for k in range(8)
    ]
    arrived = {0: sources[0], 1: swap_member(sources[1], 1), 4: swap_member(sources[4], 4)}
    near = jnp.stack([weight] + [swap(weight, "x", k) for k in (1, 2, 3)])
    (p3, p6), (near,) = after((sources[3], sources[6]), near)
    arrived[3], arrived[6] = swap_member(p3, 3), swap_member(p6, 6)
    rows_y = [near] + [swap_y(near, k) for k in (1, 2, 3)]
    pair = jnp.stack(
        [
            member_rows(jnp.stack(rows_y[0:2]), where),
            member_rows(jnp.stack(rows_y[2:4]), where),
        ]
    )
    (pair, p7, p2, p5), (arrived[1], arrived[4]) = after(
        (pair, sources[7], sources[2], sources[5]), arrived[1], arrived[4]
    )
    for k, piece in ((7, p7), (2, p2), (5, p5)):
        arrived[k] = swap_member(piece, k)
    quad = jnp.stack([pair] + [swap(pair, "z", k) for k in (1, 2, 3)])
    late = (3, 6, 7, 2, 5)
    (quad,), done = after((quad,), *[arrived[k] for k in late])
    for k, piece in zip(late, done):
        arrived[k] = piece
    other = swap(quad, "core", 1)
    normed = [norm_piece(arrived[k], gain_row) for k in range(8)]

    t_here, l_here = member // 4, member % 4
    image = lax.dynamic_slice(
        target, (0, 4 * t_here, 256 * l_here), (target.shape[0], 4, 256)
    ).reshape(-1, 256)
    truth = pl.pallas_call(
        truth_kernel,
        out_shape=jax.ShapeDtypeStruct((64, padded), F32),
        in_specs=vmem(1),
        out_specs=vmem(1)[0],
        compiler_params=params(8),
        cost_estimate=cost(2000000000, 8000000),
        name="truth",
    )(image)
    table = jnp.asarray(latitude_weights(128).reshape(32, 4))
    latw = lax.dynamic_index_in_dim(table, space * 2 + t_here, 0, keepdims=False)
    wt = jnp.broadcast_to(
        channel_weight[:, None, None] * latw[None, :, None], (channel_weight.shape[0], 4, 4)
    ).reshape(1, outs)
    wt = jnp.pad(wt, ((0, 0), (0, padded - outs)))

    full, dfield, bias_part = pl.pallas_call(
        pairs_kernel,
        out_shape=(
            jax.ShapeDtypeStruct((features, outs), BF16),
            jax.ShapeDtypeStruct((8, 2, 64, outs), BF16),
            jax.ShapeDtypeStruct((1, padded), F32),
        ),
        in_specs=[smem] + vmem(13),
        out_specs=tuple(vmem(3)),
        scratch_shapes=[
            pltpu.VMEM((1024, features), BF16),
            pltpu.VMEM((16, 64, padded), F32),
            pltpu.VMEM((8, padded), F32),
        ],
        compiler_params=params(32),
        cost_estimate=cost(20000000000, 80000000),
        name="pairs",
    )(place, quad, other, bias.reshape(1, outs), truth, wt, *[n[0] for n in normed])

    returned = {0: dfield[0], 1: swap_member(dfield[1], 1), 3: swap_member(dfield[3], 3)}
    keep, send, small = pl.pallas_call(
        grad_kernel,
        out_shape=(
            jax.ShapeDtypeStruct((2, 4, 96, outs), F32),
            jax.ShapeDtypeStruct((16 + 768, outs), BF16),
            jax.ShapeDtypeStruct((8, 512), F32),
        ),
        in_specs=[smem] + vmem(12),
        out_specs=tuple(vmem(3)),
        scratch_shapes=[
            pltpu.VMEM((features, 1024), BF16),
            pltpu.VMEM((features, outs), F32),
            pltpu.VMEM((8, features), F32),
        ],
        compiler_params=params(32),
        cost_estimate=cost(12000000000, 45000000),
        name="weight_gradient",
    )(
        place, dfield.reshape(1024, outs), full, bias_part, gain_row,
        *[n[1] for n in normed],
    )

    def pick(value, index):
        return lax.dynamic_index_in_dim(value, index, 0, keepdims=False)

    def spread(mine, blocks, small, moves):
        came = [
            move(jnp.concatenate([pack(small, outs), block.astype(BF16)], axis=0))
            for move, block in zip(moves, blocks)
        ]
        return (
            sum([c[16:].astype(F32) for c in came], mine),
            sum([unpack(c) for c in came], small),
        )

    rest = (6, 4, 5, 7, 2)
    (send, *held), (returned[1], returned[3]) = after(
        (send, *[dfield[k] for k in rest]), returned[1], returned[3]
    )
    for k, piece in zip(rest, held):
        returned[k] = swap_member(piece, k)
    came = swap(send, "core", 1)
    total = keep + came[16:].reshape(keep.shape).astype(F32)
    small = small + unpack(came)
    total, small = spread(
        total[:, 0].reshape(-1, outs),
        [total[:, k].reshape(-1, outs) for k in (1, 2, 3)],
        small,
        [functools.partial(swap, axis="z", step=k) for k in (1, 2, 3)],
    )
    result = pl.pallas_call(
        backward_kernel,
        out_shape=jax.ShapeDtypeStruct((2, 8, 64, features), BF16),
        in_specs=[smem] + vmem(11),
        out_specs=vmem(1)[0],
        scratch_shapes=[pltpu.VMEM((1024, outs), BF16), pltpu.VMEM((1024, features), F32)],
        compiler_params=params(32),
        cost_estimate=cost(16000000000, 60000000),
        name="backward",
    )(place, pieces, gain_row, full, *[returned[k] for k in range(8)])
    (total, small), (result,) = after((total, small), result)
    total = total.reshape(2, 4, 2, 12, outs)

    def slab(step):
        block = pick(total[step // 2].transpose(1, 0, 2, 3), where["yl"] ^ (step % 2))
        return block.reshape(48, outs)

    total, small = spread(
        slab(0),
        [slab(k) for k in (1, 2, 3)],
        small,
        [functools.partial(swap_y, step=k) for k in (1, 2, 3)],
    )
    total = total.reshape(4, 12, outs)
    share, small = spread(
        pick(total, where["x"]),
        [pick(total, where["x"] ^ k) for k in (1, 2, 3)],
        small,
        [functools.partial(swap, axis="x", step=k) for k in (1, 2, 3)],
    )
    return (
        result.reshape(tokens.shape),
        small[0:3].reshape(-1),
        share,
        small[3:6].reshape(-1)[:outs],
    )


def solution(mesh):
    fine = Mesh(
        mesh.devices.reshape(2, 4, 2, 4, 2), ("yh", "z", "core", "x", "yl")
    )
    both = SPACE + MEMBER
    return jax.shard_map(
        on_device,
        mesh=fine,
        in_specs=(
            P(MEMBER, SPACE, None, None),
            P(),
            P(both, None),
            P(),
            P(None, SPACE, None),
            P(),
        ),
        out_specs=(P(MEMBER, SPACE, None, None), P(), P(both, None), P()),
        check_vma=False,
    )
```

time: 1320 us -> 199 us (0.15)
  waiting for transfers between devices: 650 us -> 79.9 us
  blocking collectives: 435 us -> 0 us
  other arithmetic: 54.2 us -> 6.12 us
  Pallas kernels: 0 us -> 46.7 us
  starting transfers between devices: 86.5 us -> 45.1 us
  local copies, waits for them, and re-layouts: 51.7 us -> 19.3 us
  matrix products: 24.1 us -> 0.51 us
  between operations: 15.3 us -> 1.33 us
    all_gather x2 -> x0, waiting for transfers between devices: 649 us -> none  [the longest x1 341 us: on_device(): lax.all_gather(field, 'member', axis=0, tiled=True).astype(jnp.float32)]
    unnamed x1 -> x0, blocking collectives: 372 us -> none
    unnamed x32 -> x0, starting transfers between devices: 86.4 us -> none
    ppermute x0 -> x34, waiting for transfers between devices: none -> 79.9 us  [the longest x14 35.2 us: swap_member(): return lax.ppermute(value, MEMBER, [(i, i ^ step) for i in range(8)])]
    psum x1 -> x0, blocking collectives: 63.2 us -> none  [on_device(): lax.psum((bias_part, gain_portion), ('space', 'member'))]
    pallas_call x0 -> x12, Pallas kernels: none -> 46.7 us  [the longest x1 18.7 us: on_device(): pl.pallas_call(pairs_kernel, out_shape=(jax.ShapeDtypeStruct((features, o...]
    ppermute x0 -> x34, starting transfers between devices: none -> 45.1 us  [the longest x14 20.2 us: swap_member(): return lax.ppermute(value, MEMBER, [(i, i ^ step) for i in range(8)])]
    reduce_sum x5 -> x0, other arithmetic: 30.9 us -> none  [the longest x1 22.1 us: on_device(): pairs = jnp.sum(slope(mine[:, None] - others[None]), axis=1)]
  transfers between devices with their start and end apart: 34 -> 34, of which waited for: 2 -> 18; matrix products, arithmetic and copies ran while one was open for 2% -> 8% of each run, Pallas kernels for 0% -> 14%
where the time goes in v2:
time: 199 us
  waiting for transfers between devices  79.9 us (40%)
  Pallas kernels  46.7 us (23%)
  starting transfers between devices  45.1 us (23%)
  local copies, waits for them, and re-layouts  19.3 us (10%)
  other arithmetic  6.12 us (3%)
    ppermute x14, waiting for transfers between devices, swap_member(): return lax.ppermute(value, MEMBER, [(i, i ^ step) for i in range(8)])  35.2 us
    ppermute x14, waiting for transfers between devices, swap(): return lax.ppermute(value, axis, [(i, i ^ step) for i in range(SIZE[axis])])  28.7 us
    ppermute x14, starting transfers between devices, swap_member(): return lax.ppermute(value, MEMBER, [(i, i ^ step) for i in range(8)])  20.2 us
    pallas_call x1, Pallas kernels, on_device(): pl.pallas_call(pairs_kernel, out_shape=(jax.ShapeDtypeStruct((features, o...  18.7 us
    ppermute x6, waiting for transfers between devices, swap_y(): return lax.ppermute(value, ('yh', 'yl'), [(i, i ^ step) for i in range(4)])  15.9 us
    ppermute x14, starting transfers between devices, swap(): return lax.ppermute(value, axis, [(i, i ^ step) for i in range(SIZE[axis])])  15.2 us
    pallas_call x1, Pallas kernels, on_device(): pl.pallas_call(backward_kernel, out_shape=jax.ShapeDtypeStruct((2, 8, 64,...  13.3 us
    pallas_call x1, Pallas kernels, on_device(): pl.pallas_call(grad_kernel, out_shape=(jax.ShapeDtypeStruct((2, 4, 96, ou...  9.95 us
  transfers between devices with their start and end apart: 34, of which 18 were waited for; matrix products, arithmetic and copies ran while one was open for 8% of the time, Pallas kernels for 14%

profile of v2, /device:TPU:0, one launch (start us, length us, event | category | flops | bytes accessed | tf_op | source)
XLA Modules:
  0.0 199.0 jit_solution(13756838196030888817)
XLA Ops:
  0.6 2.9 %collective-permute-start.2 = (bf16[12,1120]{1,0:T(8,128)(2,1)}, bf16[12,1120]{1,0:T(8,128)(2,1)S(1)}, u32[]{:S(2)}, u32[]{:S(2)}) collective-permute-start(bf16[12,1120]{1,0:T(8,128)(2,1)} %param.9), channel_id=1, source_target_pairs={{0,6},{2,4},{4,2},{6,0},{1,7},{3,5},{5,3},{7,1},{8,14},{10,12},{12... | collective-permute-start | bytes 80648 | tf_op jit(solution)/shard_map/ppermute | solution.py:42
  5.4 3.4 %constant_dynamic-slice_fusion.1 = (bf16[2,1,64,1536]{3,2,1,0:T(8,128)(2,1)S(1)}, bf16[2,64,1536]{2,1,0:T(8,128)(2,1)}, bf16[2,64,1536]{2,1,0:T(8,128)(2,1)}, bf...) fusion(bf16[2,8,64,1536]{3,2,1,0:T(8,128)(2,1)} %bitcast.89, ...), kind=kLoop, calls=%fused_computation.104 | loop fusion | bytes 6291488 | tf_op jit(solution)/shard_map/jit(dynamic_index_in_dim)/dynamic_slice | solution.py:292
  10.5 1.8 collective-permute-start.7
  12.9 3.3 %collective-permute-start.4 = (bf16[4,12,1120]{2,1,0:T(8,128)(2,1)S(1)}, bf16[4,12,1120]{2,1,0:T(8,128)(2,1)S(1)}, u32[]{:S(2)}, u32[]{:S(2)}) collective-permute-start(bf16[4,12,1120]{2,1,0:T(8,128)(2,1)S(1)} %pad_maximum_fusion.10), channel_id=1, source_target_pairs={{0,64},{1,65},{64,0},{65,1},{2,66},{3,67},{66,2},{67,3},{4,68},{5,... | collective-permute-start | bytes 322568 | tf_op jit(solution)/shard_map/ppermute | solution.py:46
  17.2 6.5 %collective-permute-done.3 = bf16[4,12,1120]{2,1,0:T(8,128)(2,1)S(1)} collective-permute-done((bf16[4,12,1120]{2,1,0:T(8,128)(2,1)S(1)}, bf16[4,12,1120]{2,1,0:T(8,128)(2,1)S(1)}, u32[]{:S(2)}, u32[]{:S(2)}) %collective-permute-start.3) | collective-permute-done | bytes 107552 | tf_op jit(solution)/shard_map/ppermute | solution.py:46
  23.9 4.0 %collective-permute-done.4 = bf16[4,12,1120]{2,1,0:T(8,128)(2,1)S(1)} collective-permute-done((bf16[4,12,1120]{2,1,0:T(8,128)(2,1)S(1)}, bf16[4,12,1120]{2,1,0:T(8,128)(2,1)S(1)}, u32[]{:S(2)}, u32[]{:S(2)}) %collective-permute-start.4) | collective-permute-done | bytes 107552 | tf_op jit(solution)/shard_map/ppermute | solution.py:46
  29.4 1.9 collective-permute-start.8
  31.3 3.6 %collective-permute-start.9 = (bf16[2,96,1120]{2,1,0:T(8,128)(2,1)}, bf16[2,96,1120]{2,1,0:T(8,128)(2,1)S(1)}, u32[]{:S(2)}, u32[]{:S(2)}) collective-permute-start(bf16[2,96,1120]{2,1,0:T(8,128)(2,1)} %pad_maximum_fusion.4), channel_id=1, source_target_pairs={{0,32},{16,48},{32,0},{48,16},{1,33},{17,49},{33,1},{49,17},{2,34}... | collective-permute-start | bytes 1290248 | tf_op jit(solution)/shard_map/ppermute | solution.py:42
  35.7 2.8 %collective-permute-start.12 = (bf16[2,64,1536]{2,1,0:T(8,128)(2,1)}, bf16[2,64,1536]{2,1,0:T(8,128)(2,1)S(1)}, u32[]{:S(2)}, u32[]{:S(2)}) collective-permute-start(bf16[2,64,1536]{2,1,0:T(8,128)(2,1)} %get-tuple-element.55), channel_id=1, source_target_pairs={{0,6},{1,7},{2,4},{3,5},{4,2},{5,3},{6,0},{7,1},{8,14},{9,15},{10,... | collective-permute-start | bytes 1179656 | tf_op jit(solution)/shard_map/ppermute | solution.py:50
  38.6 4.3 %collective-permute-done.8 = bf16[2,96,1120]{2,1,0:T(8,128)(2,1)} collective-permute-done((bf16[2,96,1120]{2,1,0:T(8,128)(2,1)}, bf16[2,96,1120]{2,1,0:T(8,128)(2,1)}, u32[]{:S(2)}, u32[]{:S(2)}) %collective-permute-start.8) | collective-permute-done | bytes 430112 | tf_op jit(solution)/shard_map/ppermute | solution.py:42
  42.8 2.3 %collective-permute-start.13 = (bf16[2,64,1536]{2,1,0:T(8,128)(2,1)}, bf16[2,64,1536]{2,1,0:T(8,128)(2,1)S(1)}, u32[]{:S(2)}, u32[]{:S(2)}) collective-permute-start(bf16[2,64,1536]{2,1,0:T(8,128)(2,1)} %get-tuple-element.56), channel_id=1, source_target_pairs={{0,7},{1,6},{2,5},{3,4},{4,3},{5,2},{6,1},{7,0},{8,15},{9,14},{10,... | collective-permute-start | bytes 1179656 | tf_op jit(solution)/shard_map/ppermute | solution.py:50
  45.2 7.4 %collective-permute-done.9 = bf16[2,96,1120]{2,1,0:T(8,128)(2,1)S(1)} collective-permute-done((bf16[2,96,1120]{2,1,0:T(8,128)(2,1)}, bf16[2,96,1120]{2,1,0:T(8,128)(2,1)S(1)}, u32[]{:S(2)}, u32[]{:S(2)}) %collective-permute-start.9) | collective-permute-done | bytes 430112 | tf_op jit(solution)/shard_map/ppermute | solution.py:42
  53.0 2.2 %collective-permute-done.10 = bf16[2,96,1120]{2,1,0:T(8,128)(2,1)} collective-permute-done((bf16[2,96,1120]{2,1,0:T(8,128)(2,1)}, bf16[2,96,1120]{2,1,0:T(8,128)(2,1)}, u32[]{:S(2)}, u32[]{:S(2)}) %collective-permute-start.10) | collective-permute-done | bytes 430112 | tf_op jit(solution)/shard_map/ppermute | solution.py:42
  60.8 3.9 %collective-permute-done.14 = bf16[2,64,1536]{2,1,0:T(8,128)(2,1)S(1)} collective-permute-done((bf16[2,64,1536]{2,1,0:T(8,128)(2,1)}, bf16[2,64,1536]{2,1,0:T(8,128)(2,1)S(1)}, u32[]{:S(2)}, u32[]{:S(2)}) %collective-permute-start.14) | collective-permute-done | bytes 393248 | tf_op jit(solution)/shard_map/ppermute | solution.py:50
  65.5 5.2 %collective-permute-done.15 = bf16[2,64,1536]{2,1,0:T(8,128)(2,1)S(1)} collective-permute-done((bf16[2,64,1536]{2,1,0:T(8,128)(2,1)}, bf16[2,64,1536]{2,1,0:T(8,128)(2,1)S(1)}, u32[]{:S(2)}, u32[]{:S(2)}) %collective-permute-start.15) | collective-permute-done | bytes 393248 | tf_op jit(solution)/shard_map/ppermute | solution.py:50
  81.6 18.7 %pairs.1 = (bf16[1536,1120]{1,0:T(8,128)(2,1)S(1)}, bf16[8,2,64,1120]{3,2,1,0:T(8,128)(2,1)S(1)}, f32[1,1152]{1,0:T(1,128)S(1)}) custom-call(s32[4]{0:T(128)S(1)} %pad_add_fusion.place_ref, bf16[4,2,96,1120]{3,2,1,0:T(8,128)(2,1)S(1)} %pad_maximum_fusion.quad_ref, bf16[4,2,96,1120]{3,2,1,0:T(8,128)(2,1)} %collective-permute-done.16.other_ref, ...), custom_call_target="tpu_custom_call" | custom-call | flops 20000000000 | bytes 80000000 | tf_op jit(solution)/shard_map/pairs/pallas_call | solution.py:338
  101.5 1.9 collective-permute-start.17
  103.4 9.9 %weight_gradient.1 = (f32[2,4,96,1120]{3,2,1,0:T(8,128)S(1)}, bf16[784,1120]{1,0:T(8,128)(2,1)}, f32[8,512]{1,0:T(8,128)S(1)}) custom-call(s32[4]{0:T(128)S(1)} %copy-done.8, bf16[1024,1120]{1,0:T(8,128)(2,1)S(1)} %bitcast.91, bf16[1536,1120]{1,0:T(8,128)(2,1)S(1)} %get-tuple-element.76.full_ref, f32[1,1152]{1,0:T(1,128)S(1)} %get-tuple-element.77.bias_part_ref, ...), custom_call_target="tpu_custom_call" | custom-call | flops 12000000000 | bytes 45000000 | tf_op jit(solution)/shard_map/weight_gradient/pallas_call | solution.py:358
  113.4 4.0 %collective-permute-done.17.refs_1_ = bf16[2,64,1120]{2,1,0:T(8,128)(2,1)S(1)} collective-permute-done((bf16[2,64,1120]{2,1,0:T(8,128)(2,1)S(1)}, bf16[2,64,1120]{2,1,0:T(8,128)(2,1)S(1)}, u32[]{:S(2)}, u32[]{:S(2)}) %collective-permute-start.17) | collective-permute-done | bytes 286752 | tf_op jit(solution)/shard_map/ppermute | solution.py:50
  118.9 1.9 collective-permute-start.24
  120.8 2.8 %collective-permute-start.25 = (bf16[2,64,1120]{2,1,0:T(8,128)(2,1)}, bf16[2,64,1120]{2,1,0:T(8,128)(2,1)S(1)}, u32[]{:S(2)}, u32[]{:S(2)}) collective-permute-start(bf16[2,64,1120]{2,1,0:T(8,128)(2,1)} %get-tuple-element.94), channel_id=1, source_target_pairs={{0,5},{1,4},{2,7},{3,6},{4,1},{5,0},{6,3},{7,2},{8,13},{9,12},{10,... | collective-permute-start | bytes 860168 | tf_op jit(solution)/shard_map/ppermute | solution.py:50
  124.7 1.8 collective-permute-start.27
  130.5 4.7 %collective-permute-done.24.refs_4_ = bf16[2,64,1120]{2,1,0:T(8,128)(2,1)S(1)} collective-permute-done((bf16[2,64,1120]{2,1,0:T(8,128)(2,1)}, bf16[2,64,1120]{2,1,0:T(8,128)(2,1)S(1)}, u32[]{:S(2)}, u32[]{:S(2)}) %collective-permute-start.24) | collective-permute-done | bytes 286752 | tf_op jit(solution)/shard_map/ppermute | solution.py:50
  135.2 7.1 %collective-permute-done.25.refs_5_ = bf16[2,64,1120]{2,1,0:T(8,128)(2,1)S(1)} collective-permute-done((bf16[2,64,1120]{2,1,0:T(8,128)(2,1)}, bf16[2,64,1120]{2,1,0:T(8,128)(2,1)S(1)}, u32[]{:S(2)}, u32[]{:S(2)}) %collective-permute-start.25) | collective-permute-done | bytes 286752 | tf_op jit(solution)/shard_map/ppermute | solution.py:50
  142.3 4.9 %collective-permute-done.26.refs_6_ = bf16[2,64,1120]{2,1,0:T(8,128)(2,1)S(1)} collective-permute-done((bf16[2,64,1120]{2,1,0:T(8,128)(2,1)}, bf16[2,64,1120]{2,1,0:T(8,128)(2,1)S(1)}, u32[]{:S(2)}, u32[]{:S(2)}) %collective-permute-start.26) | collective-permute-done | bytes 286752 | tf_op jit(solution)/shard_map/ppermute | solution.py:50
  147.2 5.3 %collective-permute-done.27.refs_7_ = bf16[2,64,1120]{2,1,0:T(8,128)(2,1)S(1)} collective-permute-done((bf16[2,64,1120]{2,1,0:T(8,128)(2,1)}, bf16[2,64,1120]{2,1,0:T(8,128)(2,1)S(1)}, u32[]{:S(2)}, u32[]{:S(2)}) %collective-permute-start.27) | collective-permute-done | bytes 286752 | tf_op jit(solution)/shard_map/ppermute | solution.py:50
  152.6 13.3 %backward.1 = bf16[2,8,64,1536]{3,2,1,0:T(8,128)(2,1)} custom-call(s32[4]{0:T(128)S(1)} %copy-done.9, bf16[2,8,64,1536]{3,2,1,0:T(8,128)(2,1)S(1)} %bitcast.90, f32[1,1536]{1,0:T(1,128)S(1)} %copy-done.6, bf16[1536,1120]{1,0:T(8,128)(2,1)S(1)} %copy-done.23, bf16[2,64,1120]{2,1,0:T(8,128)(2,1)S(1)} %copy-done.3, bf16[2,64,1120]{2,1,0:T(8,128)(2,1)S(1)} %copy-done.19, ...), custom_call_target="tpu_custom_call" | custom-call | flops 16000000000 | bytes 60000000 | tf_op jit(solution)/shard_map/backward/pallas_call | solution.py:408
  166.0 11.8 %collective-permute-done.20 = bf16[208,1120]{1,0:T(8,128)(2,1)S(1)} collective-permute-done((bf16[208,1120]{1,0:T(8,128)(2,1)S(1)}, bf16[208,1120]{1,0:T(8,128)(2,1)S(1)}, u32[]{:S(2)}, u32[]{:S(2)}) %collective-permute-start.20) | collective-permute-done | bytes 465952 | tf_op jit(solution)/shard_map/ppermute | solution.py:42
  178.5 2.1 %collective-permute-start.28 = (bf16[64,1120]{1,0:T(8,128)(2,1)S(1)}, bf16[64,1120]{1,0:T(8,128)(2,1)S(1)}, u32[]{:S(2)}, u32[]{:S(2)}) collective-permute-start(bf16[64,1120]{1,0:T(8,128)(2,1)S(1)} %get-tuple-element.133), channel_id=1, source_target_pairs={{0,1},{1,0},{64,65},{65,64},{2,3},{3,2},{66,67},{67,66},{4,5},{5,4... | collective-permute-start | bytes 430088 | tf_op jit(solution)/shard_map/ppermute | solution.py:46
  181.0 2.4 %collective-permute-start.30 = (bf16[64,1120]{1,0:T(8,128)(2,1)S(1)}, bf16[64,1120]{1,0:T(8,128)(2,1)S(1)}, u32[]{:S(2)}, u32[]{:S(2)}) collective-permute-start(bf16[64,1120]{1,0:T(8,128)(2,1)S(1)} %get-tuple-element.135), channel_id=1, source_target_pairs={{0,65},{1,64},{64,1},{65,0},{2,67},{3,66},{66,3},{67,2},{4,69},{5,... | collective-permute-start | bytes 430088 | tf_op jit(solution)/shard_map/ppermute | solution.py:46
  184.7 2.7 %collective-permute-done.29 = bf16[64,1120]{1,0:T(8,128)(2,1)S(1)} collective-permute-done((bf16[64,1120]{1,0:T(8,128)(2,1)S(1)}, bf16[64,1120]{1,0:T(8,128)(2,1)S(1)}, u32[]{:S(2)}, u32[]{:S(2)}) %collective-permute-start.29) | collective-permute-done | bytes 143392 | tf_op jit(solution)/shard_map/ppermute | solution.py:46
  190.9 3.0 %collective-permute-start.32 = (bf16[28,1120]{1,0:T(8,128)(2,1)S(1)}, bf16[28,1120]{1,0:T(8,128)(2,1)S(1)}, u32[]{:S(2)}, u32[]{:S(2)}) collective-permute-start(bf16[28,1120]{1,0:T(8,128)(2,1)S(1)} %get-tuple-element.131), channel_id=1, source_target_pairs={{0,4},{2,6},{4,0},{6,2},{1,5},{3,7},{5,1},{7,3},{8,12},{10,14},{12... | collective-permute-start | bytes 188168 | tf_op jit(solution)/shard_map/ppermute | solution.py:42
  (173 shorter events, 43.8 us)
Async XLA Ops:
  0.6 11.7 %collective-permute-start.2 = (bf16[12,1120]{1,0:T(8,128)(2,1)}, bf16[12,1120]{1,0:T(8,128)(2,1)S(1)}, u32[]{:S(2)}, u32[]{:S(2)}) collective-permute-start(bf16[12,1120]{1,0:T(8,128)(2,1)} %param.9), channel_id=1, source_target_pairs={{0,6},{2,4},{4,2},{6,0},{1,7},{3,5},{5,3},{7,1},{8,14},{10,12},{12... | collective-permute-start | bytes 80648 | tf_op jit(solution)/shard_map/ppermute | solution.py:42
  3.6 8.7 %collective-permute-start = (bf16[12,1120]{1,0:T(8,128)(2,1)}, bf16[12,1120]{1,0:T(8,128)(2,1)S(1)}, u32[]{:S(2)}, u32[]{:S(2)}) collective-permute-start(bf16[12,1120]{1,0:T(8,128)(2,1)} %param.9), channel_id=1, source_target_pairs={{0,2},{2,0},{4,6},{6,4},{1,3},{3,1},{5,7},{7,5},{8,10},{10,8},{12,... | collective-permute-start | bytes 80648 | tf_op jit(solution)/shard_map/ppermute | solution.py:42
  3.8 8.5 %collective-permute-start.1 = (bf16[12,1120]{1,0:T(8,128)(2,1)}, bf16[12,1120]{1,0:T(8,128)(2,1)S(1)}, u32[]{:S(2)}, u32[]{:S(2)}) collective-permute-start(bf16[12,1120]{1,0:T(8,128)(2,1)} %param.9), channel_id=1, source_target_pairs={{0,4},{2,6},{4,0},{6,2},{1,5},{3,7},{5,1},{7,3},{8,12},{10,14},{12... | collective-permute-start | bytes 80648 | tf_op jit(solution)/shard_map/ppermute | solution.py:42
  8.8 20.6 %collective-permute-start.6 = (bf16[2,64,1536]{2,1,0:T(8,128)(2,1)}, bf16[2,64,1536]{2,1,0:T(8,128)(2,1)S(1)}, u32[]{:S(2)}, u32[]{:S(2)}) collective-permute-start(bf16[2,64,1536]{2,1,0:T(8,128)(2,1)} %get-tuple-element.108), channel_id=1, source_target_pairs={{0,1},{1,0},{2,3},{3,2},{4,5},{5,4},{6,7},{7,6},{8,9},{9,8},{10,11... | collective-permute-start | bytes 1179656 | tf_op jit(solution)/shard_map/ppermute | solution.py:50
  10.5 18.9 %collective-permute-start.7 = (bf16[2,64,1536]{2,1,0:T(8,128)(2,1)}, bf16[2,64,1536]{2,1,0:T(8,128)(2,1)S(1)}, u32[]{:S(2)}, u32[]{:S(2)}) collective-permute-start(bf16[2,64,1536]{2,1,0:T(8,128)(2,1)} %get-tuple-element.107), channel_id=1, source_target_pairs={{0,4},{1,5},{2,6},{3,7},{4,0},{5,1},{6,2},{7,3},{8,12},{9,13},{10,... | collective-permute-start | bytes 1179656 | tf_op jit(solution)/shard_map/ppermute | solution.py:50
  12.4 11.4 %collective-permute-start.3 = (bf16[4,12,1120]{2,1,0:T(8,128)(2,1)S(1)}, bf16[4,12,1120]{2,1,0:T(8,128)(2,1)S(1)}, u32[]{:S(2)}, u32[]{:S(2)}) collective-permute-start(bf16[4,12,1120]{2,1,0:T(8,128)(2,1)S(1)} %pad_maximum_fusion.10), channel_id=1, source_target_pairs={{0,1},{1,0},{64,65},{65,64},{2,3},{3,2},{66,67},{67,66},{4,5},{5,4... | collective-permute-start | bytes 322568 | tf_op jit(solution)/shard_map/ppermute | solution.py:46
  12.9 15.0 %collective-permute-start.4 = (bf16[4,12,1120]{2,1,0:T(8,128)(2,1)S(1)}, bf16[4,12,1120]{2,1,0:T(8,128)(2,1)S(1)}, u32[]{:S(2)}, u32[]{:S(2)}) collective-permute-start(bf16[4,12,1120]{2,1,0:T(8,128)(2,1)S(1)} %pad_maximum_fusion.10), channel_id=1, source_target_pairs={{0,64},{1,65},{64,0},{65,1},{2,66},{3,67},{66,2},{67,3},{4,68},{5,... | collective-permute-start | bytes 322568 | tf_op jit(solution)/shard_map/ppermute | solution.py:46
  16.2 11.7 %collective-permute-start.5 = (bf16[4,12,1120]{2,1,0:T(8,128)(2,1)S(1)}, bf16[4,12,1120]{2,1,0:T(8,128)(2,1)S(1)}, u32[]{:S(2)}, u32[]{:S(2)}) collective-permute-start(bf16[4,12,1120]{2,1,0:T(8,128)(2,1)S(1)} %pad_maximum_fusion.10), channel_id=1, source_target_pairs={{0,65},{1,64},{64,1},{65,0},{2,67},{3,66},{66,3},{67,2},{4,69},{5,... | collective-permute-start | bytes 322568 | tf_op jit(solution)/shard_map/ppermute | solution.py:46
  29.4 13.4 %collective-permute-start.8 = (bf16[2,96,1120]{2,1,0:T(8,128)(2,1)}, bf16[2,96,1120]{2,1,0:T(8,128)(2,1)}, u32[]{:S(2)}, u32[]{:S(2)}) collective-permute-start(bf16[2,96,1120]{2,1,0:T(8,128)(2,1)} %pad_maximum_fusion.4), channel_id=1, source_target_pairs={{0,16},{16,0},{32,48},{48,32},{1,17},{17,1},{33,49},{49,33},{2,18}... | collective-permute-start | bytes 1290248 | tf_op jit(solution)/shard_map/ppermute | solution.py:42
  31.3 21.2 %collective-permute-start.9 = (bf16[2,96,1120]{2,1,0:T(8,128)(2,1)}, bf16[2,96,1120]{2,1,0:T(8,128)(2,1)S(1)}, u32[]{:S(2)}, u32[]{:S(2)}) collective-permute-start(bf16[2,96,1120]{2,1,0:T(8,128)(2,1)} %pad_maximum_fusion.4), channel_id=1, source_target_pairs={{0,32},{16,48},{32,0},{48,16},{1,33},{17,49},{33,1},{49,17},{2,34}... | collective-permute-start | bytes 1290248 | tf_op jit(solution)/shard_map/ppermute | solution.py:42
  34.9 20.3 %collective-permute-start.10 = (bf16[2,96,1120]{2,1,0:T(8,128)(2,1)}, bf16[2,96,1120]{2,1,0:T(8,128)(2,1)}, u32[]{:S(2)}, u32[]{:S(2)}) collective-permute-start(bf16[2,96,1120]{2,1,0:T(8,128)(2,1)} %pad_maximum_fusion.4), channel_id=1, source_target_pairs={{0,48},{16,32},{32,16},{48,0},{1,49},{17,33},{33,17},{49,1},{2,50}... | collective-permute-start | bytes 1290248 | tf_op jit(solution)/shard_map/ppermute | solution.py:42
  35.7 23.6 %collective-permute-start.11 = (bf16[2,64,1536]{2,1,0:T(8,128)(2,1)}, bf16[2,64,1536]{2,1,0:T(8,128)(2,1)S(1)}, u32[]{:S(2)}, u32[]{:S(2)}) collective-permute-start(bf16[2,64,1536]{2,1,0:T(8,128)(2,1)} %get-tuple-element.54), channel_id=1, source_target_pairs={{0,3},{1,2},{2,1},{3,0},{4,7},{5,6},{6,5},{7,4},{8,11},{9,10},{10,... | collective-permute-start | bytes 1179656 | tf_op jit(solution)/shard_map/ppermute | solution.py:50
  35.7 24.4 %collective-permute-start.12 = (bf16[2,64,1536]{2,1,0:T(8,128)(2,1)}, bf16[2,64,1536]{2,1,0:T(8,128)(2,1)S(1)}, u32[]{:S(2)}, u32[]{:S(2)}) collective-permute-start(bf16[2,64,1536]{2,1,0:T(8,128)(2,1)} %get-tuple-element.55), channel_id=1, source_target_pairs={{0,6},{1,7},{2,4},{3,5},{4,2},{5,3},{6,0},{7,1},{8,14},{9,15},{10,... | collective-permute-start | bytes 1179656 | tf_op jit(solution)/shard_map/ppermute | solution.py:50
  42.8 17.3 %collective-permute-start.13 = (bf16[2,64,1536]{2,1,0:T(8,128)(2,1)}, bf16[2,64,1536]{2,1,0:T(8,128)(2,1)S(1)}, u32[]{:S(2)}, u32[]{:S(2)}) collective-permute-start(bf16[2,64,1536]{2,1,0:T(8,128)(2,1)} %get-tuple-element.56), channel_id=1, source_target_pairs={{0,7},{1,6},{2,5},{3,4},{4,3},{5,2},{6,1},{7,0},{8,15},{9,14},{10,... | collective-permute-start | bytes 1179656 | tf_op jit(solution)/shard_map/ppermute | solution.py:50
  52.5 12.2 %collective-permute-start.14 = (bf16[2,64,1536]{2,1,0:T(8,128)(2,1)}, bf16[2,64,1536]{2,1,0:T(8,128)(2,1)S(1)}, u32[]{:S(2)}, u32[]{:S(2)}) collective-permute-start(bf16[2,64,1536]{2,1,0:T(8,128)(2,1)} %get-tuple-element.57), channel_id=1, source_target_pairs={{0,2},{1,3},{2,0},{3,1},{4,6},{5,7},{6,4},{7,5},{8,10},{9,11},{10,... | collective-permute-start | bytes 1179656 | tf_op jit(solution)/shard_map/ppermute | solution.py:50
  55.2 15.5 %collective-permute-start.15 = (bf16[2,64,1536]{2,1,0:T(8,128)(2,1)}, bf16[2,64,1536]{2,1,0:T(8,128)(2,1)S(1)}, u32[]{:S(2)}, u32[]{:S(2)}) collective-permute-start(bf16[2,64,1536]{2,1,0:T(8,128)(2,1)} %get-tuple-element.58), channel_id=1, source_target_pairs={{0,5},{1,4},{2,7},{3,6},{4,1},{5,0},{6,3},{7,2},{8,13},{9,12},{10,... | collective-permute-start | bytes 1179656 | tf_op jit(solution)/shard_map/ppermute | solution.py:50
  71.5 10.0 %collective-permute-start.16 = (bf16[4,2,96,1120]{3,2,1,0:T(8,128)(2,1)S(1)}, bf16[4,2,96,1120]{3,2,1,0:T(8,128)(2,1)}, u32[]{:S(2)}, u32[]{:S(2)}) collective-permute-start(bf16[4,2,96,1120]{3,2,1,0:T(8,128)(2,1)S(1)} %pad_maximum_fusion.quad_ref), channel_id=1, source_target_pairs={{0,8},{8,0},{1,9},{9,1},{2,10},{10,2},{3,11},{11,3},{4,12},{12,4},... | collective-permute-start | bytes 5160968 | tf_op jit(solution)/shard_map/ppermute | solution.py:42
  101.5 15.9 %collective-permute-start.17 = (bf16[2,64,1120]{2,1,0:T(8,128)(2,1)S(1)}, bf16[2,64,1120]{2,1,0:T(8,128)(2,1)S(1)}, u32[]{:S(2)}, u32[]{:S(2)}) collective-permute-start(bf16[2,64,1120]{2,1,0:T(8,128)(2,1)S(1)} %get-tuple-element.116), channel_id=1, source_target_pairs={{0,1},{1,0},{2,3},{3,2},{4,5},{5,4},{6,7},{7,6},{8,9},{9,8},{10,11... | collective-permute-start | bytes 860168 | tf_op jit(solution)/shard_map/ppermute | solution.py:50
  103.4 14.7 %collective-permute-start.18 = (bf16[2,64,1120]{2,1,0:T(8,128)(2,1)S(1)}, bf16[2,64,1120]{2,1,0:T(8,128)(2,1)S(1)}, u32[]{:S(2)}, u32[]{:S(2)}) collective-permute-start(bf16[2,64,1120]{2,1,0:T(8,128)(2,1)S(1)} %get-tuple-element.115), channel_id=1, source_target_pairs={{0,3},{1,2},{2,1},{3,0},{4,7},{5,6},{6,5},{7,4},{8,11},{9,10},{10,... | collective-permute-start | bytes 860168 | tf_op jit(solution)/shard_map/ppermute | solution.py:50
  118.9 11.6 %collective-permute-start.23 = (bf16[2,64,1120]{2,1,0:T(8,128)(2,1)}, bf16[2,64,1120]{2,1,0:T(8,128)(2,1)S(1)}, u32[]{:S(2)}, u32[]{:S(2)}) collective-permute-start(bf16[2,64,1120]{2,1,0:T(8,128)(2,1)} %get-tuple-element.91), channel_id=1, source_target_pairs={{0,2},{1,3},{2,0},{3,1},{4,6},{5,7},{6,4},{7,5},{8,10},{9,11},{10,... | collective-permute-start | bytes 860168 | tf_op jit(solution)/shard_map/ppermute | solution.py:50
  118.9 16.3 %collective-permute-start.24 = (bf16[2,64,1120]{2,1,0:T(8,128)(2,1)}, bf16[2,64,1120]{2,1,0:T(8,128)(2,1)S(1)}, u32[]{:S(2)}, u32[]{:S(2)}) collective-permute-start(bf16[2,64,1120]{2,1,0:T(8,128)(2,1)} %get-tuple-element.93), channel_id=1, source_target_pairs={{0,4},{1,5},{2,6},{3,7},{4,0},{5,1},{6,2},{7,3},{8,12},{9,13},{10,... | collective-permute-start | bytes 860168 | tf_op jit(solution)/shard_map/ppermute | solution.py:50
  120.8 21.5 %collective-permute-start.25 = (bf16[2,64,1120]{2,1,0:T(8,128)(2,1)}, bf16[2,64,1120]{2,1,0:T(8,128)(2,1)S(1)}, u32[]{:S(2)}, u32[]{:S(2)}) collective-permute-start(bf16[2,64,1120]{2,1,0:T(8,128)(2,1)} %get-tuple-element.94), channel_id=1, source_target_pairs={{0,5},{1,4},{2,7},{3,6},{4,1},{5,0},{6,3},{7,2},{8,13},{9,12},{10,... | collective-permute-start | bytes 860168 | tf_op jit(solution)/shard_map/ppermute | solution.py:50
  123.6 23.7 %collective-permute-start.26 = (bf16[2,64,1120]{2,1,0:T(8,128)(2,1)}, bf16[2,64,1120]{2,1,0:T(8,128)(2,1)S(1)}, u32[]{:S(2)}, u32[]{:S(2)}) collective-permute-start(bf16[2,64,1120]{2,1,0:T(8,128)(2,1)} %get-tuple-element.95), channel_id=1, source_target_pairs={{0,6},{1,7},{2,4},{3,5},{4,2},{5,3},{6,0},{7,1},{8,14},{9,15},{10,... | collective-permute-start | bytes 860168 | tf_op jit(solution)/shard_map/ppermute | solution.py:50
  124.7 27.8 %collective-permute-start.27 = (bf16[2,64,1120]{2,1,0:T(8,128)(2,1)}, bf16[2,64,1120]{2,1,0:T(8,128)(2,1)S(1)}, u32[]{:S(2)}, u32[]{:S(2)}) collective-permute-start(bf16[2,64,1120]{2,1,0:T(8,128)(2,1)} %get-tuple-element.96), channel_id=1, source_target_pairs={{0,7},{1,6},{2,5},{3,4},{4,3},{5,2},{6,1},{7,0},{8,15},{9,14},{10,... | collective-permute-start | bytes 860168 | tf_op jit(solution)/shard_map/ppermute | solution.py:50
  130.4 35.5 %collective-permute-start.22 = (bf16[208,1120]{1,0:T(8,128)(2,1)S(1)}, bf16[208,1120]{1,0:T(8,128)(2,1)S(1)}, u32[]{:S(2)}, u32[]{:S(2)}) collective-permute-start(bf16[208,1120]{1,0:T(8,128)(2,1)S(1)} %get-tuple-element.138), channel_id=1, source_target_pairs={{0,48},{16,32},{32,16},{48,0},{1,49},{17,33},{33,17},{49,1},{2,50}... | collective-permute-start | bytes 1397768 | tf_op jit(solution)/shard_map/ppermute | solution.py:42
  135.2 30.8 %collective-permute-start.21 = (bf16[208,1120]{1,0:T(8,128)(2,1)S(1)}, bf16[208,1120]{1,0:T(8,128)(2,1)S(1)}, u32[]{:S(2)}, u32[]{:S(2)}) collective-permute-start(bf16[208,1120]{1,0:T(8,128)(2,1)S(1)} %get-tuple-element.137), channel_id=1, source_target_pairs={{0,32},{16,48},{32,0},{48,16},{1,33},{17,49},{33,1},{49,17},{2,34}... | collective-permute-start | bytes 1397768 | tf_op jit(solution)/shard_map/ppermute | solution.py:42
  165.9 11.9 %collective-permute-start.20 = (bf16[208,1120]{1,0:T(8,128)(2,1)S(1)}, bf16[208,1120]{1,0:T(8,128)(2,1)S(1)}, u32[]{:S(2)}, u32[]{:S(2)}) collective-permute-start(bf16[208,1120]{1,0:T(8,128)(2,1)S(1)} %get-tuple-element.136), channel_id=1, source_target_pairs={{0,16},{16,0},{32,48},{48,32},{1,17},{17,1},{33,49},{49,33},{2,18}... | collective-permute-start | bytes 1397768 | tf_op jit(solution)/shard_map/ppermute | solution.py:42
  180.6 6.7 %collective-permute-start.29 = (bf16[64,1120]{1,0:T(8,128)(2,1)S(1)}, bf16[64,1120]{1,0:T(8,128)(2,1)S(1)}, u32[]{:S(2)}, u32[]{:S(2)}) collective-permute-start(bf16[64,1120]{1,0:T(8,128)(2,1)S(1)} %get-tuple-element.134), channel_id=1, source_target_pairs={{0,64},{1,65},{64,0},{65,1},{2,66},{3,67},{66,2},{67,3},{4,68},{5,... | collective-permute-start | bytes 430088 | tf_op jit(solution)/shard_map/ppermute | solution.py:46
  181.0 7.9 %collective-permute-start.30 = (bf16[64,1120]{1,0:T(8,128)(2,1)S(1)}, bf16[64,1120]{1,0:T(8,128)(2,1)S(1)}, u32[]{:S(2)}, u32[]{:S(2)}) collective-permute-start(bf16[64,1120]{1,0:T(8,128)(2,1)S(1)} %get-tuple-element.135), channel_id=1, source_target_pairs={{0,65},{1,64},{64,1},{65,0},{2,67},{3,66},{66,3},{67,2},{4,69},{5,... | collective-permute-start | bytes 430088 | tf_op jit(solution)/shard_map/ppermute | solution.py:46
  189.2 6.4 %collective-permute-start.33 = (bf16[28,1120]{1,0:T(8,128)(2,1)S(1)}, bf16[28,1120]{1,0:T(8,128)(2,1)S(1)}, u32[]{:S(2)}, u32[]{:S(2)}) collective-permute-start(bf16[28,1120]{1,0:T(8,128)(2,1)S(1)} %get-tuple-element.132), channel_id=1, source_target_pairs={{0,6},{2,4},{4,2},{6,0},{1,7},{3,5},{5,3},{7,1},{8,14},{10,12},{12... | collective-permute-start | bytes 188168 | tf_op jit(solution)/shard_map/ppermute | solution.py:42
  190.1 7.0 %collective-permute-start.31 = (bf16[28,1120]{1,0:T(8,128)(2,1)S(1)}, bf16[28,1120]{1,0:T(8,128)(2,1)S(1)}, u32[]{:S(2)}, u32[]{:S(2)}) collective-permute-start(bf16[28,1120]{1,0:T(8,128)(2,1)S(1)} %get-tuple-element.130), channel_id=1, source_target_pairs={{0,2},{2,0},{4,6},{6,4},{1,3},{3,1},{5,7},{7,5},{8,10},{10,8},{12,... | collective-permute-start | bytes 188168 | tf_op jit(solution)/shard_map/ppermute | solution.py:42
  190.9 6.2 %collective-permute-start.32 = (bf16[28,1120]{1,0:T(8,128)(2,1)S(1)}, bf16[28,1120]{1,0:T(8,128)(2,1)S(1)}, u32[]{:S(2)}, u32[]{:S(2)}) collective-permute-start(bf16[28,1120]{1,0:T(8,128)(2,1)S(1)} %get-tuple-element.131), channel_id=1, source_target_pairs={{0,4},{2,6},{4,0},{6,2},{1,5},{3,7},{5,1},{7,3},{8,12},{10,14},{12... | collective-permute-start | bytes 188168 | tf_op jit(solution)/shard_map/ppermute | solution.py:42
  (31 other events, 332.0 us)

commit v3 on v2

--- a/solution.py
+++ b/solution.py
@@ -16,6 +16,7 @@
 SPACE = ("yh", "z", "core")
 MEMBER = ("x", "yl")
 BF16 = jnp.bfloat16
+FIRST, SECOND = (0, 1, 4, 5), (3, 6, 7, 2)
 F32 = jnp.float32
 
 
@@ -109,7 +110,8 @@
     place_ref, quad_ref, other_ref, bias_ref, truth_ref, wt_ref, *refs
 ):
     pieces = refs[:8]
-    full_ref, dfield_ref, bias_out_ref, normed_ref, field, sums = refs[8:]
+    full_ref, bias_out_ref, *dfield_refs = refs[8:18]
+    normed_ref, field, sums = refs[18:]
     for k in range(8):
         normed_ref[pl.ds(128 * k, 128), :] = pieces[k][...]
     width = full_ref.shape[1]
@@ -161,18 +163,17 @@
     lax.fori_loop(0, 8 * tiles, pairs, 0)
     bias_out_ref[...] = jnp.sum(sums[...], axis=0, keepdims=True)
 
-    def store(step, carry):
-        dfield_ref[step] = field[pl.ds(step * 2, 2), :, 0:width].astype(BF16)
-        return carry
-
-    lax.fori_loop(0, count // 2, store, 0)
-
-
-def grad_kernel(place_ref, dfield_ref, full_ref, bias_part_ref, gain_ref, *refs):
-    pieces = refs[:8]
-    keep_ref, send_ref, small_ref, flipped_ref, grad, rows = refs[8:]
+    for k in range(8):
+        for m in range(2):
+            dfield_refs[k][64 * m : 64 * m + 64, :] = field[2 * k + m, :, 0:width].astype(BF16)
+
+
+def grad_kernel(place_ref, full_ref, bias_part_ref, gain_ref, *refs):
+    pieces, fields = refs[:8], refs[8:16]
+    keep_ref, send_ref, small_ref, flipped_ref, dfield_ref, grad, rows = refs[16:]
     for k in range(8):
         flipped_ref[:, pl.ds(128 * k, 128)] = pieces[k][...]
+        dfield_ref[pl.ds(128 * k, 128), :] = fields[k][...]
     width = full_ref.shape[1]
     features = full_ref.shape[0]
 
@@ -201,11 +202,7 @@
         small_ref[n : n + 1, :] = rows[0:1, cut] / gain_ref[:, cut]
         stop = min(512 * (n + 1), width)
         small_ref[3 + n : 4 + n, 0 : stop - 512 * n] = bias_part_ref[:, 512 * n : stop]
-    small = small_ref[...]
-    high = small.astype(BF16)
-    low = (small - high.astype(F32)).astype(BF16)
-    send_ref[0:16, :] = jnp.zeros((16, width), BF16)
-    send_ref[0:16, 0:512] = jnp.concatenate([high, low], axis=0)
+    put_small(send_ref, small_ref[...])
     for yh in range(2):
         for step in range(4):
             base = (place_ref[0] ^ yh) * 8 + (place_ref[1] ^ step) * 2
@@ -216,11 +213,13 @@
             send_ref[start : start + 96, :] = grad[pl.ds(other, 96), :].astype(BF16)
 
 
-def backward_kernel(place_ref, tokens_ref, gain_ref, full_ref, *refs):
-    pieces, out_ref, dfield, grad = refs[:8], refs[8], refs[9], refs[10]
+def backward_kernel(order, before, place_ref, tokens_ref, gain_ref, full_ref, *refs):
+    count = len(order)
+    earlier, pieces = refs[:before], refs[before : before + count]
+    out_ref, dfield, grad = refs[before + count :]
     features = full_ref.shape[0]
-    for k in range(8):
-        dfield[pl.ds(128 * k, 128), :] = pieces[k][...].reshape(128, -1)
+    for n in range(count):
+        dfield[pl.ds(128 * n, 128), :] = pieces[n][...].reshape(128, -1)
 
     def matmul(step, carry):
         lane = pl.multiple_of(step * 256, 256)
@@ -231,26 +230,34 @@
         return carry
 
     lax.fori_loop(0, features // 256, matmul, 0)
-
-    def rows(step, carry):
-        k, m = step // 2, step % 2
+    for n, k in enumerate(order):
         j = place_ref[3] ^ k
-        wide = tokens_ref[m, j].astype(F32)
-        mean = jnp.mean(wide, -1, keepdims=True)
-        centred = wide - mean
-        variance = jnp.mean(centred * centred, -1, keepdims=True)
-        inverse = lax.rsqrt(variance + EPS)
-        xhat = centred * inverse
-        scaled = grad[pl.ds(pl.multiple_of(step * 64, 64), 64), :] * gain_ref[...]
-        out = inverse * (
-            scaled
-            - jnp.mean(scaled, -1, keepdims=True)
-            - xhat * jnp.mean(scaled * xhat, -1, keepdims=True)
-        )
-        out_ref[m, j] = out.astype(BF16)
-        return carry
-
-    lax.fori_loop(0, 16, rows, 0)
+
+        def rows(m, carry, n=n, j=j):
+            wide = tokens_ref[m, j].astype(F32)
+            mean = jnp.mean(wide, -1, keepdims=True)
+            centred = wide - mean
+            variance = jnp.mean(centred * centred, -1, keepdims=True)
+            inverse = lax.rsqrt(variance + EPS)
+            xhat = centred * inverse
+            start = pl.multiple_of(128 * n + m * 64, 64)
+            scaled = grad[pl.ds(start, 64), :] * gain_ref[...]
+            out = inverse * (
+                scaled
+                - jnp.mean(scaled, -1, keepdims=True)
+                - xhat * jnp.mean(scaled * xhat, -1, keepdims=True)
+            )
+            if before:
+                out_ref[m, j] = out.astype(BF16)
+            else:
+                out_ref[n, m] = out.astype(BF16)
+            return carry
+
+        lax.fori_loop(0, 2, rows, 0)
+    if before:
+        for n, k in enumerate(FIRST):
+            for m in range(2):
+                out_ref[m, place_ref[3] ^ k] = earlier[0][n, m]
 
 
 def member_rows(parts, where):
@@ -258,29 +265,103 @@
     members = 8 * rows
     index = jnp.arange(members)
     block, inside = index // rows, index % rows
-    source = (((block % 2) ^ where["yl"]) * 4 + ((block // 2) ^ where["x"])) * rows + inside
+    source = (((block // 2) ^ where["x"]) * 2 + ((block % 2) ^ where["yl"])) * rows + inside
     pick = (source[:, None] == jnp.arange(members)[None, :]).astype(BF16)
     return jnp.dot(
         pick, parts.reshape(members, width), preferred_element_type=F32
     ).astype(BF16)
 
 
-def pack(small, width):
-    high = lax.reduce_precision(small, 8, 7)
-    both = jnp.concatenate([high, small - high], axis=0).astype(BF16)
-    return jnp.pad(both, ((0, 0), (0, width - both.shape[1])))
-
-
-def unpack(rows):
-    rows = rows[:, :512].astype(F32)
-    return rows[:8] + rows[8:16]
+def put_small(ref, small):
+    high = small.astype(BF16)
+    low = (small - high.astype(F32)).astype(BF16)
+    ref[0:16, :] = jnp.zeros((16, ref.shape[1]), BF16)
+    ref[0:16, 0:512] = jnp.concatenate([high, low], axis=0)
+
+
+def get_small(ref):
+    rows = ref[0:16, 0:512].astype(F32)
+    return rows[0:8] + rows[8:16]
+
+
+def rows_of(picked, values):
+    high = values.astype(BF16)
+    low = (values - high.astype(F32)).astype(BF16)
+    picked = picked.astype(BF16)
+    return jnp.dot(picked, high, preferred_element_type=F32), jnp.dot(
+        picked, low, preferred_element_type=F32
+    )
+
+
+def core_kernel(keep_ref, small_ref, came_ref, own_ref, small_out_ref, *sends):
+    small = small_ref[...] + get_small(came_ref)
+    small_out_ref[...] = small
+    for step in range(4):
+        for yh in range(2):
+            start = 16 + 96 * (yh * 4 + step)
+            block = keep_ref[yh, step] + came_ref[start : start + 96, :].astype(F32)
+            if step == 0:
+                own_ref[96 * yh : 96 * yh + 96, :] = block
+            else:
+                sends[step - 1][16 + 96 * yh : 112 + 96 * yh, :] = block.astype(BF16)
+    for ref in sends:
+        put_small(ref, small)
+
+
+def iota(shape, axis):
+    return lax.broadcasted_iota(jnp.int32, shape, axis)
+
+
+def gather_sums(own_ref, small_ref, came):
+    total, small = own_ref[...], small_ref[...]
+    for ref in came:
+        total = total + ref[16 : 16 + own_ref.shape[0], :].astype(F32)
+        small = small + get_small(ref)
+    return total, small
+
+
+def z_kernel(place_ref, own_ref, small_ref, a_ref, b_ref, c_ref, own_out_ref, small_out_ref, *sends):
+    total, small = gather_sums(own_ref, small_ref, (a_ref, b_ref, c_ref))
+    small_out_ref[...] = small
+    row, source = iota((48, 192), 0), iota((48, 192), 1)
+    for step in range(4):
+        yl = place_ref[5] ^ (step % 2)
+        wanted = (step // 2) * 96 + (row // 12) * 24 + yl * 12 + row % 12
+        high, low = rows_of(source == wanted, total)
+        if step == 0:
+            own_out_ref[...] = high + low
+        else:
+            sends[step - 1][16:64, :] = high.astype(BF16)
+            put_small(sends[step - 1], small)
+
+
+def y_kernel(place_ref, own_ref, small_ref, a_ref, b_ref, c_ref, own_out_ref, small_out_ref, *sends):
+    total, small = gather_sums(own_ref, small_ref, (a_ref, b_ref, c_ref))
+    small_out_ref[...] = small
+    row, source = iota((16, 48), 0), iota((16, 48), 1)
+    for step in range(4):
+        wanted = (place_ref[4] ^ step) * 12 + row
+        high, low = rows_of((source == wanted) & (row < 12), total)
+        if step == 0:
+            own_out_ref[...] = high + low
+        else:
+            sends[step - 1][16:32, :] = high.astype(BF16)
+            put_small(sends[step - 1], small)
+
+
+def x_kernel(own_ref, small_ref, a_ref, b_ref, c_ref, share_ref, small_out_ref):
+    total, small = gather_sums(own_ref, small_ref, (a_ref, b_ref, c_ref))
+    share_ref[...] = total[0:12]
+    small_out_ref[...] = small
 
 
 def on_device(tokens, gain, weight, bias, target, channel_weight):
     where = {axis: lax.axis_index(axis) for axis in SIZE}
     member = where["x"] * 2 + where["yl"]
     space = (where["yh"] * 4 + where["z"]) * 2 + where["core"]
-    place = jnp.stack([where["yh"], where["z"], where["core"], member]).astype(jnp.int32)
+    place = jnp.stack(
+        [where["yh"], where["z"], where["core"], member, where["x"], where["yl"]]
+    ).astype(jnp.int32)
     smem = pl.BlockSpec(memory_space=pltpu.SMEM)
     features = tokens.shape[-1]
     outs = weight.shape[1]
@@ -291,30 +372,6 @@
     sources = [
         lax.dynamic_index_in_dim(pieces, member ^ k, 1, keepdims=False) for k in range(8)
     ]
-    arrived = {0: sources[0], 1: swap_member(sources[1], 1), 4: swap_member(sources[4], 4)}
-    near = jnp.stack([weight] + [swap(weight, "x", k) for k in (1, 2, 3)])
-    (p3, p6), (near,) = after((sources[3], sources[6]), near)
-    arrived[3], arrived[6] = swap_member(p3, 3), swap_member(p6, 6)
-    rows_y = [near] + [swap_y(near, k) for k in (1, 2, 3)]
-    pair = jnp.stack(
-        [
-            member_rows(jnp.stack(rows_y[0:2]), where),
-            member_rows(jnp.stack(rows_y[2:4]), where),
-        ]
-    )
-    (pair, p7, p2, p5), (arrived[1], arrived[4]) = after(
-        (pair, sources[7], sources[2], sources[5]), arrived[1], arrived[4]
-    )
-    for k, piece in ((7, p7), (2, p2), (5, p5)):
-        arrived[k] = swap_member(piece, k)
-    quad = jnp.stack([pair] + [swap(pair, "z", k) for k in (1, 2, 3)])
-    late = (3, 6, 7, 2, 5)
-    (quad,), done = after((quad,), *[arrived[k] for k in late])
-    for k, piece in zip(late, done):
-        arrived[k] = piece
-    other = swap(quad, "core", 1)
-    normed = [norm_piece(arrived[k], gain_row) for k in range(8)]
-
     t_here, l_here = member // 4, member % 4
     image = lax.dynamic_slice(
         target, (0, 4 * t_here, 256 * l_here), (target.shape[0], 4, 256)
@@ -335,15 +392,41 @@
     ).reshape(1, outs)
     wt = jnp.pad(wt, ((0, 0), (0, padded - outs)))
 
-    full, dfield, bias_part = pl.pallas_call(
+    arrived = {0: sources[0], 4: swap_member(sources[4], 4)}
+    near = jnp.stack([weight] + [swap_y(weight, k) for k in (1, 2, 3)])
+    (p1, p2), (near,) = after((sources[1], sources[2]), near)
+    wide = jnp.stack([near] + [swap(near, "x", k) for k in (1, 2, 3)])
+    arrived[1], arrived[2] = swap_member(p1, 1), swap_member(p2, 2)
+    pair = jnp.stack([member_rows(wide[:, 2 * k : 2 * k + 2], where) for k in range(2)])
+    (pair, p3, p6), done = after(
+        (pair, sources[3], sources[6]), arrived[4], arrived[1], arrived[2], truth, wt
+    )
+    arrived[4], arrived[1], arrived[2], truth, wt = done
+    quad = jnp.stack([pair] + [swap(pair, "z", k) for k in (1, 2, 3)])
+    arrived[3], arrived[6] = swap_member(p3, 3), swap_member(p6, 6)
+    (p7, p5), (arrived[3], arrived[6]) = after(
+        (sources[7], sources[5]), arrived[3], arrived[6]
+    )
+    arrived[7], arrived[5] = swap_member(p7, 7), swap_member(p5, 5)
+    normed = {k: norm_piece(arrived[k], gain_row) for k in (0, 4, 1, 2, 3, 6)}
+    early = [n for k in (0, 4, 1, 2, 3, 6) for n in normed[k]]
+    (quad,), done = after((quad,), arrived[7], *early)
+    arrived[7] = done[0]
+    for n, k in enumerate((0, 4, 1, 2, 3, 6)):
+        normed[k] = done[1 + 2 * n : 3 + 2 * n]
+    other = swap(quad, "core", 1)
+    for k in (7, 5):
+        normed[k] = norm_piece(arrived[k], gain_row)
+
+    full, bias_part, *dfield = pl.pallas_call(
         pairs_kernel,
         out_shape=(
             jax.ShapeDtypeStruct((features, outs), BF16),
-            jax.ShapeDtypeStruct((8, 2, 64, outs), BF16),
             jax.ShapeDtypeStruct((1, padded), F32),
-        ),
+        )
+        + (jax.ShapeDtypeStruct((128, outs), BF16),) * 8,
         in_specs=[smem] + vmem(13),
-        out_specs=tuple(vmem(3)),
+        out_specs=tuple(vmem(10)),
         scratch_shapes=[
             pltpu.VMEM((1024, features), BF16),
             pltpu.VMEM((16, 64, padded), F32),
@@ -352,9 +435,11 @@
         compiler_params=params(32),
         cost_estimate=cost(20000000000, 80000000),
         name="pairs",
-    )(place, quad, other, bias.reshape(1, outs), truth, wt, *[n[0] for n in normed])
-
-    returned = {0: dfield[0], 1: swap_member(dfield[1], 1), 3: swap_member(dfield[3], 3)}
+    )(place, quad, other, bias.reshape(1, outs), truth, wt, *[normed[k][0] for k in range(8)])
+
+    returned = {0: dfield[0]}
+    for k in (1, 4, 5):
+        returned[k] = swap_member(dfield[k], k)
     keep, send, small = pl.pallas_call(
         grad_kernel,
         out_shape=(
@@ -362,79 +447,80 @@
             jax.ShapeDtypeStruct((16 + 768, outs), BF16),
             jax.ShapeDtypeStruct((8, 512), F32),
         ),
-        in_specs=[smem] + vmem(12),
+        in_specs=[smem] + vmem(19),
         out_specs=tuple(vmem(3)),
         scratch_shapes=[
             pltpu.VMEM((features, 1024), BF16),
+            pltpu.VMEM((1024, outs), BF16),
             pltpu.VMEM((features, outs), F32),
             pltpu.VMEM((8, features), F32),
         ],
-        compiler_params=params(32),
+        compiler_params=params(34),
         cost_estimate=cost(12000000000, 45000000),
         name="weight_gradient",
     )(
-        place, dfield.reshape(1024, outs), full, bias_part, gain_row,
-        *[n[1] for n in normed],
-    )
-
-    def pick(value, index):
-        return lax.dynamic_index_in_dim(value, index, 0, keepdims=False)
-
-    def spread(mine, blocks, small, moves):
-        came = [
-            move(jnp.concatenate([pack(small, outs), block.astype(BF16)], axis=0))
-            for move, block in zip(moves, blocks)
-        ]
-        return (
-            sum([c[16:].astype(F32) for c in came], mine),
-            sum([unpack(c) for c in came], small),
-        )
-
-    rest = (6, 4, 5, 7, 2)
-    (send, *held), (returned[1], returned[3]) = after(
-        (send, *[dfield[k] for k in rest]), returned[1], returned[3]
-    )
-    for k, piece in zip(rest, held):
-        returned[k] = swap_member(piece, k)
+        place, full, bias_part, gain_row,
+        *[normed[k][1] for k in range(8)], *dfield,
+    )
+
+    def backward(order, before):
+        count = len(order)
+        return pl.pallas_call(
+            functools.partial(backward_kernel, order, len(before)),
+            out_shape=jax.ShapeDtypeStruct(
+                (2, 8, 64, features) if before else (count, 2, 64, features), BF16
+            ),
+            in_specs=[smem] + vmem(3 + count + len(before)),
+            out_specs=vmem(1)[0],
+            scratch_shapes=[
+                pltpu.VMEM((128 * count, outs), BF16),
+                pltpu.VMEM((128 * count, features), F32),
+            ],
+            compiler_params=params(32),
+            cost_estimate=cost(8000000000, 30000000),
+            name="backward",
+        )(place, pieces, gain_row, full, *before, *[returned[k] for k in order])
+
+    def combine(kernel, name, own_rows, send_rows, sends, *operands):
+        return pl.pallas_call(
+            kernel,
+            out_shape=(
+                jax.ShapeDtypeStruct((own_rows, outs), F32),
+                jax.ShapeDtypeStruct((8, 512), F32),
+            )
+            + (jax.ShapeDtypeStruct((send_rows, outs), BF16),) * sends,
+            in_specs=([smem] if operands[0] is place else [])
+            + vmem(len(operands) - (operands[0] is place)),
+            out_specs=tuple(vmem(2 + sends)),
+            compiler_params=params(16),
+            cost_estimate=cost(1000000000, 4000000),
+            name=name,
+        )(*operands)
+
+    (send,), done = after((send,), returned[1], returned[4], returned[5])
+    returned[1], returned[4], returned[5] = done
     came = swap(send, "core", 1)
-    total = keep + came[16:].reshape(keep.shape).astype(F32)
-    small = small + unpack(came)
-    total, small = spread(
-        total[:, 0].reshape(-1, outs),
-        [total[:, k].reshape(-1, outs) for k in (1, 2, 3)],
-        small,
-        [functools.partial(swap, axis="z", step=k) for k in (1, 2, 3)],
-    )
-    result = pl.pallas_call(
-        backward_kernel,
-        out_shape=jax.ShapeDtypeStruct((2, 8, 64, features), BF16),
-        in_specs=[smem] + vmem(11),
-        out_specs=vmem(1)[0],
-        scratch_shapes=[pltpu.VMEM((1024, outs), BF16), pltpu.VMEM((1024, features), F32)],
-        compiler_params=params(32),
-        cost_estimate=cost(16000000000, 60000000),
-        name="backward",
-    )(place, pieces, gain_row, full, *[returned[k] for k in range(8)])
-    (total, small), (result,) = after((total, small), result)
-    total = total.reshape(2, 4, 2, 12, outs)
-
-    def slab(step):
-        block = pick(total[step // 2].transpose(1, 0, 2, 3), where["yl"] ^ (step % 2))
-        return block.reshape(48, outs)
-
-    total, small = spread(
-        slab(0),
-        [slab(k) for k in (1, 2, 3)],
-        small,
-        [functools.partial(swap_y, step=k) for k in (1, 2, 3)],
-    )
-    total = total.reshape(4, 12, outs)
-    share, small = spread(
-        pick(total, where["x"]),
-        [pick(total, where["x"] ^ k) for k in (1, 2, 3)],
-        small,
-        [functools.partial(swap, axis="x", step=k) for k in (1, 2, 3)],
-    )
+    own, small, *sends = combine(core_kernel, "core_sums", 192, 208, 3, keep, small, came)
+    sends[0], sends[1], sends[2], d3, d6 = after(
+        (*sends, dfield[3], dfield[6])
+    )[0]
+    came = [swap(value, "z", k) for k, value in zip((1, 2, 3), sends)]
+    returned[3], returned[6] = swap_member(d3, 3), swap_member(d6, 6)
+    half = backward(FIRST, ())
+    (d7, d2), (half, returned[3], returned[6]) = after(
+        (dfield[7], dfield[2]), half, returned[3], returned[6]
+    )
+    returned[7], returned[2] = swap_member(d7, 7), swap_member(d2, 2)
+    came, (half, returned[7], returned[2]) = after(
+        came, half, returned[7], returned[2]
+    )
+    own, small, *sends = combine(z_kernel, "z_sums", 48, 64, 3, place, own, small, *came)
+    came = [swap_y(value, k) for k, value in zip((1, 2, 3), sends)]
+    result = backward(SECOND, (half,))
+    came, (result,) = after(came, result)
+    own, small, *sends = combine(y_kernel, "y_sums", 16, 32, 3, place, own, small, *came)
+    came = [swap(value, "x", k) for k, value in zip((1, 2, 3), sends)]
+    share, small = combine(x_kernel, "x_sums", 12, 0, 0, own, small, *came)
     return (
         result.reshape(tokens.shape),
         small[0:3].reshape(-1),

time: 199 us -> 180 us (0.905)
  waiting for transfers between devices: 79.9 us -> 59.5 us
  starting transfers between devices: 45.1 us -> 51.4 us
  other arithmetic: 6.12 us -> 0.64 us
  Pallas kernels: 46.7 us -> 51.8 us
  local copies, waits for them, and re-layouts: 19.3 us -> 15.2 us
    ppermute x6, waiting for transfers between devices: 15.9 us -> 0.02 us  [swap_y(): return lax.ppermute(value, ('yh', 'yl'), [(i, i ^ step) for i in range(4)])]
    pallas_call x1 -> x6, Pallas kernels: 13.3 us -> 18.2 us  [the longest x2 15 us: backward(): pl.pallas_call(functools.partial(backward_kernel, order, len(before)), ou...]
    ppermute x14, starting transfers between devices: 15.2 us -> 18.6 us  [swap(): return lax.ppermute(value, axis, [(i, i ^ step) for i in range(SIZE[axis])])]
    ppermute x14, starting transfers between devices: 20.2 us -> 23.4 us  [swap_member(): return lax.ppermute(value, MEMBER, [(i, i ^ step) for i in range(8)])]
    ppermute x14, waiting for transfers between devices: 28.7 us -> 26 us  [swap(): return lax.ppermute(value, axis, [(i, i ^ step) for i in range(SIZE[axis])])]
    unnamed x58 -> x66, local copies, waits for them, and re-layouts: 6.75 us -> 9.03 us
  transfers between devices with their start and end apart: 34 -> 34, of which waited for: 18 -> 13; matrix products, arithmetic and copies ran while one was open for 8% -> 3% of each run, Pallas kernels for 14% -> 16%
where the time goes in v3:
time: 180 us
  waiting for transfers between devices  59.5 us (33%)
  Pallas kernels  51.8 us (29%)
  starting transfers between devices  51.4 us (29%)
  local copies, waits for them, and re-layouts  15.2 us (8%)
    ppermute x14, waiting for transfers between devices, swap_member(): return lax.ppermute(value, MEMBER, [(i, i ^ step) for i in range(8)])  33.5 us
    ppermute x14, waiting for transfers between devices, swap(): return lax.ppermute(value, axis, [(i, i ^ step) for i in range(SIZE[axis])])  26 us
    ppermute x14, starting transfers between devices, swap_member(): return lax.ppermute(value, MEMBER, [(i, i ^ step) for i in range(8)])  23.4 us
    pallas_call x1, Pallas kernels, on_device(): pl.pallas_call(pairs_kernel, out_shape=(jax.ShapeDtypeStruct((features, o...  18.9 us
    ppermute x14, starting transfers between devices, swap(): return lax.ppermute(value, axis, [(i, i ^ step) for i in range(SIZE[axis])])  18.6 us
    pallas_call x2, Pallas kernels, backward(): pl.pallas_call(functools.partial(backward_kernel, order, len(before)), ou...  15 us
    ppermute x6, starting transfers between devices, swap_y(): return lax.ppermute(value, ('yh', 'yl'), [(i, i ^ step) for i in range(4)])  9.41 us
    unnamed x66, local copies, waits for them, and re-layouts  9.03 us
  transfers between devices with their start and end apart: 34, of which 13 were waited for; matrix products, arithmetic and copies ran while one was open for 3% of the time, Pallas kernels for 16%

profile of v3, /device:TPU:0, one launch (start us, length us, event | category | flops | bytes accessed | tf_op | source)
XLA Modules:
  0.0 180.1 jit_solution(3572272785738350494)
XLA Ops:
  0.6 1.7 collective-permute-start
  2.4 2.2 %collective-permute-start.2 = (bf16[12,1120]{1,0:T(8,128)(2,1)}, bf16[12,1120]{1,0:T(8,128)(2,1)S(1)}, u32[]{:S(2)}, u32[]{:S(2)}) collective-permute-start(bf16[12,1120]{1,0:T(8,128)(2,1)} %param.9), channel_id=1, source_target_pairs={{0,65},{1,64},{64,1},{65,0},{2,67},{3,66},{66,3},{67,2},{4,69},{5,... | collective-permute-start | bytes 80648 | tf_op jit(solution)/shard_map/ppermute | solution.py:47
  5.3 3.4 %constant_dynamic-slice_fusion = (bf16[2,1,64,1536]{3,2,1,0:T(8,128)(2,1)S(1)}, bf16[2,64,1536]{2,1,0:T(8,128)(2,1)}, bf16[2,64,1536]{2,1,0:T(8,128)(2,1)}, bf16...) fusion(bf16[2,8,64,1536]{3,2,1,0:T(8,128)(2,1)} %bitcast.51, ...), kind=kLoop, calls=%fused_computation.19 | loop fusion | bytes 6291488 | tf_op jit(solution)/shard_map/jit(dynamic_index_in_dim)/dynamic_slice | solution.py:373
  8.7 3.0 %collective-permute-start.6 = (bf16[2,64,1536]{2,1,0:T(8,128)(2,1)}, bf16[2,64,1536]{2,1,0:T(8,128)(2,1)S(1)}, u32[]{:S(2)}, u32[]{:S(2)}) collective-permute-start(bf16[2,64,1536]{2,1,0:T(8,128)(2,1)} %get-tuple-element.205), channel_id=1, source_target_pairs={{0,4},{1,5},{2,6},{3,7},{4,0},{5,1},{6,2},{7,3},{8,12},{9,13},{10,... | collective-permute-start | bytes 1179656 | tf_op jit(solution)/shard_map/ppermute | solution.py:51
  17.6 1.5 collective-permute-start.4
  21.9 5.1 %collective-permute-done.5 = bf16[4,12,1120]{2,1,0:T(8,128)(2,1)S(1)} collective-permute-done((bf16[4,12,1120]{2,1,0:T(8,128)(2,1)S(1)}, bf16[4,12,1120]{2,1,0:T(8,128)(2,1)S(1)}, u32[]{:S(2)}, u32[]{:S(2)}) %collective-permute-start.5) | collective-permute-done | bytes 107552 | tf_op jit(solution)/shard_map/ppermute | solution.py:43
  27.0 1.5 collective-permute-start.8
  30.1 8.2 %collective-permute-done.8 = bf16[2,64,1536]{2,1,0:T(8,128)(2,1)S(1)} collective-permute-done((bf16[2,64,1536]{2,1,0:T(8,128)(2,1)}, bf16[2,64,1536]{2,1,0:T(8,128)(2,1)S(1)}, u32[]{:S(2)}, u32[]{:S(2)}) %collective-permute-start.8) | collective-permute-done | bytes 393248 | tf_op jit(solution)/shard_map/ppermute | solution.py:51
  38.3 4.0 %collective-permute-start.11 = (bf16[2,96,1120]{2,1,0:T(8,128)(2,1)S(1)}, bf16[2,96,1120]{2,1,0:T(8,128)(2,1)S(1)}, u32[]{:S(2)}, u32[]{:S(2)}) collective-permute-start(bf16[2,96,1120]{2,1,0:T(8,128)(2,1)S(1)} %pad_maximum_fusion.2), channel_id=1, source_target_pairs={{0,48},{16,32},{32,16},{48,0},{1,49},{17,33},{33,17},{49,1},{2,50}... | collective-permute-start | bytes 1290248 | tf_op jit(solution)/shard_map/ppermute | solution.py:43
  43.2 1.8 %collective-permute-start.12 = (bf16[2,64,1536]{2,1,0:T(8,128)(2,1)}, bf16[2,64,1536]{2,1,0:T(8,128)(2,1)S(1)}, u32[]{:S(2)}, u32[]{:S(2)}) collective-permute-start(bf16[2,64,1536]{2,1,0:T(8,128)(2,1)} %get-tuple-element.107), channel_id=1, source_target_pairs={{0,3},{1,2},{2,1},{3,0},{4,7},{5,6},{6,5},{7,4},{8,11},{9,10},{10,... | collective-permute-start | bytes 1179656 | tf_op jit(solution)/shard_map/ppermute | solution.py:51
  45.0 2.1 %collective-permute-start.13 = (bf16[2,64,1536]{2,1,0:T(8,128)(2,1)}, bf16[2,64,1536]{2,1,0:T(8,128)(2,1)S(1)}, u32[]{:S(2)}, u32[]{:S(2)}) collective-permute-start(bf16[2,64,1536]{2,1,0:T(8,128)(2,1)} %get-tuple-element.108), channel_id=1, source_target_pairs={{0,6},{1,7},{2,4},{3,5},{4,2},{5,3},{6,0},{7,1},{8,14},{9,15},{10,... | collective-permute-start | bytes 1179656 | tf_op jit(solution)/shard_map/ppermute | solution.py:51
  51.7 2.2 %collective-permute-done.12 = bf16[2,64,1536]{2,1,0:T(8,128)(2,1)S(1)} collective-permute-done((bf16[2,64,1536]{2,1,0:T(8,128)(2,1)}, bf16[2,64,1536]{2,1,0:T(8,128)(2,1)S(1)}, u32[]{:S(2)}, u32[]{:S(2)}) %collective-permute-start.12) | collective-permute-done | bytes 393248 | tf_op jit(solution)/shard_map/ppermute | solution.py:51
  53.9 1.9 %collective-permute-done.13 = bf16[2,64,1536]{2,1,0:T(8,128)(2,1)S(1)} collective-permute-done((bf16[2,64,1536]{2,1,0:T(8,128)(2,1)}, bf16[2,64,1536]{2,1,0:T(8,128)(2,1)S(1)}, u32[]{:S(2)}, u32[]{:S(2)}) %collective-permute-start.13) | collective-permute-done | bytes 393248 | tf_op jit(solution)/shard_map/ppermute | solution.py:51
  55.8 2.6 %collective-permute-start.14 = (bf16[2,64,1536]{2,1,0:T(8,128)(2,1)S(1)}, bf16[2,64,1536]{2,1,0:T(8,128)(2,1)S(1)}, u32[]{:S(2)}, u32[]{:S(2)}) collective-permute-start(bf16[2,64,1536]{2,1,0:T(8,128)(2,1)S(1)} %copy-done.28), channel_id=1, source_target_pairs={{0,7},{1,6},{2,5},{3,4},{4,3},{5,2},{6,1},{7,0},{8,15},{9,14},{10,... | collective-permute-start | bytes 1179656 | tf_op jit(solution)/shard_map/ppermute | solution.py:51
  62.7 3.6 %collective-permute-done.14 = bf16[2,64,1536]{2,1,0:T(8,128)(2,1)S(1)} collective-permute-done((bf16[2,64,1536]{2,1,0:T(8,128)(2,1)S(1)}, bf16[2,64,1536]{2,1,0:T(8,128)(2,1)S(1)}, u32[]{:S(2)}, u32[]{:S(2)}) %collective-permute-start.14) | collective-permute-done | bytes 393248 | tf_op jit(solution)/shard_map/ppermute | solution.py:51
  67.3 13.3 %collective-permute-done.16 = bf16[2,64,1536]{2,1,0:T(8,128)(2,1)} collective-permute-done((bf16[2,64,1536]{2,1,0:T(8,128)(2,1)}, bf16[2,64,1536]{2,1,0:T(8,128)(2,1)}, u32[]{:S(2)}, u32[]{:S(2)}) %collective-permute-start.16) | collective-permute-done | bytes 393248 | tf_op jit(solution)/shard_map/ppermute | solution.py:51
  83.7 18.9 %pairs.1 = (bf16[1536,1120]{1,0:T(8,128)(2,1)S(1)}, f32[1,1152]{1,0:T(1,128)S(1)}, bf16[128,1120]{1,0:T(8,128)(2,1)S(1)}, bf16[128,1120]{1,0:T(8,128)(2,1)S(1)},...) custom-call(s32[6]{0:T(128)S(1)} %stack.81.place_ref, ...), custom_call_target="tpu_custom_call" | custom-call | flops 20000000000 | bytes 80000000 | tf_op jit(solution)/shard_map/pairs/pallas_call | solution.py:421
  104.1 3.6 %collective-permute-start.19 = (bf16[128,1120]{1,0:T(8,128)(2,1)S(1)}, bf16[128,1120]{1,0:T(8,128)(2,1)S(1)}, u32[]{:S(2)}, u32[]{:S(2)}) collective-permute-start(bf16[128,1120]{1,0:T(8,128)(2,1)S(1)} %get-tuple-element.155.refs_13_), channel_id=1, source_target_pairs={{0,5},{1,4},{2,7},{3,6},{4,1},{5,0},{6,3},{7,2},{8,13},{9,12},{10,... | collective-permute-start | bytes 860168 | tf_op jit(solution)/shard_map/ppermute | solution.py:51
  107.7 8.9 %weight_gradient.1 = (f32[2,4,96,1120]{3,2,1,0:T(8,128)S(1)}, bf16[784,1120]{1,0:T(8,128)(2,1)S(1)}, f32[8,512]{1,0:T(8,128)S(1)}) custom-call(s32[6]{0:T(128)S(1)} %stack.81.place_ref, bf16[1536,1120]{1,0:T(8,128)(2,1)S(1)} %get-tuple-element.140.full_ref, f32[1,1152]{1,0:T(1,128)S(1)} %get-tuple-element.141.bias_part_ref, ...), custom_call_target="tpu_custom_call" | custom-call | flops 12000000000 | bytes 45000000 | tf_op jit(solution)/shard_map/weight_gradient/pallas_call | solution.py:443
  116.7 3.7 %collective-permute-done.19.refs_3_ = bf16[128,1120]{1,0:T(8,128)(2,1)S(1)} collective-permute-done((bf16[128,1120]{1,0:T(8,128)(2,1)S(1)}, bf16[128,1120]{1,0:T(8,128)(2,1)S(1)}, u32[]{:S(2)}, u32[]{:S(2)}) %collective-permute-start.19) | collective-permute-done | bytes 286752 | tf_op jit(solution)/shard_map/ppermute | solution.py:51
  120.4 3.7 %collective-permute-done.20.came_ref = bf16[784,1120]{1,0:T(8,128)(2,1)S(1)} collective-permute-done((bf16[784,1120]{1,0:T(8,128)(2,1)S(1)}, bf16[784,1120]{1,0:T(8,128)(2,1)S(1)}, u32[]{:S(2)}, u32[]{:S(2)}) %collective-permute-start.20) | collective-permute-done | bytes 1756192 | tf_op jit(solution)/shard_map/ppermute | solution.py:43
  124.8 1.9 %collective-permute-start.25 = (bf16[128,1120]{1,0:T(8,128)(2,1)S(1)}, bf16[128,1120]{1,0:T(8,128)(2,1)S(1)}, u32[]{:S(2)}, u32[]{:S(2)}) collective-permute-start(bf16[128,1120]{1,0:T(8,128)(2,1)S(1)} %get-tuple-element.174.refs_14_), channel_id=1, source_target_pairs={{0,6},{1,7},{2,4},{3,5},{4,2},{5,3},{6,0},{7,1},{8,14},{9,15},{10,... | collective-permute-start | bytes 860168 | tf_op jit(solution)/shard_map/ppermute | solution.py:51
  127.9 3.0 %collective-permute-start.22 = (bf16[208,1120]{1,0:T(8,128)(2,1)S(1)}, bf16[208,1120]{1,0:T(8,128)(2,1)S(1)}, u32[]{:S(2)}, u32[]{:S(2)}) collective-permute-start(bf16[208,1120]{1,0:T(8,128)(2,1)S(1)} %get-tuple-element.168), channel_id=1, source_target_pairs={{0,32},{16,48},{32,0},{48,16},{1,33},{17,49},{33,1},{49,17},{2,34}... | collective-permute-start | bytes 1397768 | tf_op jit(solution)/shard_map/ppermute | solution.py:43
  131.5 6.6 %backward.2.refs_0_ = bf16[4,2,64,1536]{3,2,1,0:T(8,128)(2,1)S(1)} custom-call(s32[6]{0:T(128)S(1)} %stack.81.place_ref, bf16[2,8,64,1536]{3,2,1,0:T(8,128)(2,1)S(1)} %bitcast.52, f32[1,1536]{1,0:T(1,128)S(1)} %reshape.154.gain_ref, bf16[1536,1120]{1,0:T(8,128)(2,1)S(1)} %get-tuple-element.140.full_ref, ...), custom_call_target="tpu_custom_call" | custom-call | flops 8000000000 | bytes 30000000 | tf_op jit(solution)/shard_map/backward/pallas_call | solution.py:468
  138.1 1.8 collective-permute-start.26
  141.0 11.0 %collective-permute-done.22.b_ref = bf16[208,1120]{1,0:T(8,128)(2,1)S(1)} collective-permute-done((bf16[208,1120]{1,0:T(8,128)(2,1)S(1)}, bf16[208,1120]{1,0:T(8,128)(2,1)S(1)}, u32[]{:S(2)}, u32[]{:S(2)}) %collective-permute-start.22) | collective-permute-done | bytes 465952 | tf_op jit(solution)/shard_map/ppermute | solution.py:43
  152.0 2.6 %collective-permute-done.23.c_ref = bf16[208,1120]{1,0:T(8,128)(2,1)S(1)} collective-permute-done((bf16[208,1120]{1,0:T(8,128)(2,1)S(1)}, bf16[208,1120]{1,0:T(8,128)(2,1)S(1)}, u32[]{:S(2)}, u32[]{:S(2)}) %collective-permute-start.23) | collective-permute-done | bytes 465952 | tf_op jit(solution)/shard_map/ppermute | solution.py:43
  157.1 2.5 %collective-permute-start.29 = (bf16[64,1120]{1,0:T(8,128)(2,1)S(1)}, bf16[64,1120]{1,0:T(8,128)(2,1)S(1)}, u32[]{:S(2)}, u32[]{:S(2)}) collective-permute-start(bf16[64,1120]{1,0:T(8,128)(2,1)S(1)} %get-tuple-element.182), channel_id=1, source_target_pairs={{0,64},{1,65},{64,0},{65,1},{2,66},{3,67},{66,2},{67,3},{4,68},{5,... | collective-permute-start | bytes 430088 | tf_op jit(solution)/shard_map/ppermute | solution.py:47
  160.7 8.4 %backward.3 = bf16[2,8,64,1536]{3,2,1,0:T(8,128)(2,1)} custom-call(s32[6]{0:T(128)S(1)} %stack.81.place_ref, bf16[2,8,64,1536]{3,2,1,0:T(8,128)(2,1)S(1)} %bitcast.53, f32[1,1536]{1,0:T(1,128)S(1)} %reshape.154.gain_ref, bf16[1536,1120]{1,0:T(8,128)(2,1)S(1)} %get-tuple-element.140.full_ref, bf16[4,2,64,1536]{3,2,1,0:T(8,128)(2,1)S(1)} %backward.2.refs_0_, ...), custom_call_target="tpu_custom_call" | custom-call | flops 8000000000 | bytes 30000000 | tf_op jit(solution)/shard_map/backward/pallas_call | solution.py:468
  169.9 1.7 collective-permute-start.31
  172.6 2.1 %collective-permute-start.33 = (bf16[32,1120]{1,0:T(8,128)(2,1)S(1)}, bf16[32,1120]{1,0:T(8,128)(2,1)S(1)}, u32[]{:S(2)}, u32[]{:S(2)}) collective-permute-start(bf16[32,1120]{1,0:T(8,128)(2,1)S(1)} %get-tuple-element.199), channel_id=1, source_target_pairs={{0,6},{2,4},{4,2},{6,0},{1,7},{3,5},{5,3},{7,1},{8,14},{10,12},{12... | collective-permute-start | bytes 215048 | tf_op jit(solution)/shard_map/ppermute | solution.py:43
  174.7 2.8 %collective-permute-done.32.b_ref = bf16[32,1120]{1,0:T(8,128)(2,1)S(1)} collective-permute-done((bf16[32,1120]{1,0:T(8,128)(2,1)S(1)}, bf16[32,1120]{1,0:T(8,128)(2,1)S(1)}, u32[]{:S(2)}, u32[]{:S(2)}) %collective-permute-start.32) | collective-permute-done | bytes 71712 | tf_op jit(solution)/shard_map/ppermute | solution.py:43
  (143 shorter events, 37.6 us)
Async XLA Ops:
  0.6 15.7 %collective-permute-start = (bf16[12,1120]{1,0:T(8,128)(2,1)}, bf16[12,1120]{1,0:T(8,128)(2,1)S(1)}, u32[]{:S(2)}, u32[]{:S(2)}) collective-permute-start(bf16[12,1120]{1,0:T(8,128)(2,1)} %param.9), channel_id=1, source_target_pairs={{0,1},{1,0},{64,65},{65,64},{2,3},{3,2},{66,67},{67,66},{4,5},{5,4... | collective-permute-start | bytes 80648 | tf_op jit(solution)/shard_map/ppermute | solution.py:47
  2.4 14.0 %collective-permute-start.2 = (bf16[12,1120]{1,0:T(8,128)(2,1)}, bf16[12,1120]{1,0:T(8,128)(2,1)S(1)}, u32[]{:S(2)}, u32[]{:S(2)}) collective-permute-start(bf16[12,1120]{1,0:T(8,128)(2,1)} %param.9), channel_id=1, source_target_pairs={{0,65},{1,64},{64,1},{65,0},{2,67},{3,66},{66,3},{67,2},{4,69},{5,... | collective-permute-start | bytes 80648 | tf_op jit(solution)/shard_map/ppermute | solution.py:47
  4.6 11.8 %collective-permute-start.1 = (bf16[12,1120]{1,0:T(8,128)(2,1)}, bf16[12,1120]{1,0:T(8,128)(2,1)S(1)}, u32[]{:S(2)}, u32[]{:S(2)}) collective-permute-start(bf16[12,1120]{1,0:T(8,128)(2,1)} %param.9), channel_id=1, source_target_pairs={{0,64},{1,65},{64,0},{65,1},{2,66},{3,67},{66,2},{67,3},{4,68},{5,... | collective-permute-start | bytes 80648 | tf_op jit(solution)/shard_map/ppermute | solution.py:47
  8.7 20.8 %collective-permute-start.6 = (bf16[2,64,1536]{2,1,0:T(8,128)(2,1)}, bf16[2,64,1536]{2,1,0:T(8,128)(2,1)S(1)}, u32[]{:S(2)}, u32[]{:S(2)}) collective-permute-start(bf16[2,64,1536]{2,1,0:T(8,128)(2,1)} %get-tuple-element.205), channel_id=1, source_target_pairs={{0,4},{1,5},{2,6},{3,7},{4,0},{5,1},{6,2},{7,3},{8,12},{9,13},{10,... | collective-permute-start | bytes 1179656 | tf_op jit(solution)/shard_map/ppermute | solution.py:51
  16.4 10.6 %collective-permute-start.5 = (bf16[4,12,1120]{2,1,0:T(8,128)(2,1)S(1)}, bf16[4,12,1120]{2,1,0:T(8,128)(2,1)S(1)}, u32[]{:S(2)}, u32[]{:S(2)}) collective-permute-start(bf16[4,12,1120]{2,1,0:T(8,128)(2,1)S(1)} %pad_maximum_fusion.3), channel_id=1, source_target_pairs={{0,6},{2,4},{4,2},{6,0},{1,7},{3,5},{5,3},{7,1},{8,14},{10,12},{12... | collective-permute-start | bytes 322568 | tf_op jit(solution)/shard_map/ppermute | solution.py:43
  17.6 10.9 %collective-permute-start.4 = (bf16[4,12,1120]{2,1,0:T(8,128)(2,1)S(1)}, bf16[4,12,1120]{2,1,0:T(8,128)(2,1)S(1)}, u32[]{:S(2)}, u32[]{:S(2)}) collective-permute-start(bf16[4,12,1120]{2,1,0:T(8,128)(2,1)S(1)} %pad_maximum_fusion.3), channel_id=1, source_target_pairs={{0,4},{2,6},{4,0},{6,2},{1,5},{3,7},{5,1},{7,3},{8,12},{10,14},{12... | collective-permute-start | bytes 322568 | tf_op jit(solution)/shard_map/ppermute | solution.py:43
  19.2 9.3 %collective-permute-start.3 = (bf16[4,12,1120]{2,1,0:T(8,128)(2,1)S(1)}, bf16[4,12,1120]{2,1,0:T(8,128)(2,1)S(1)}, u32[]{:S(2)}, u32[]{:S(2)}) collective-permute-start(bf16[4,12,1120]{2,1,0:T(8,128)(2,1)S(1)} %pad_maximum_fusion.3), channel_id=1, source_target_pairs={{0,2},{2,0},{4,6},{6,4},{1,3},{3,1},{5,7},{7,5},{8,10},{10,8},{12,... | collective-permute-start | bytes 322568 | tf_op jit(solution)/shard_map/ppermute | solution.py:43
  20.6 9.5 %collective-permute-start.7 = (bf16[2,64,1536]{2,1,0:T(8,128)(2,1)}, bf16[2,64,1536]{2,1,0:T(8,128)(2,1)S(1)}, u32[]{:S(2)}, u32[]{:S(2)}) collective-permute-start(bf16[2,64,1536]{2,1,0:T(8,128)(2,1)} %get-tuple-element.104), channel_id=1, source_target_pairs={{0,1},{1,0},{2,3},{3,2},{4,5},{5,4},{6,7},{7,6},{8,9},{9,8},{10,11... | collective-permute-start | bytes 1179656 | tf_op jit(solution)/shard_map/ppermute | solution.py:51
  27.0 11.2 %collective-permute-start.8 = (bf16[2,64,1536]{2,1,0:T(8,128)(2,1)}, bf16[2,64,1536]{2,1,0:T(8,128)(2,1)S(1)}, u32[]{:S(2)}, u32[]{:S(2)}) collective-permute-start(bf16[2,64,1536]{2,1,0:T(8,128)(2,1)} %get-tuple-element.105), channel_id=1, source_target_pairs={{0,2},{1,3},{2,0},{3,1},{4,6},{5,7},{6,4},{7,5},{8,10},{9,11},{10,... | collective-permute-start | bytes 1179656 | tf_op jit(solution)/shard_map/ppermute | solution.py:51
  38.3 24.1 %collective-permute-start.11 = (bf16[2,96,1120]{2,1,0:T(8,128)(2,1)S(1)}, bf16[2,96,1120]{2,1,0:T(8,128)(2,1)S(1)}, u32[]{:S(2)}, u32[]{:S(2)}) collective-permute-start(bf16[2,96,1120]{2,1,0:T(8,128)(2,1)S(1)} %pad_maximum_fusion.2), channel_id=1, source_target_pairs={{0,48},{16,32},{32,16},{48,0},{1,49},{17,33},{33,17},{49,1},{2,50}... | collective-permute-start | bytes 1290248 | tf_op jit(solution)/shard_map/ppermute | solution.py:43
  42.3 20.1 %collective-permute-start.10 = (bf16[2,96,1120]{2,1,0:T(8,128)(2,1)S(1)}, bf16[2,96,1120]{2,1,0:T(8,128)(2,1)S(1)}, u32[]{:S(2)}, u32[]{:S(2)}) collective-permute-start(bf16[2,96,1120]{2,1,0:T(8,128)(2,1)S(1)} %pad_maximum_fusion.2), channel_id=1, source_target_pairs={{0,32},{16,48},{32,0},{48,16},{1,33},{17,49},{33,1},{49,17},{2,34}... | collective-permute-start | bytes 1290248 | tf_op jit(solution)/shard_map/ppermute | solution.py:43
  42.3 20.1 %collective-permute-start.9 = (bf16[2,96,1120]{2,1,0:T(8,128)(2,1)S(1)}, bf16[2,96,1120]{2,1,0:T(8,128)(2,1)S(1)}, u32[]{:S(2)}, u32[]{:S(2)}) collective-permute-start(bf16[2,96,1120]{2,1,0:T(8,128)(2,1)S(1)} %pad_maximum_fusion.2), channel_id=1, source_target_pairs={{0,16},{16,0},{32,48},{48,32},{1,17},{17,1},{33,49},{49,33},{2,18}... | collective-permute-start | bytes 1290248 | tf_op jit(solution)/shard_map/ppermute | solution.py:43
  43.2 10.7 %collective-permute-start.12 = (bf16[2,64,1536]{2,1,0:T(8,128)(2,1)}, bf16[2,64,1536]{2,1,0:T(8,128)(2,1)S(1)}, u32[]{:S(2)}, u32[]{:S(2)}) collective-permute-start(bf16[2,64,1536]{2,1,0:T(8,128)(2,1)} %get-tuple-element.107), channel_id=1, source_target_pairs={{0,3},{1,2},{2,1},{3,0},{4,7},{5,6},{6,5},{7,4},{8,11},{9,10},{10,... | collective-permute-start | bytes 1179656 | tf_op jit(solution)/shard_map/ppermute | solution.py:51
  45.0 10.8 %collective-permute-start.13 = (bf16[2,64,1536]{2,1,0:T(8,128)(2,1)}, bf16[2,64,1536]{2,1,0:T(8,128)(2,1)S(1)}, u32[]{:S(2)}, u32[]{:S(2)}) collective-permute-start(bf16[2,64,1536]{2,1,0:T(8,128)(2,1)} %get-tuple-element.108), channel_id=1, source_target_pairs={{0,6},{1,7},{2,4},{3,5},{4,2},{5,3},{6,0},{7,1},{8,14},{9,15},{10,... | collective-permute-start | bytes 1179656 | tf_op jit(solution)/shard_map/ppermute | solution.py:51
  55.8 10.5 %collective-permute-start.14 = (bf16[2,64,1536]{2,1,0:T(8,128)(2,1)S(1)}, bf16[2,64,1536]{2,1,0:T(8,128)(2,1)S(1)}, u32[]{:S(2)}, u32[]{:S(2)}) collective-permute-start(bf16[2,64,1536]{2,1,0:T(8,128)(2,1)S(1)} %copy-done.28), channel_id=1, source_target_pairs={{0,7},{1,6},{2,5},{3,4},{4,3},{5,2},{6,1},{7,0},{8,15},{9,14},{10,... | collective-permute-start | bytes 1179656 | tf_op jit(solution)/shard_map/ppermute | solution.py:51
  66.3 16.2 %collective-permute-start.15 = (bf16[4,2,96,1120]{3,2,1,0:T(8,128)(2,1)S(1)}, bf16[4,2,96,1120]{3,2,1,0:T(8,128)(2,1)}, u32[]{:S(2)}, u32[]{:S(2)}) collective-permute-start(bf16[4,2,96,1120]{3,2,1,0:T(8,128)(2,1)S(1)} %pad_maximum_fusion.quad_ref), channel_id=1, source_target_pairs={{0,8},{8,0},{1,9},{9,1},{2,10},{10,2},{3,11},{11,3},{4,12},{12,4},... | collective-permute-start | bytes 5160968 | tf_op jit(solution)/shard_map/ppermute | solution.py:43
  66.3 14.2 %collective-permute-start.16 = (bf16[2,64,1536]{2,1,0:T(8,128)(2,1)}, bf16[2,64,1536]{2,1,0:T(8,128)(2,1)}, u32[]{:S(2)}, u32[]{:S(2)}) collective-permute-start(bf16[2,64,1536]{2,1,0:T(8,128)(2,1)} %get-tuple-element.135), channel_id=1, source_target_pairs={{0,5},{1,4},{2,7},{3,6},{4,1},{5,0},{6,3},{7,2},{8,13},{9,12},{10,... | collective-permute-start | bytes 1179656 | tf_op jit(solution)/shard_map/ppermute | solution.py:51
  102.6 14.0 %collective-permute-start.17 = (bf16[128,1120]{1,0:T(8,128)(2,1)S(1)}, bf16[128,1120]{1,0:T(8,128)(2,1)S(1)}, u32[]{:S(2)}, u32[]{:S(2)}) collective-permute-start(bf16[128,1120]{1,0:T(8,128)(2,1)S(1)} %get-tuple-element.151.refs_9_), channel_id=1, source_target_pairs={{0,1},{1,0},{2,3},{3,2},{4,5},{5,4},{6,7},{7,6},{8,9},{9,8},{10,11... | collective-permute-start | bytes 860168 | tf_op jit(solution)/shard_map/ppermute | solution.py:51
  103.8 12.8 %collective-permute-start.18 = (bf16[128,1120]{1,0:T(8,128)(2,1)S(1)}, bf16[128,1120]{1,0:T(8,128)(2,1)S(1)}, u32[]{:S(2)}, u32[]{:S(2)}) collective-permute-start(bf16[128,1120]{1,0:T(8,128)(2,1)S(1)} %get-tuple-element.154.refs_12_), channel_id=1, source_target_pairs={{0,4},{1,5},{2,6},{3,7},{4,0},{5,1},{6,2},{7,3},{8,12},{9,13},{10,... | collective-permute-start | bytes 860168 | tf_op jit(solution)/shard_map/ppermute | solution.py:51
  104.1 16.2 %collective-permute-start.19 = (bf16[128,1120]{1,0:T(8,128)(2,1)S(1)}, bf16[128,1120]{1,0:T(8,128)(2,1)S(1)}, u32[]{:S(2)}, u32[]{:S(2)}) collective-permute-start(bf16[128,1120]{1,0:T(8,128)(2,1)S(1)} %get-tuple-element.155.refs_13_), channel_id=1, source_target_pairs={{0,5},{1,4},{2,7},{3,6},{4,1},{5,0},{6,3},{7,2},{8,13},{9,12},{10,... | collective-permute-start | bytes 860168 | tf_op jit(solution)/shard_map/ppermute | solution.py:51
  124.5 13.6 %collective-permute-start.24 = (bf16[128,1120]{1,0:T(8,128)(2,1)S(1)}, bf16[128,1120]{1,0:T(8,128)(2,1)S(1)}, u32[]{:S(2)}, u32[]{:S(2)}) collective-permute-start(bf16[128,1120]{1,0:T(8,128)(2,1)S(1)} %get-tuple-element.173.refs_11_), channel_id=1, source_target_pairs={{0,3},{1,2},{2,1},{3,0},{4,7},{5,6},{6,5},{7,4},{8,11},{9,10},{10,... | collective-permute-start | bytes 860168 | tf_op jit(solution)/shard_map/ppermute | solution.py:51
  124.8 13.3 %collective-permute-start.25 = (bf16[128,1120]{1,0:T(8,128)(2,1)S(1)}, bf16[128,1120]{1,0:T(8,128)(2,1)S(1)}, u32[]{:S(2)}, u32[]{:S(2)}) collective-permute-start(bf16[128,1120]{1,0:T(8,128)(2,1)S(1)} %get-tuple-element.174.refs_14_), channel_id=1, source_target_pairs={{0,6},{1,7},{2,4},{3,5},{4,2},{5,3},{6,0},{7,1},{8,14},{9,15},{10,... | collective-permute-start | bytes 860168 | tf_op jit(solution)/shard_map/ppermute | solution.py:51
  126.8 14.2 %collective-permute-start.21 = (bf16[208,1120]{1,0:T(8,128)(2,1)S(1)}, bf16[208,1120]{1,0:T(8,128)(2,1)S(1)}, u32[]{:S(2)}, u32[]{:S(2)}) collective-permute-start(bf16[208,1120]{1,0:T(8,128)(2,1)S(1)} %get-tuple-element.167), channel_id=1, source_target_pairs={{0,16},{16,0},{32,48},{48,32},{1,17},{17,1},{33,49},{49,33},{2,18}... | collective-permute-start | bytes 1397768 | tf_op jit(solution)/shard_map/ppermute | solution.py:43
  127.9 24.0 %collective-permute-start.22 = (bf16[208,1120]{1,0:T(8,128)(2,1)S(1)}, bf16[208,1120]{1,0:T(8,128)(2,1)S(1)}, u32[]{:S(2)}, u32[]{:S(2)}) collective-permute-start(bf16[208,1120]{1,0:T(8,128)(2,1)S(1)} %get-tuple-element.168), channel_id=1, source_target_pairs={{0,32},{16,48},{32,0},{48,16},{1,33},{17,49},{33,1},{49,17},{2,34}... | collective-permute-start | bytes 1397768 | tf_op jit(solution)/shard_map/ppermute | solution.py:43
  130.9 23.6 %collective-permute-start.23 = (bf16[208,1120]{1,0:T(8,128)(2,1)S(1)}, bf16[208,1120]{1,0:T(8,128)(2,1)S(1)}, u32[]{:S(2)}, u32[]{:S(2)}) collective-permute-start(bf16[208,1120]{1,0:T(8,128)(2,1)S(1)} %get-tuple-element.169), channel_id=1, source_target_pairs={{0,48},{16,32},{32,16},{48,0},{1,49},{17,33},{33,17},{49,1},{2,50}... | collective-permute-start | bytes 1397768 | tf_op jit(solution)/shard_map/ppermute | solution.py:43
  138.1 16.4 %collective-permute-start.26 = (bf16[128,1120]{1,0:T(8,128)(2,1)S(1)}, bf16[128,1120]{1,0:T(8,128)(2,1)S(1)}, u32[]{:S(2)}, u32[]{:S(2)}) collective-permute-start(bf16[128,1120]{1,0:T(8,128)(2,1)S(1)} %get-tuple-element.176.refs_15_), channel_id=1, source_target_pairs={{0,7},{1,6},{2,5},{3,4},{4,3},{5,2},{6,1},{7,0},{8,15},{9,14},{10,... | collective-permute-start | bytes 860168 | tf_op jit(solution)/shard_map/ppermute | solution.py:51
  139.9 14.7 %collective-permute-start.27 = (bf16[128,1120]{1,0:T(8,128)(2,1)S(1)}, bf16[128,1120]{1,0:T(8,128)(2,1)S(1)}, u32[]{:S(2)}, u32[]{:S(2)}) collective-permute-start(bf16[128,1120]{1,0:T(8,128)(2,1)S(1)} %get-tuple-element.177.refs_10_), channel_id=1, source_target_pairs={{0,2},{1,3},{2,0},{3,1},{4,6},{5,7},{6,4},{7,5},{8,10},{9,11},{10,... | collective-permute-start | bytes 860168 | tf_op jit(solution)/shard_map/ppermute | solution.py:51
  155.9 13.2 %collective-permute-start.28 = (bf16[64,1120]{1,0:T(8,128)(2,1)S(1)}, bf16[64,1120]{1,0:T(8,128)(2,1)S(1)}, u32[]{:S(2)}, u32[]{:S(2)}) collective-permute-start(bf16[64,1120]{1,0:T(8,128)(2,1)S(1)} %get-tuple-element.181), channel_id=1, source_target_pairs={{0,1},{1,0},{64,65},{65,64},{2,3},{3,2},{66,67},{67,66},{4,5},{5,4... | collective-permute-start | bytes 430088 | tf_op jit(solution)/shard_map/ppermute | solution.py:47
  157.1 12.0 %collective-permute-start.29 = (bf16[64,1120]{1,0:T(8,128)(2,1)S(1)}, bf16[64,1120]{1,0:T(8,128)(2,1)S(1)}, u32[]{:S(2)}, u32[]{:S(2)}) collective-permute-start(bf16[64,1120]{1,0:T(8,128)(2,1)S(1)} %get-tuple-element.182), channel_id=1, source_target_pairs={{0,64},{1,65},{64,0},{65,1},{2,66},{3,67},{66,2},{67,3},{4,68},{5,... | collective-permute-start | bytes 430088 | tf_op jit(solution)/shard_map/ppermute | solution.py:47
  159.6 9.5 %collective-permute-start.30 = (bf16[64,1120]{1,0:T(8,128)(2,1)S(1)}, bf16[64,1120]{1,0:T(8,128)(2,1)S(1)}, u32[]{:S(2)}, u32[]{:S(2)}) collective-permute-start(bf16[64,1120]{1,0:T(8,128)(2,1)S(1)} %get-tuple-element.183), channel_id=1, source_target_pairs={{0,65},{1,64},{64,1},{65,0},{2,67},{3,66},{66,3},{67,2},{4,69},{5,... | collective-permute-start | bytes 430088 | tf_op jit(solution)/shard_map/ppermute | solution.py:47
  171.6 5.9 %collective-permute-start.32 = (bf16[32,1120]{1,0:T(8,128)(2,1)S(1)}, bf16[32,1120]{1,0:T(8,128)(2,1)S(1)}, u32[]{:S(2)}, u32[]{:S(2)}) collective-permute-start(bf16[32,1120]{1,0:T(8,128)(2,1)S(1)} %get-tuple-element.198), channel_id=1, source_target_pairs={{0,4},{2,6},{4,0},{6,2},{1,5},{3,7},{5,1},{7,3},{8,12},{10,14},{12... | collective-permute-start | bytes 215048 | tf_op jit(solution)/shard_map/ppermute | solution.py:43
  172.6 5.6 %collective-permute-start.33 = (bf16[32,1120]{1,0:T(8,128)(2,1)S(1)}, bf16[32,1120]{1,0:T(8,128)(2,1)S(1)}, u32[]{:S(2)}, u32[]{:S(2)}) collective-permute-start(bf16[32,1120]{1,0:T(8,128)(2,1)S(1)} %get-tuple-element.199), channel_id=1, source_target_pairs={{0,6},{2,4},{4,2},{6,0},{1,7},{3,5},{5,3},{7,1},{8,14},{10,12},{12... | collective-permute-start | bytes 215048 | tf_op jit(solution)/shard_map/ppermute | solution.py:43
  (35 other events, 222.6 us)

commit v4 on v3

--- a/solution.py
+++ b/solution.py
@@ -16,7 +16,7 @@
 SPACE = ("yh", "z", "core")
 MEMBER = ("x", "yl")
 BF16 = jnp.bfloat16
-FIRST, SECOND = (0, 1, 4, 5), (3, 6, 7, 2)
+FIRST, SECOND = (0, 1, 4), (3, 6, 7, 2, 5)
 F32 = jnp.float32
 
 
@@ -215,11 +215,11 @@
 
 def backward_kernel(order, before, place_ref, tokens_ref, gain_ref, full_ref, *refs):
     count = len(order)
-    earlier, pieces = refs[:before], refs[before : before + count]
-    out_ref, dfield, grad = refs[before + count :]
+    earlier, pieces = refs[: len(before)], refs[len(before) : len(before) + count]
+    out_ref, dfield, grad = refs[len(before) + count :]
     features = full_ref.shape[0]
     for n in range(count):
-        dfield[pl.ds(128 * n, 128), :] = pieces[n][...].reshape(128, -1)
+        dfield[pl.ds(128 * n, 128), :] = pieces[n][...]
 
     def matmul(step, carry):
         lane = pl.multiple_of(step * 256, 256)
@@ -254,10 +254,10 @@
             return carry
 
         lax.fori_loop(0, 2, rows, 0)
-    if before:
-        for n, k in enumerate(FIRST):
+    for done, ref in zip(before, earlier):
+        for n, k in enumerate(done):
             for m in range(2):
-                out_ref[m, place_ref[3] ^ k] = earlier[0][n, m]
+                out_ref[m, place_ref[3] ^ k] = ref[n, m]
 
 
 def member_rows(parts, where):
@@ -282,15 +282,6 @@
 def get_small(ref):
     rows = ref[0:16, 0:512].astype(F32)
     return rows[0:8] + rows[8:16]
-
-
-def rows_of(picked, values):
-    high = values.astype(BF16)
-    low = (values - high.astype(F32)).astype(BF16)
-    picked = picked.astype(BF16)
-    return jnp.dot(picked, high, preferred_element_type=F32), jnp.dot(
-        picked, low, preferred_element_type=F32
-    )
 
 
 def core_kernel(keep_ref, small_ref, came_ref, own_ref, small_out_ref, *sends):
@@ -320,39 +311,35 @@
     return total, small
 
 
-def z_kernel(place_ref, own_ref, small_ref, a_ref, b_ref, c_ref, own_out_ref, small_out_ref, *sends):
+def z_kernel(own_ref, small_ref, a_ref, b_ref, c_ref, own_out_ref, small_out_ref, send_ref):
     total, small = gather_sums(own_ref, small_ref, (a_ref, b_ref, c_ref))
     small_out_ref[...] = small
-    row, source = iota((48, 192), 0), iota((48, 192), 1)
-    for step in range(4):
-        yl = place_ref[5] ^ (step % 2)
-        wanted = (step // 2) * 96 + (row // 12) * 24 + yl * 12 + row % 12
-        high, low = rows_of(source == wanted, total)
-        if step == 0:
-            own_out_ref[...] = high + low
-        else:
-            sends[step - 1][16:64, :] = high.astype(BF16)
-            put_small(sends[step - 1], small)
-
-
-def y_kernel(place_ref, own_ref, small_ref, a_ref, b_ref, c_ref, own_out_ref, small_out_ref, *sends):
-    total, small = gather_sums(own_ref, small_ref, (a_ref, b_ref, c_ref))
-    small_out_ref[...] = small
-    row, source = iota((16, 48), 0), iota((16, 48), 1)
-    for step in range(4):
-        wanted = (place_ref[4] ^ step) * 12 + row
-        high, low = rows_of((source == wanted) & (row < 12), total)
-        if step == 0:
-            own_out_ref[...] = high + low
-        else:
-            sends[step - 1][16:32, :] = high.astype(BF16)
-            put_small(sends[step - 1], small)
-
-
-def x_kernel(own_ref, small_ref, a_ref, b_ref, c_ref, share_ref, small_out_ref):
-    total, small = gather_sums(own_ref, small_ref, (a_ref, b_ref, c_ref))
+    own_out_ref[...] = total[0:96]
+    send_ref[16:112, :] = total[96:192].astype(BF16)
+    put_small(send_ref, small)
+
+
+def yh_kernel(own_ref, small_ref, came_ref, out_ref):
+    total, small = gather_sums(own_ref, small_ref, (came_ref,))
+    row, source = iota((128, 96), 0), iota((128, 96), 1)
+    pick = (source == row // 16 * 12 + row % 16) & (row % 16 < 12)
+    picked = jnp.dot(
+        pick.astype(BF16), total.astype(BF16), preferred_element_type=F32
+    ).astype(BF16)
+    for n in range(8):
+        put_small(out_ref.at[n], small)
+        out_ref[n, 16:32, :] = picked[16 * n : 16 * n + 16]
+
+
+def member_kernel(came_ref, share_ref, small_ref):
+    total = came_ref[0, 16:32, :].astype(F32)
+    small = get_small(came_ref.at[0])
+    for n in range(1, 8):
+        total = total + came_ref[n, 16:32, :].astype(F32)
+        small = small + get_small(came_ref.at[n])
     share_ref[...] = total[0:12]
-    small_out_ref[...] = small
+    for n in range(24):
+        small_ref[n : n + 1, :] = small[n // 4 : n // 4 + 1, 128 * (n % 4) : 128 * (n % 4 + 1)]
 
 
 def on_device(tokens, gain, weight, bias, target, channel_weight):
@@ -394,28 +381,30 @@
 
     arrived = {0: sources[0], 4: swap_member(sources[4], 4)}
     near = jnp.stack([weight] + [swap_y(weight, k) for k in (1, 2, 3)])
-    (p1, p2), (near,) = after((sources[1], sources[2]), near)
+    (p1,), (near,) = after((sources[1],), near)
+    arrived[1] = swap_member(p1, 1)
     wide = jnp.stack([near] + [swap(near, "x", k) for k in (1, 2, 3)])
-    arrived[1], arrived[2] = swap_member(p1, 1), swap_member(p2, 2)
+    (wide, p3, p6), (arrived[4], truth, wt) = after(
+        (wide, sources[3], sources[6]), arrived[4], truth, wt
+    )
     pair = jnp.stack([member_rows(wide[:, 2 * k : 2 * k + 2], where) for k in range(2)])
-    (pair, p3, p6), done = after(
-        (pair, sources[3], sources[6]), arrived[4], arrived[1], arrived[2], truth, wt
-    )
-    arrived[4], arrived[1], arrived[2], truth, wt = done
     quad = jnp.stack([pair] + [swap(pair, "z", k) for k in (1, 2, 3)])
     arrived[3], arrived[6] = swap_member(p3, 3), swap_member(p6, 6)
-    (p7, p5), (arrived[3], arrived[6]) = after(
-        (sources[7], sources[5]), arrived[3], arrived[6]
-    )
-    arrived[7], arrived[5] = swap_member(p7, 7), swap_member(p5, 5)
-    normed = {k: norm_piece(arrived[k], gain_row) for k in (0, 4, 1, 2, 3, 6)}
-    early = [n for k in (0, 4, 1, 2, 3, 6) for n in normed[k]]
-    (quad,), done = after((quad,), arrived[7], *early)
-    arrived[7] = done[0]
-    for n, k in enumerate((0, 4, 1, 2, 3, 6)):
-        normed[k] = done[1 + 2 * n : 3 + 2 * n]
+    (p7, p2), (arrived[1], arrived[6]) = after(
+        (sources[7], sources[2]), arrived[1], arrived[6]
+    )
+    arrived[7], arrived[2] = swap_member(p7, 7), swap_member(p2, 2)
+    (p5,), (arrived[3],) = after((sources[5],), arrived[3])
+    arrived[5] = swap_member(p5, 5)
+    early = (0, 4, 1, 3, 6)
+    normed = {k: norm_piece(arrived[k], gain_row) for k in early}
+    held = [n for k in early for n in normed[k]]
+    (quad,), done = after((quad,), arrived[7], arrived[2], arrived[5], *held)
+    arrived[7], arrived[2], arrived[5] = done[:3]
+    for n, k in enumerate(early):
+        normed[k] = done[3 + 2 * n : 5 + 2 * n]
     other = swap(quad, "core", 1)
-    for k in (7, 5):
+    for k in (7, 2, 5):
         normed[k] = norm_piece(arrived[k], gain_row)
 
     full, bias_part, *dfield = pl.pallas_call(
@@ -438,7 +427,7 @@
     )(place, quad, other, bias.reshape(1, outs), truth, wt, *[normed[k][0] for k in range(8)])
 
     returned = {0: dfield[0]}
-    for k in (1, 4, 5):
+    for k in (1, 4):
         returned[k] = swap_member(dfield[k], k)
     keep, send, small = pl.pallas_call(
         grad_kernel,
@@ -463,13 +452,12 @@
         *[normed[k][1] for k in range(8)], *dfield,
     )
 
-    def backward(order, before):
+    def backward(order, *before):
         count = len(order)
+        shape = (2, 8, 64, features) if before else (count, 2, 64, features)
         return pl.pallas_call(
-            functools.partial(backward_kernel, order, len(before)),
-            out_shape=jax.ShapeDtypeStruct(
-                (2, 8, 64, features) if before else (count, 2, 64, features), BF16
-            ),
+            functools.partial(backward_kernel, order, [done for done, _ in before]),
+            out_shape=jax.ShapeDtypeStruct(shape, BF16),
             in_specs=[smem] + vmem(3 + count + len(before)),
             out_specs=vmem(1)[0],
             scratch_shapes=[
@@ -477,9 +465,12 @@
                 pltpu.VMEM((128 * count, features), F32),
             ],
             compiler_params=params(32),
-            cost_estimate=cost(8000000000, 30000000),
+            cost_estimate=cost(1000, 1000),
             name="backward",
-        )(place, pieces, gain_row, full, *before, *[returned[k] for k in order])
+        )(
+            place, pieces, gain_row, full,
+            *[part for _, part in before], *[returned[k] for k in order],
+        )
 
     def combine(kernel, name, own_rows, send_rows, sends, *operands):
         return pl.pallas_call(
@@ -497,35 +488,54 @@
             name=name,
         )(*operands)
 
-    (send,), done = after((send,), returned[1], returned[4], returned[5])
-    returned[1], returned[4], returned[5] = done
+    (send,), done = after((send,), *[returned[k] for k in (1, 4)])
+    for k, piece in zip((1, 4), done):
+        returned[k] = piece
     came = swap(send, "core", 1)
     own, small, *sends = combine(core_kernel, "core_sums", 192, 208, 3, keep, small, came)
-    sends[0], sends[1], sends[2], d3, d6 = after(
-        (*sends, dfield[3], dfield[6])
-    )[0]
     came = [swap(value, "z", k) for k, value in zip((1, 2, 3), sends)]
+    (d3, d6), (small,) = after((dfield[3], dfield[6]), small)
     returned[3], returned[6] = swap_member(d3, 3), swap_member(d6, 6)
-    half = backward(FIRST, ())
-    (d7, d2), (half, returned[3], returned[6]) = after(
-        (dfield[7], dfield[2]), half, returned[3], returned[6]
-    )
-    returned[7], returned[2] = swap_member(d7, 7), swap_member(d2, 2)
-    came, (half, returned[7], returned[2]) = after(
-        came, half, returned[7], returned[2]
-    )
-    own, small, *sends = combine(z_kernel, "z_sums", 48, 64, 3, place, own, small, *came)
-    came = [swap_y(value, k) for k, value in zip((1, 2, 3), sends)]
-    result = backward(SECOND, (half,))
-    came, (result,) = after(came, result)
-    own, small, *sends = combine(y_kernel, "y_sums", 16, 32, 3, place, own, small, *came)
-    came = [swap(value, "x", k) for k, value in zip((1, 2, 3), sends)]
-    share, small = combine(x_kernel, "x_sums", 12, 0, 0, own, small, *came)
+    late = (7, 2, 5)
+    held, (returned[3], returned[6]) = after(
+        [dfield[k] for k in late], returned[3], returned[6]
+    )
+    for k, piece in zip(late, held):
+        returned[k] = swap_member(piece, k)
+    first = backward(FIRST)
+    came, (first,) = after(came, first)
+    own, small, send = combine(z_kernel, "z_sums", 96, 112, 1, own, small, *came)
+    came = swap(send, "yh", 1)
+    result = backward(SECOND, (FIRST, first))
+    (came,), (result,) = after((came,), result)
+    send = pl.pallas_call(
+        yh_kernel,
+        out_shape=jax.ShapeDtypeStruct((8, 32, outs), BF16),
+        in_specs=vmem(3),
+        out_specs=vmem(1)[0],
+        compiler_params=params(16),
+        cost_estimate=cost(1000000000, 4000000),
+        name="yh_sums",
+    )(own, small, came)
+    came = lax.all_to_all(send, MEMBER, 0, 0)
+    share, small = pl.pallas_call(
+        member_kernel,
+        out_shape=(
+            jax.ShapeDtypeStruct((12, outs), F32),
+            jax.ShapeDtypeStruct((24, 128), F32),
+        ),
+        in_specs=vmem(1),
+        out_specs=tuple(vmem(2)),
+        compiler_params=params(16),
+        cost_estimate=cost(1000000000, 4000000),
+        name="member_sums",
+    )(came)
+    small = small.reshape(-1)
     return (
         result.reshape(tokens.shape),
-        small[0:3].reshape(-1),
+        small[:features],
         share,
-        small[3:6].reshape(-1)[:outs],
+        small[features : features + outs],
     )
 
 

time: 180 us -> 159 us (0.88)
  waiting for transfers between devices: 59.5 us -> 34.5 us
  blocking collectives: 0 us -> 11.5 us
  starting transfers between devices: 51.4 us -> 47 us
  Pallas kernels: 51.8 us -> 48.8 us
    ppermute x14, waiting for transfers between devices: 33.5 us -> 13.6 us  [swap_member(): return lax.ppermute(value, MEMBER, [(i, i ^ step) for i in range(8)])]
    all_to_all x0 -> x1, blocking collectives: none -> 11.5 us  [on_device(): came = lax.all_to_all(send, MEMBER, 0, 0)]
    ppermute x14 -> x12, waiting for transfers between devices: 26 us -> 20.9 us  [swap(): return lax.ppermute(value, axis, [(i, i ^ step) for i in range(SIZE[axis])])]
    ppermute x6 -> x3, starting transfers between devices: 9.41 us -> 4.64 us  [swap_y(): return lax.ppermute(value, ('yh', 'yl'), [(i, i ^ step) for i in range(4)])]
    pallas_call x4 -> x2, Pallas kernels: 3.18 us -> 0.52 us  [combine(): pl.pallas_call(kernel, out_shape=(jax.ShapeDtypeStruct((own_rows, outs),...]
    pallas_call x2 -> x4, Pallas kernels: 15 us -> 15.9 us  [the longest x2 15 us: backward(): pl.pallas_call(functools.partial(backward_kernel, order, [done for done,...]
    ppermute x14 -> x12, starting transfers between devices: 18.6 us -> 17.8 us  [swap(): return lax.ppermute(value, axis, [(i, i ^ step) for i in range(SIZE[axis])])]
    unnamed x66 -> x70, local copies, waits for them, and re-layouts: 9.03 us -> 8.94 us
  transfers between devices with their start and end apart: 34 -> 29, of which waited for: 13 -> 13; matrix products, arithmetic and copies ran while one was open for 3% -> 4% of each run, Pallas kernels for 16% -> 18%
where the time goes in v4:
time: 159 us
  Pallas kernels  48.8 us (31%)
  starting transfers between devices  47 us (30%)
  waiting for transfers between devices  34.5 us (22%)
  local copies, waits for them, and re-layouts  14.8 us (9%)
  blocking collectives  11.5 us (7%)
    ppermute x14, starting transfers between devices, swap_member(): return lax.ppermute(value, MEMBER, [(i, i ^ step) for i in range(8)])  24.6 us
    ppermute x12, waiting for transfers between devices, swap(): return lax.ppermute(value, axis, [(i, i ^ step) for i in range(SIZE[axis])])  20.9 us
    pallas_call x1, Pallas kernels, on_device(): pl.pallas_call(pairs_kernel, out_shape=(jax.ShapeDtypeStruct((features, o...  18.8 us
    ppermute x12, starting transfers between devices, swap(): return lax.ppermute(value, axis, [(i, i ^ step) for i in range(SIZE[axis])])  17.8 us
    pallas_call x2, Pallas kernels, backward(): pl.pallas_call(functools.partial(backward_kernel, order, [done for done,...  15 us
    ppermute x14, waiting for transfers between devices, swap_member(): return lax.ppermute(value, MEMBER, [(i, i ^ step) for i in range(8)])  13.6 us
    all_to_all x1, blocking collectives, on_device(): came = lax.all_to_all(send, MEMBER, 0, 0)  11.5 us
    unnamed x70, local copies, waits for them, and re-layouts  8.94 us
  transfers between devices with their start and end apart: 29, of which 13 were waited for; matrix products, arithmetic and copies ran while one was open for 4% of the time, Pallas kernels for 18%

profile of v4, /device:TPU:0, one launch (start us, length us, event | category | flops | bytes accessed | tf_op | source)
XLA Modules:
  0.0 159.0 jit_solution(12808681169660617709)
XLA Ops:
  0.6 1.7 %collective-permute-start = (bf16[12,1120]{1,0:T(8,128)(2,1)}, bf16[12,1120]{1,0:T(8,128)(2,1)S(1)}, u32[]{:S(2)}, u32[]{:S(2)}) collective-permute-start(bf16[12,1120]{1,0:T(8,128)(2,1)} %param.9), channel_id=1, source_target_pairs={{0,1},{1,0},{64,65},{65,64},{2,3},{3,2},{66,67},{67,66},{4,5},{5,4... | collective-permute-start | bytes 80648 | tf_op jit(solution)/shard_map/ppermute | solution.py:47
  2.4 2.2 %collective-permute-start.2 = (bf16[12,1120]{1,0:T(8,128)(2,1)}, bf16[12,1120]{1,0:T(8,128)(2,1)S(1)}, u32[]{:S(2)}, u32[]{:S(2)}) collective-permute-start(bf16[12,1120]{1,0:T(8,128)(2,1)} %param.9), channel_id=1, source_target_pairs={{0,65},{1,64},{64,1},{65,0},{2,67},{3,66},{66,3},{67,2},{4,69},{5,... | collective-permute-start | bytes 80648 | tf_op jit(solution)/shard_map/ppermute | solution.py:47
  5.3 3.1 %constant_dynamic-slice_fusion = (bf16[2,1,64,1536]{3,2,1,0:T(8,128)(2,1)S(1)}, bf16[2,64,1536]{2,1,0:T(8,128)(2,1)}, bf16[2,64,1536]{2,1,0:T(8,128)(2,1)}, bf16...) fusion(bf16[2,8,64,1536]{3,2,1,0:T(8,128)(2,1)} %bitcast.54, ...), kind=kLoop, calls=%fused_computation.20 | loop fusion | bytes 6291488 | tf_op jit(solution)/shard_map/jit(dynamic_index_in_dim)/dynamic_slice | solution.py:360
  8.4 3.0 %collective-permute-start.6 = (bf16[2,64,1536]{2,1,0:T(8,128)(2,1)S(1)}, bf16[2,64,1536]{2,1,0:T(8,128)(2,1)S(1)}, u32[]{:S(2)}, u32[]{:S(2)}) collective-permute-start(bf16[2,64,1536]{2,1,0:T(8,128)(2,1)S(1)} %get-tuple-element.176), channel_id=1, source_target_pairs={{0,4},{1,5},{2,6},{3,7},{4,0},{5,1},{6,2},{7,3},{8,12},{9,13},{10,... | collective-permute-start | bytes 1179656 | tf_op jit(solution)/shard_map/ppermute | solution.py:51
  11.7 1.3 truth.1.truth_ref
  17.4 1.5 collective-permute-start.4
  18.9 1.4 collective-permute-start.3
  20.3 1.3 collective-permute-start.10
  21.6 5.0 %collective-permute-done.5 = bf16[4,12,1120]{2,1,0:T(8,128)(2,1)S(1)} collective-permute-done((bf16[4,12,1120]{2,1,0:T(8,128)(2,1)S(1)}, bf16[4,12,1120]{2,1,0:T(8,128)(2,1)S(1)}, u32[]{:S(2)}, u32[]{:S(2)}) %collective-permute-start.5) | collective-permute-done | bytes 107552 | tf_op jit(solution)/shard_map/ppermute | solution.py:43
  27.6 2.7 %collective-permute-start.11 = (bf16[2,64,1536]{2,1,0:T(8,128)(2,1)}, bf16[2,64,1536]{2,1,0:T(8,128)(2,1)S(1)}, u32[]{:S(2)}, u32[]{:S(2)}) collective-permute-start(bf16[2,64,1536]{2,1,0:T(8,128)(2,1)} %get-tuple-element.91), channel_id=1, source_target_pairs={{0,6},{1,7},{2,4},{3,5},{4,2},{5,3},{6,0},{7,1},{8,14},{9,15},{10,... | collective-permute-start | bytes 1179656 | tf_op jit(solution)/shard_map/ppermute | solution.py:51
  31.0 4.0 %collective-permute-start.8 = (bf16[2,96,1120]{2,1,0:T(8,128)(2,1)S(1)}, bf16[2,96,1120]{2,1,0:T(8,128)(2,1)S(1)}, u32[]{:S(2)}, u32[]{:S(2)}) collective-permute-start(bf16[2,96,1120]{2,1,0:T(8,128)(2,1)S(1)} %get-tuple-element.183), channel_id=1, source_target_pairs={{0,32},{16,48},{32,0},{48,16},{1,33},{17,49},{33,1},{49,17},{2,34}... | collective-permute-start | bytes 1290248 | tf_op jit(solution)/shard_map/ppermute | solution.py:43
  37.2 2.9 %collective-permute-done.11 = bf16[2,64,1536]{2,1,0:T(8,128)(2,1)S(1)} collective-permute-done((bf16[2,64,1536]{2,1,0:T(8,128)(2,1)}, bf16[2,64,1536]{2,1,0:T(8,128)(2,1)S(1)}, u32[]{:S(2)}, u32[]{:S(2)}) %collective-permute-start.11) | collective-permute-done | bytes 393248 | tf_op jit(solution)/shard_map/ppermute | solution.py:51
  40.0 3.1 %collective-permute-start.12 = (bf16[2,64,1536]{2,1,0:T(8,128)(2,1)S(1)}, bf16[2,64,1536]{2,1,0:T(8,128)(2,1)S(1)}, u32[]{:S(2)}, u32[]{:S(2)}) collective-permute-start(bf16[2,64,1536]{2,1,0:T(8,128)(2,1)S(1)} %copy-done.30), channel_id=1, source_target_pairs={{0,7},{1,6},{2,5},{3,4},{4,3},{5,2},{6,1},{7,0},{8,15},{9,14},{10,... | collective-permute-start | bytes 1179656 | tf_op jit(solution)/shard_map/ppermute | solution.py:51
  46.0 2.4 %collective-permute-start.15 = (bf16[2,64,1536]{2,1,0:T(8,128)(2,1)S(1)}, bf16[2,64,1536]{2,1,0:T(8,128)(2,1)S(1)}, u32[]{:S(2)}, u32[]{:S(2)}) collective-permute-start(bf16[2,64,1536]{2,1,0:T(8,128)(2,1)S(1)} %copy-done.28), channel_id=1, source_target_pairs={{0,5},{1,4},{2,7},{3,6},{4,1},{5,0},{6,3},{7,2},{8,13},{9,12},{10,... | collective-permute-start | bytes 1179656 | tf_op jit(solution)/shard_map/ppermute | solution.py:51
  50.4 4.6 %collective-permute-done.7 = bf16[2,96,1120]{2,1,0:T(8,128)(2,1)S(1)} collective-permute-done((bf16[2,96,1120]{2,1,0:T(8,128)(2,1)S(1)}, bf16[2,96,1120]{2,1,0:T(8,128)(2,1)S(1)}, u32[]{:S(2)}, u32[]{:S(2)}) %collective-permute-start.7) | collective-permute-done | bytes 430112 | tf_op jit(solution)/shard_map/ppermute | solution.py:43
  56.1 5.7 %collective-permute-done.15 = bf16[2,64,1536]{2,1,0:T(8,128)(2,1)S(1)} collective-permute-done((bf16[2,64,1536]{2,1,0:T(8,128)(2,1)S(1)}, bf16[2,64,1536]{2,1,0:T(8,128)(2,1)S(1)}, u32[]{:S(2)}, u32[]{:S(2)}) %collective-permute-start.15) | collective-permute-done | bytes 393248 | tf_op jit(solution)/shard_map/ppermute | solution.py:51
  66.7 18.8 %pairs.1 = (bf16[1536,1120]{1,0:T(8,128)(2,1)S(1)}, f32[1,1152]{1,0:T(1,128)S(1)}, bf16[128,1120]{1,0:T(8,128)(2,1)S(1)}, bf16[128,1120]{1,0:T(8,128)(2,1)S(1)},...) custom-call(s32[6]{0:T(128)S(1)} %stack.81.place_ref, ...), custom_call_target="tpu_custom_call" | custom-call | flops 20000000000 | bytes 80000000 | tf_op jit(solution)/shard_map/pairs/pallas_call | solution.py:410
  86.5 2.0 %collective-permute-start.18 = (bf16[128,1120]{1,0:T(8,128)(2,1)S(1)}, bf16[128,1120]{1,0:T(8,128)(2,1)S(1)}, u32[]{:S(2)}, u32[]{:S(2)}) collective-permute-start(bf16[128,1120]{1,0:T(8,128)(2,1)S(1)} %get-tuple-element.138.refs_12_), channel_id=1, source_target_pairs={{0,4},{1,5},{2,6},{3,7},{4,0},{5,1},{6,2},{7,3},{8,12},{9,13},{10,... | collective-permute-start | bytes 860168 | tf_op jit(solution)/shard_map/ppermute | solution.py:51
  88.5 8.7 %weight_gradient.1 = (f32[2,4,96,1120]{3,2,1,0:T(8,128)S(1)}, bf16[784,1120]{1,0:T(8,128)(2,1)S(1)}, f32[8,512]{1,0:T(8,128)S(1)}) custom-call(s32[6]{0:T(128)S(1)} %stack.81.place_ref, bf16[1536,1120]{1,0:T(8,128)(2,1)S(1)} %get-tuple-element.124.full_ref, f32[1,1152]{1,0:T(1,128)S(1)} %get-tuple-element.125.bias_part_ref, ...), custom_call_target="tpu_custom_call" | custom-call | flops 12000000000 | bytes 45000000 | tf_op jit(solution)/shard_map/weight_gradient/pallas_call | solution.py:432
  97.4 3.7 %collective-permute-done.19.came_ref = bf16[784,1120]{1,0:T(8,128)(2,1)S(1)} collective-permute-done((bf16[784,1120]{1,0:T(8,128)(2,1)S(1)}, bf16[784,1120]{1,0:T(8,128)(2,1)S(1)}, u32[]{:S(2)}, u32[]{:S(2)}) %collective-permute-start.19) | collective-permute-done | bytes 1756192 | tf_op jit(solution)/shard_map/ppermute | solution.py:43
  101.4 2.0 %collective-permute-start.20 = (bf16[208,1120]{1,0:T(8,128)(2,1)S(1)}, bf16[208,1120]{1,0:T(8,128)(2,1)S(1)}, u32[]{:S(2)}, u32[]{:S(2)}) collective-permute-start(bf16[208,1120]{1,0:T(8,128)(2,1)S(1)} %get-tuple-element.149), channel_id=1, source_target_pairs={{0,16},{16,0},{32,48},{48,32},{1,17},{17,1},{33,49},{49,33},{2,18}... | collective-permute-start | bytes 1397768 | tf_op jit(solution)/shard_map/ppermute | solution.py:43
  103.4 3.6 %collective-permute-start.21 = (bf16[208,1120]{1,0:T(8,128)(2,1)S(1)}, bf16[208,1120]{1,0:T(8,128)(2,1)S(1)}, u32[]{:S(2)}, u32[]{:S(2)}) collective-permute-start(bf16[208,1120]{1,0:T(8,128)(2,1)S(1)} %get-tuple-element.150), channel_id=1, source_target_pairs={{0,32},{16,48},{32,0},{48,16},{1,33},{17,49},{33,1},{49,17},{2,34}... | collective-permute-start | bytes 1397768 | tf_op jit(solution)/shard_map/ppermute | solution.py:43
  107.0 2.3 %collective-permute-start.24 = (bf16[128,1120]{1,0:T(8,128)(2,1)S(1)}, bf16[128,1120]{1,0:T(8,128)(2,1)S(1)}, u32[]{:S(2)}, u32[]{:S(2)}) collective-permute-start(bf16[128,1120]{1,0:T(8,128)(2,1)S(1)} %get-tuple-element.159.refs_11_), channel_id=1, source_target_pairs={{0,3},{1,2},{2,1},{3,0},{4,7},{5,6},{6,5},{7,4},{8,11},{9,10},{10,... | collective-permute-start | bytes 860168 | tf_op jit(solution)/shard_map/ppermute | solution.py:51
  109.9 5.4 %backward.2.refs_0_ = bf16[3,2,64,1536]{3,2,1,0:T(8,128)(2,1)S(1)} custom-call(s32[6]{0:T(128)S(1)} %stack.81.place_ref, bf16[2,8,64,1536]{3,2,1,0:T(8,128)(2,1)S(1)} %bitcast.55, f32[1,1536]{1,0:T(1,128)S(1)} %reshape.152.gain_ref, bf16[1536,1120]{1,0:T(8,128)(2,1)S(1)} %get-tuple-element.124.full_ref, ...), custom_call_target="tpu_custom_call" | custom-call | flops 1000 | bytes 1000 | tf_op jit(solution)/shard_map/backward/pallas_call | solution.py:458
  116.4 2.3 %collective-permute-done.25.refs_2_ = bf16[128,1120]{1,0:T(8,128)(2,1)S(1)} collective-permute-done((bf16[128,1120]{1,0:T(8,128)(2,1)S(1)}, bf16[128,1120]{1,0:T(8,128)(2,1)S(1)}, u32[]{:S(2)}, u32[]{:S(2)}) %collective-permute-start.25) | collective-permute-done | bytes 286752 | tf_op jit(solution)/shard_map/ppermute | solution.py:51
  120.2 4.1 %collective-permute-start.28 = (bf16[128,1120]{1,0:T(8,128)(2,1)S(1)}, bf16[128,1120]{1,0:T(8,128)(2,1)S(1)}, u32[]{:S(2)}, u32[]{:S(2)}) collective-permute-start(bf16[128,1120]{1,0:T(8,128)(2,1)S(1)} %get-tuple-element.165.refs_13_), channel_id=1, source_target_pairs={{0,5},{1,4},{2,7},{3,6},{4,1},{5,0},{6,3},{7,2},{8,13},{9,12},{10,... | collective-permute-start | bytes 860168 | tf_op jit(solution)/shard_map/ppermute | solution.py:51
  124.3 4.0 %collective-permute-done.21.b_ref = bf16[208,1120]{1,0:T(8,128)(2,1)S(1)} collective-permute-done((bf16[208,1120]{1,0:T(8,128)(2,1)S(1)}, bf16[208,1120]{1,0:T(8,128)(2,1)S(1)}, u32[]{:S(2)}, u32[]{:S(2)}) %collective-permute-start.21) | collective-permute-done | bytes 465952 | tf_op jit(solution)/shard_map/ppermute | solution.py:43
  128.4 2.6 %collective-permute-done.22.c_ref = bf16[208,1120]{1,0:T(8,128)(2,1)S(1)} collective-permute-done((bf16[208,1120]{1,0:T(8,128)(2,1)S(1)}, bf16[208,1120]{1,0:T(8,128)(2,1)S(1)}, u32[]{:S(2)}, u32[]{:S(2)}) %collective-permute-start.22) | collective-permute-done | bytes 465952 | tf_op jit(solution)/shard_map/ppermute | solution.py:43
  131.1 3.0 %collective-permute-start.23 = (bf16[112,1120]{1,0:T(8,128)(2,1)S(1)}, bf16[112,1120]{1,0:T(8,128)(2,1)S(1)}, u32[]{:S(2)}, u32[]{:S(2)}) collective-permute-start(bf16[112,1120]{1,0:T(8,128)(2,1)S(1)} %get-tuple-element.157), channel_id=1, source_target_pairs={{0,64},{64,0},{1,65},{65,1},{2,66},{66,2},{3,67},{67,3},{4,68},{68... | collective-permute-start | bytes 752648 | tf_op jit(solution)/shard_map/ppermute | solution.py:43
  134.1 1.6 collective-permute-done.28.refs_5_
  135.7 9.6 %backward.3 = bf16[2,8,64,1536]{3,2,1,0:T(8,128)(2,1)} custom-call(s32[6]{0:T(128)S(1)} %stack.81.place_ref, bf16[2,8,64,1536]{3,2,1,0:T(8,128)(2,1)S(1)} %bitcast.56, f32[1,1536]{1,0:T(1,128)S(1)} %reshape.152.gain_ref, bf16[1536,1120]{1,0:T(8,128)(2,1)S(1)} %get-tuple-element.124.full_ref, bf16[3,2,64,1536]{3,2,1,0:T(8,128)(2,1)S(1)} %backward.2.refs_0_, ...), custom_call_target="tpu_custom_call" | custom-call | flops 1000 | bytes 1000 | tf_op jit(solution)/shard_map/backward/pallas_call | solution.py:458
  145.6 11.5 %all_to_all.5.came_ref = bf16[8,32,1120]{2,1,0:T(8,128)(2,1)S(1)} all-to-all(bf16[8,32,1120]{2,1,0:T(8,128)(2,1)S(1)} %yh_sums.1), channel_id=1, replica_groups=mesh['yh'=2,'z'=4,'core'=2,'x'=4,'yl'=2] {'x','yl'}, dimensions={0} | all-to-all | bytes 1146880 | tf_op jit(solution)/shard_map/all_to_all | solution.py:520
  (137 shorter events, 26.7 us)
Async XLA Ops:
  0.6 15.4 %collective-permute-start = (bf16[12,1120]{1,0:T(8,128)(2,1)}, bf16[12,1120]{1,0:T(8,128)(2,1)S(1)}, u32[]{:S(2)}, u32[]{:S(2)}) collective-permute-start(bf16[12,1120]{1,0:T(8,128)(2,1)} %param.9), channel_id=1, source_target_pairs={{0,1},{1,0},{64,65},{65,64},{2,3},{3,2},{66,67},{67,66},{4,5},{5,4... | collective-permute-start | bytes 80648 | tf_op jit(solution)/shard_map/ppermute | solution.py:47
  2.4 13.7 %collective-permute-start.2 = (bf16[12,1120]{1,0:T(8,128)(2,1)}, bf16[12,1120]{1,0:T(8,128)(2,1)S(1)}, u32[]{:S(2)}, u32[]{:S(2)}) collective-permute-start(bf16[12,1120]{1,0:T(8,128)(2,1)} %param.9), channel_id=1, source_target_pairs={{0,65},{1,64},{64,1},{65,0},{2,67},{3,66},{66,3},{67,2},{4,69},{5,... | collective-permute-start | bytes 80648 | tf_op jit(solution)/shard_map/ppermute | solution.py:47
  4.6 11.5 %collective-permute-start.1 = (bf16[12,1120]{1,0:T(8,128)(2,1)}, bf16[12,1120]{1,0:T(8,128)(2,1)S(1)}, u32[]{:S(2)}, u32[]{:S(2)}) collective-permute-start(bf16[12,1120]{1,0:T(8,128)(2,1)} %param.9), channel_id=1, source_target_pairs={{0,64},{1,65},{64,0},{65,1},{2,66},{3,67},{66,2},{67,3},{4,68},{5,... | collective-permute-start | bytes 80648 | tf_op jit(solution)/shard_map/ppermute | solution.py:47
  8.4 18.4 %collective-permute-start.6 = (bf16[2,64,1536]{2,1,0:T(8,128)(2,1)S(1)}, bf16[2,64,1536]{2,1,0:T(8,128)(2,1)S(1)}, u32[]{:S(2)}, u32[]{:S(2)}) collective-permute-start(bf16[2,64,1536]{2,1,0:T(8,128)(2,1)S(1)} %get-tuple-element.176), channel_id=1, source_target_pairs={{0,4},{1,5},{2,6},{3,7},{4,0},{5,1},{6,2},{7,3},{8,12},{9,13},{10,... | collective-permute-start | bytes 1179656 | tf_op jit(solution)/shard_map/ppermute | solution.py:51
  16.1 10.4 %collective-permute-start.5 = (bf16[4,12,1120]{2,1,0:T(8,128)(2,1)S(1)}, bf16[4,12,1120]{2,1,0:T(8,128)(2,1)S(1)}, u32[]{:S(2)}, u32[]{:S(2)}) collective-permute-start(bf16[4,12,1120]{2,1,0:T(8,128)(2,1)S(1)} %pad_maximum_fusion.3), channel_id=1, source_target_pairs={{0,6},{2,4},{4,2},{6,0},{1,7},{3,5},{5,3},{7,1},{8,14},{10,12},{12... | collective-permute-start | bytes 322568 | tf_op jit(solution)/shard_map/ppermute | solution.py:43
  17.4 9.2 %collective-permute-start.4 = (bf16[4,12,1120]{2,1,0:T(8,128)(2,1)S(1)}, bf16[4,12,1120]{2,1,0:T(8,128)(2,1)S(1)}, u32[]{:S(2)}, u32[]{:S(2)}) collective-permute-start(bf16[4,12,1120]{2,1,0:T(8,128)(2,1)S(1)} %pad_maximum_fusion.3), channel_id=1, source_target_pairs={{0,4},{2,6},{4,0},{6,2},{1,5},{3,7},{5,1},{7,3},{8,12},{10,14},{12... | collective-permute-start | bytes 322568 | tf_op jit(solution)/shard_map/ppermute | solution.py:43
  18.9 7.8 %collective-permute-start.3 = (bf16[4,12,1120]{2,1,0:T(8,128)(2,1)S(1)}, bf16[4,12,1120]{2,1,0:T(8,128)(2,1)S(1)}, u32[]{:S(2)}, u32[]{:S(2)}) collective-permute-start(bf16[4,12,1120]{2,1,0:T(8,128)(2,1)S(1)} %pad_maximum_fusion.3), channel_id=1, source_target_pairs={{0,2},{2,0},{4,6},{6,4},{1,3},{3,1},{5,7},{7,5},{8,10},{10,8},{12,... | collective-permute-start | bytes 322568 | tf_op jit(solution)/shard_map/ppermute | solution.py:43
  20.3 16.8 %collective-permute-start.10 = (bf16[2,64,1536]{2,1,0:T(8,128)(2,1)}, bf16[2,64,1536]{2,1,0:T(8,128)(2,1)S(1)}, u32[]{:S(2)}, u32[]{:S(2)}) collective-permute-start(bf16[2,64,1536]{2,1,0:T(8,128)(2,1)} %get-tuple-element.90), channel_id=1, source_target_pairs={{0,1},{1,0},{2,3},{3,2},{4,5},{5,4},{6,7},{7,6},{8,9},{9,8},{10,11... | collective-permute-start | bytes 1179656 | tf_op jit(solution)/shard_map/ppermute | solution.py:51
  27.6 12.4 %collective-permute-start.11 = (bf16[2,64,1536]{2,1,0:T(8,128)(2,1)}, bf16[2,64,1536]{2,1,0:T(8,128)(2,1)S(1)}, u32[]{:S(2)}, u32[]{:S(2)}) collective-permute-start(bf16[2,64,1536]{2,1,0:T(8,128)(2,1)} %get-tuple-element.91), channel_id=1, source_target_pairs={{0,6},{1,7},{2,4},{3,5},{4,2},{5,3},{6,0},{7,1},{8,14},{9,15},{10,... | collective-permute-start | bytes 1179656 | tf_op jit(solution)/shard_map/ppermute | solution.py:51
  30.3 12.8 %collective-permute-start.14 = (bf16[2,64,1536]{2,1,0:T(8,128)(2,1)S(1)}, bf16[2,64,1536]{2,1,0:T(8,128)(2,1)S(1)}, u32[]{:S(2)}, u32[]{:S(2)}) collective-permute-start(bf16[2,64,1536]{2,1,0:T(8,128)(2,1)S(1)} %get-tuple-element.94), channel_id=1, source_target_pairs={{0,3},{1,2},{2,1},{3,0},{4,7},{5,6},{6,5},{7,4},{8,11},{9,10},{10,... | collective-permute-start | bytes 1179656 | tf_op jit(solution)/shard_map/ppermute | solution.py:51
  31.0 15.0 %collective-permute-start.8 = (bf16[2,96,1120]{2,1,0:T(8,128)(2,1)S(1)}, bf16[2,96,1120]{2,1,0:T(8,128)(2,1)S(1)}, u32[]{:S(2)}, u32[]{:S(2)}) collective-permute-start(bf16[2,96,1120]{2,1,0:T(8,128)(2,1)S(1)} %get-tuple-element.183), channel_id=1, source_target_pairs={{0,32},{16,48},{32,0},{48,16},{1,33},{17,49},{33,1},{49,17},{2,34}... | collective-permute-start | bytes 1290248 | tf_op jit(solution)/shard_map/ppermute | solution.py:43
  34.9 20.0 %collective-permute-start.7 = (bf16[2,96,1120]{2,1,0:T(8,128)(2,1)S(1)}, bf16[2,96,1120]{2,1,0:T(8,128)(2,1)S(1)}, u32[]{:S(2)}, u32[]{:S(2)}) collective-permute-start(bf16[2,96,1120]{2,1,0:T(8,128)(2,1)S(1)} %get-tuple-element.183), channel_id=1, source_target_pairs={{0,16},{16,0},{32,48},{48,32},{1,17},{17,1},{33,49},{49,33},{2,18}... | collective-permute-start | bytes 1290248 | tf_op jit(solution)/shard_map/ppermute | solution.py:43
  37.2 17.8 %collective-permute-start.9 = (bf16[2,96,1120]{2,1,0:T(8,128)(2,1)S(1)}, bf16[2,96,1120]{2,1,0:T(8,128)(2,1)S(1)}, u32[]{:S(2)}, u32[]{:S(2)}) collective-permute-start(bf16[2,96,1120]{2,1,0:T(8,128)(2,1)S(1)} %get-tuple-element.183), channel_id=1, source_target_pairs={{0,48},{16,32},{32,16},{48,0},{1,49},{17,33},{33,17},{49,1},{2,50}... | collective-permute-start | bytes 1290248 | tf_op jit(solution)/shard_map/ppermute | solution.py:43
  40.0 15.3 %collective-permute-start.12 = (bf16[2,64,1536]{2,1,0:T(8,128)(2,1)S(1)}, bf16[2,64,1536]{2,1,0:T(8,128)(2,1)S(1)}, u32[]{:S(2)}, u32[]{:S(2)}) collective-permute-start(bf16[2,64,1536]{2,1,0:T(8,128)(2,1)S(1)} %copy-done.30), channel_id=1, source_target_pairs={{0,7},{1,6},{2,5},{3,4},{4,3},{5,2},{6,1},{7,0},{8,15},{9,14},{10,... | collective-permute-start | bytes 1179656 | tf_op jit(solution)/shard_map/ppermute | solution.py:51
  43.1 12.2 %collective-permute-start.13 = (bf16[2,64,1536]{2,1,0:T(8,128)(2,1)S(1)}, bf16[2,64,1536]{2,1,0:T(8,128)(2,1)S(1)}, u32[]{:S(2)}, u32[]{:S(2)}) collective-permute-start(bf16[2,64,1536]{2,1,0:T(8,128)(2,1)S(1)} %copy-done.29), channel_id=1, source_target_pairs={{0,2},{1,3},{2,0},{3,1},{4,6},{5,7},{6,4},{7,5},{8,10},{9,11},{10,... | collective-permute-start | bytes 1179656 | tf_op jit(solution)/shard_map/ppermute | solution.py:51
  46.0 15.8 %collective-permute-start.15 = (bf16[2,64,1536]{2,1,0:T(8,128)(2,1)S(1)}, bf16[2,64,1536]{2,1,0:T(8,128)(2,1)S(1)}, u32[]{:S(2)}, u32[]{:S(2)}) collective-permute-start(bf16[2,64,1536]{2,1,0:T(8,128)(2,1)S(1)} %copy-done.28), channel_id=1, source_target_pairs={{0,5},{1,4},{2,7},{3,6},{4,1},{5,0},{6,3},{7,2},{8,13},{9,12},{10,... | collective-permute-start | bytes 1179656 | tf_op jit(solution)/shard_map/ppermute | solution.py:51
  62.6 3.8 %collective-permute-start.16 = (bf16[4,2,96,1120]{3,2,1,0:T(8,128)(2,1)S(1)}, bf16[4,2,96,1120]{3,2,1,0:T(8,128)(2,1)}, u32[]{:S(2)}, u32[]{:S(2)}) collective-permute-start(bf16[4,2,96,1120]{3,2,1,0:T(8,128)(2,1)S(1)} %pad_maximum_fusion.quad_ref), channel_id=1, source_target_pairs={{0,8},{8,0},{1,9},{9,1},{2,10},{10,2},{3,11},{11,3},{4,12},{12,4},... | collective-permute-start | bytes 5160968 | tf_op jit(solution)/shard_map/ppermute | solution.py:43
  66.7 21.8 %copy-start.15 = (bf16[1536,128]{1,0:T(8,128)(2,1)S(1)}, bf16[1536,128]{1,0:T(8,128)(2,1)}, u32[]{:S(2)}) copy-start(bf16[1536,128]{1,0:T(8,128)(2,1)} %copy-done.14) | copy-start | bytes 1179652
  66.7 21.8 %copy-start.17 = (bf16[1536,128]{1,0:T(8,128)(2,1)S(1)}, bf16[1536,128]{1,0:T(8,128)(2,1)}, u32[]{:S(2)}) copy-start(bf16[1536,128]{1,0:T(8,128)(2,1)} %copy-done.16) | copy-start | bytes 1179652
  66.7 21.8 %copy-start.19 = (bf16[1536,128]{1,0:T(8,128)(2,1)S(1)}, bf16[1536,128]{1,0:T(8,128)(2,1)}, u32[]{:S(2)}) copy-start(bf16[1536,128]{1,0:T(8,128)(2,1)} %copy-done.18) | copy-start | bytes 1179652
  85.5 11.7 %collective-permute-start.17 = (bf16[128,1120]{1,0:T(8,128)(2,1)S(1)}, bf16[128,1120]{1,0:T(8,128)(2,1)S(1)}, u32[]{:S(2)}, u32[]{:S(2)}) collective-permute-start(bf16[128,1120]{1,0:T(8,128)(2,1)S(1)} %get-tuple-element.135.refs_9_), channel_id=1, source_target_pairs={{0,1},{1,0},{2,3},{3,2},{4,5},{5,4},{6,7},{7,6},{8,9},{9,8},{10,11... | collective-permute-start | bytes 860168 | tf_op jit(solution)/shard_map/ppermute | solution.py:51
  86.5 10.7 %collective-permute-start.18 = (bf16[128,1120]{1,0:T(8,128)(2,1)S(1)}, bf16[128,1120]{1,0:T(8,128)(2,1)S(1)}, u32[]{:S(2)}, u32[]{:S(2)}) collective-permute-start(bf16[128,1120]{1,0:T(8,128)(2,1)S(1)} %get-tuple-element.138.refs_12_), channel_id=1, source_target_pairs={{0,4},{1,5},{2,6},{3,7},{4,0},{5,1},{6,2},{7,3},{8,12},{9,13},{10,... | collective-permute-start | bytes 860168 | tf_op jit(solution)/shard_map/ppermute | solution.py:51
  97.3 3.8 %collective-permute-start.19 = (bf16[784,1120]{1,0:T(8,128)(2,1)S(1)}, bf16[784,1120]{1,0:T(8,128)(2,1)S(1)}, u32[]{:S(2)}, u32[]{:S(2)}) collective-permute-start(bf16[784,1120]{1,0:T(8,128)(2,1)S(1)} %get-tuple-element.145), channel_id=1, source_target_pairs={{0,8},{8,0},{1,9},{9,1},{2,10},{10,2},{3,11},{11,3},{4,12},{12,4},... | collective-permute-start | bytes 5268488 | tf_op jit(solution)/shard_map/ppermute | solution.py:43
  101.4 18.8 %collective-permute-start.20 = (bf16[208,1120]{1,0:T(8,128)(2,1)S(1)}, bf16[208,1120]{1,0:T(8,128)(2,1)S(1)}, u32[]{:S(2)}, u32[]{:S(2)}) collective-permute-start(bf16[208,1120]{1,0:T(8,128)(2,1)S(1)} %get-tuple-element.149), channel_id=1, source_target_pairs={{0,16},{16,0},{32,48},{48,32},{1,17},{17,1},{33,49},{49,33},{2,18}... | collective-permute-start | bytes 1397768 | tf_op jit(solution)/shard_map/ppermute | solution.py:43
  103.4 24.9 %collective-permute-start.21 = (bf16[208,1120]{1,0:T(8,128)(2,1)S(1)}, bf16[208,1120]{1,0:T(8,128)(2,1)S(1)}, u32[]{:S(2)}, u32[]{:S(2)}) collective-permute-start(bf16[208,1120]{1,0:T(8,128)(2,1)S(1)} %get-tuple-element.150), channel_id=1, source_target_pairs={{0,32},{16,48},{32,0},{48,16},{1,33},{17,49},{33,1},{49,17},{2,34}... | collective-permute-start | bytes 1397768 | tf_op jit(solution)/shard_map/ppermute | solution.py:43
  107.0 23.9 %collective-permute-start.22 = (bf16[208,1120]{1,0:T(8,128)(2,1)S(1)}, bf16[208,1120]{1,0:T(8,128)(2,1)S(1)}, u32[]{:S(2)}, u32[]{:S(2)}) collective-permute-start(bf16[208,1120]{1,0:T(8,128)(2,1)S(1)} %get-tuple-element.151), channel_id=1, source_target_pairs={{0,48},{16,32},{32,16},{48,0},{1,49},{17,33},{33,17},{49,1},{2,50}... | collective-permute-start | bytes 1397768 | tf_op jit(solution)/shard_map/ppermute | solution.py:43
  107.0 9.4 %collective-permute-start.24 = (bf16[128,1120]{1,0:T(8,128)(2,1)S(1)}, bf16[128,1120]{1,0:T(8,128)(2,1)S(1)}, u32[]{:S(2)}, u32[]{:S(2)}) collective-permute-start(bf16[128,1120]{1,0:T(8,128)(2,1)S(1)} %get-tuple-element.159.refs_11_), channel_id=1, source_target_pairs={{0,3},{1,2},{2,1},{3,0},{4,7},{5,6},{6,5},{7,4},{8,11},{9,10},{10,... | collective-permute-start | bytes 860168 | tf_op jit(solution)/shard_map/ppermute | solution.py:51
  109.3 9.4 %collective-permute-start.25 = (bf16[128,1120]{1,0:T(8,128)(2,1)S(1)}, bf16[128,1120]{1,0:T(8,128)(2,1)S(1)}, u32[]{:S(2)}, u32[]{:S(2)}) collective-permute-start(bf16[128,1120]{1,0:T(8,128)(2,1)S(1)} %get-tuple-element.160.refs_14_), channel_id=1, source_target_pairs={{0,6},{1,7},{2,4},{3,5},{4,2},{5,3},{6,0},{7,1},{8,14},{9,15},{10,... | collective-permute-start | bytes 860168 | tf_op jit(solution)/shard_map/ppermute | solution.py:51
  118.7 15.4 %collective-permute-start.26 = (bf16[128,1120]{1,0:T(8,128)(2,1)S(1)}, bf16[128,1120]{1,0:T(8,128)(2,1)S(1)}, u32[]{:S(2)}, u32[]{:S(2)}) collective-permute-start(bf16[128,1120]{1,0:T(8,128)(2,1)S(1)} %get-tuple-element.163.refs_15_), channel_id=1, source_target_pairs={{0,7},{1,6},{2,5},{3,4},{4,3},{5,2},{6,1},{7,0},{8,15},{9,14},{10,... | collective-permute-start | bytes 860168 | tf_op jit(solution)/shard_map/ppermute | solution.py:51
  119.9 14.2 %collective-permute-start.27 = (bf16[128,1120]{1,0:T(8,128)(2,1)S(1)}, bf16[128,1120]{1,0:T(8,128)(2,1)S(1)}, u32[]{:S(2)}, u32[]{:S(2)}) collective-permute-start(bf16[128,1120]{1,0:T(8,128)(2,1)S(1)} %get-tuple-element.164.refs_10_), channel_id=1, source_target_pairs={{0,2},{1,3},{2,0},{3,1},{4,6},{5,7},{6,4},{7,5},{8,10},{9,11},{10,... | collective-permute-start | bytes 860168 | tf_op jit(solution)/shard_map/ppermute | solution.py:51
  120.2 15.5 %collective-permute-start.28 = (bf16[128,1120]{1,0:T(8,128)(2,1)S(1)}, bf16[128,1120]{1,0:T(8,128)(2,1)S(1)}, u32[]{:S(2)}, u32[]{:S(2)}) collective-permute-start(bf16[128,1120]{1,0:T(8,128)(2,1)S(1)} %get-tuple-element.165.refs_13_), channel_id=1, source_target_pairs={{0,5},{1,4},{2,7},{3,6},{4,1},{5,0},{6,3},{7,2},{8,13},{9,12},{10,... | collective-permute-start | bytes 860168 | tf_op jit(solution)/shard_map/ppermute | solution.py:51
  131.1 14.2 %collective-permute-start.23 = (bf16[112,1120]{1,0:T(8,128)(2,1)S(1)}, bf16[112,1120]{1,0:T(8,128)(2,1)S(1)}, u32[]{:S(2)}, u32[]{:S(2)}) collective-permute-start(bf16[112,1120]{1,0:T(8,128)(2,1)S(1)} %get-tuple-element.157), channel_id=1, source_target_pairs={{0,64},{64,0},{1,65},{65,1},{2,66},{66,2},{3,67},{67,3},{4,68},{68... | collective-permute-start | bytes 752648 | tf_op jit(solution)/shard_map/ppermute | solution.py:43
  (32 other events, 132.8 us)

commit v5 on v4

--- a/solution.py
+++ b/solution.py
@@ -106,111 +106,120 @@
     return value * lax.rsqrt(value * value + DELTA * DELTA)
 
 
-def pairs_kernel(
-    place_ref, quad_ref, other_ref, bias_ref, truth_ref, wt_ref, *refs
-):
-    pieces = refs[:8]
-    full_ref, bias_out_ref, *dfield_refs = refs[8:18]
-    normed_ref, field, sums = refs[18:]
-    for k in range(8):
-        normed_ref[pl.ds(128 * k, 128), :] = pieces[k][...]
-    width = full_ref.shape[1]
-    padded = field.shape[2]
+def fair_slopes(field, row, lane, true, scale, sums):
     count = 16
     coef = (1.0 - (1.0 - ALPHA) / count) / (count * (count - 1))
-    for core, ref in ((0, quad_ref), (1, other_ref)):
+    here = (pl.ds(row, 8), pl.ds(lane, 128))
+    values = [field[m, here[0], here[1]] for m in range(count)]
+    total = [None] * count
+    for m in range(count):
+        for k in range(m + 1, count):
+            s = slope(values[m] - values[k])
+            total[m] = s if total[m] is None else total[m] + s
+            total[k] = -s if total[k] is None else total[k] - s
+    column = None
+    for m in range(count):
+        value = scale * (slope(values[m] - true) * (1.0 / count) - coef * total[m])
+        value = value.astype(BF16).astype(F32)
+        field[m, here[0], here[1]] = value
+        column = value if column is None else column + value
+    sums[:, pl.ds(lane, 128)] += column
+
+
+def middle_kernel(place_ref, quad_ref, other_ref, bias_ref, truth_ref, wt_ref, gain_ref, *refs):
+    pieces, turned = refs[:8], refs[8:16]
+    full_ref, keep_ref, send_ref, small_ref = refs[16:20]
+    dfield_refs = refs[20:28]
+    normed, flipped, field0, field1, slopes0, slopes1, part, sums, rows = refs[28:]
+    fields, slopes = (field0, field1), (slopes0, slopes1)
+    features, width = full_ref.shape
+    count = 16
+    tiles = [(at, min(256, width - at)) for at in range(0, width, 256)]
+    core = place_ref[2]
+    for k in range(8):
+        normed[pl.ds(128 * k, 128), :] = pieces[k][...]
+        flipped[:, pl.ds(128 * k, 128)] = turned[k][...]
+    for c, ref in ((0, quad_ref), (1, other_ref)):
         for yh, step in [(yh, step) for yh in range(2) for step in range(4)]:
-            block = (
-                (place_ref[0] ^ yh) * 8 + (place_ref[1] ^ step) * 2 + (place_ref[2] ^ core)
-            )
+            block = (place_ref[0] ^ yh) * 8 + (place_ref[1] ^ step) * 2 + (core ^ c)
             full_ref[pl.ds(pl.multiple_of(block * 96, 96), 96), :] = ref[step, yh]
-
-    def project(step, carry):
-        row = pl.multiple_of(step * 256, 256)
-        part = jnp.dot(
-            normed_ref[pl.ds(row, 256), :], full_ref[...], preferred_element_type=F32
-        ) + bias_ref[...]
-        part = part.astype(BF16).astype(F32).reshape(4, 64, width)
-        field[pl.ds(step * 4, 4), :, 0:width] = part
-        return carry
-
-    lax.fori_loop(0, 4, project, 0)
+    rows[...] = jnp.zeros_like(rows)
     sums[...] = jnp.zeros_like(sums)
-    tiles = padded // 128
-
-    def pairs(step, carry):
-        row = pl.multiple_of((step // tiles) * 8, 8)
-        lane = pl.multiple_of((step % tiles) * 128, 128)
-        here = (pl.ds(row, 8), pl.ds(lane, 128))
-        values = [field[m, here[0], here[1]] for m in range(count)]
-        total = [None] * count
-        for m in range(count):
-            for k in range(m + 1, count):
-                s = slope(values[m] - values[k])
-                total[m] = s if total[m] is None else total[m] + s
-                total[k] = -s if total[k] is None else total[k] - s
-        true = truth_ref[here[0], here[1]]
-        scale = wt_ref[0:1, pl.ds(lane, 128)]
-        column = None
-        for m in range(count):
-            value = scale * (slope(values[m] - true) * (1.0 / count) - coef * total[m])
-            value = value.astype(BF16).astype(F32)
-            field[m, here[0], here[1]] = value
-            column = value if column is None else column + value
-        sums[:, pl.ds(lane, 128)] += column
-        return carry
-
-    lax.fori_loop(0, 8 * tiles, pairs, 0)
-    bias_out_ref[...] = jnp.sum(sums[...], axis=0, keepdims=True)
-
-    for k in range(8):
-        for m in range(2):
-            dfield_refs[k][64 * m : 64 * m + 64, :] = field[2 * k + m, :, 0:width].astype(BF16)
-
-
-def grad_kernel(place_ref, full_ref, bias_part_ref, gain_ref, *refs):
-    pieces, fields = refs[:8], refs[8:16]
-    keep_ref, send_ref, small_ref, flipped_ref, dfield_ref, grad, rows = refs[16:]
-    for k in range(8):
-        flipped_ref[:, pl.ds(128 * k, 128)] = pieces[k][...]
-        dfield_ref[pl.ds(128 * k, 128), :] = fields[k][...]
-    width = full_ref.shape[1]
-    features = full_ref.shape[0]
-
-    def weight_grad(step, carry):
-        row = pl.multiple_of(step * 512, 512)
-        grad[pl.ds(row, 512), :] = jnp.dot(
-            flipped_ref[pl.ds(row, 512), :], dfield_ref[...], preferred_element_type=F32
+    send_ref[0:16, :] = jnp.zeros((16, width), BF16)
+
+    def project(tile, step):
+        at, wide = tiles[tile]
+        row = pl.multiple_of(step * 1024, 256)
+        out = jnp.dot(
+            normed[pl.ds(row, 1024), :], full_ref[:, at : at + wide],
+            preferred_element_type=F32,
+        ) + bias_ref[:, at : at + wide]
+        out = out.astype(BF16).astype(F32).reshape(16, 64, wide)
+        fields[tile % 2][pl.ds(step * 16, 16), :, 0:wide] = out
+
+    def pairs(tile, step):
+        at, wide = tiles[tile]
+        field, out = fields[tile % 2], slopes[tile % 2]
+        row = pl.multiple_of(step * 64, 16)
+        for lane in range(0, wide, 128):
+            scale = wt_ref[0:1, at + lane : at + lane + 128]
+            for half in range(0, 64, 8):
+                start = pl.multiple_of(row + half, 8)
+                true = truth_ref[pl.ds(start, 8), at + lane : at + lane + 128]
+                fair_slopes(field, start, lane, true, scale, sums.at[:, at : at + 256])
+            for m in range(count):
+                out[pl.ds(pl.multiple_of(64 * m + row, 16), 64), lane : lane + 128] = field[
+                    m, pl.ds(row, 64), lane : lane + 128
+                ].astype(BF16)
+
+    def weight_grad(tile, step):
+        at, wide = tiles[tile]
+        row = pl.multiple_of(step * 1536, 384)
+        out = jnp.dot(
+            flipped[pl.ds(row, 1536), :], slopes[tile % 2][:, 0:wide],
+            preferred_element_type=F32,
         )
-        return carry
-
-    lax.fori_loop(0, features // 512, weight_grad, 0)
-
-    def gain_part(step, carry):
-        row = pl.multiple_of(step * 128, 128)
-        part = jnp.sum(
-            grad[pl.ds(row, 128), :] * full_ref[pl.ds(row, 128), :].astype(F32),
-            axis=1, keepdims=True,
+        part[:, 0:wide] = out
+        here = out * full_ref[pl.ds(row, 1536), at : at + wide].astype(F32)
+        for lane in range(0, wide, 128):
+            stop = min(lane + 128, wide)
+            rows[pl.ds(row, 1536), 0 : stop - lane] += here[:, lane:stop]
+        for q in range(8):
+            mine = part[pl.ds(pl.multiple_of(192 * q + core * 96, 96), 96), 0:wide]
+            other = part[pl.ds(pl.multiple_of(192 * q + (core ^ 1) * 96, 96), 96), 0:wide]
+            keep_ref[8 * step + q, :, at : at + wide] = mine
+            start = pl.multiple_of(16 + 96 * (8 * step + q), 16)
+            send_ref[pl.ds(start, 96), at : at + wide] = other.astype(BF16)
+
+    for phase in range(len(tiles) + 2):
+
+        def body(step, carry, phase=phase):
+            if phase - 2 >= 0:
+                weight_grad(phase - 2, step)
+            if phase < len(tiles):
+                project(phase, step)
+            if 0 <= phase - 1 < len(tiles):
+                pairs(phase - 1, step)
+            return carry
+
+        lax.fori_loop(0, 1, body, 0)
+        if 0 <= phase - 1 < len(tiles):
+            at, wide = tiles[phase - 1]
+            for k in range(8):
+                dfield_refs[k][:, at : at + wide] = slopes[(phase - 1) % 2][
+                    128 * k : 128 * k + 128, 0:wide
+                ]
+    small_ref[...] = jnp.zeros_like(small_ref)
+    bias_sums = jnp.sum(sums[...], axis=0, keepdims=True)
+    for n in range(3):
+        turned_rows = jnp.concatenate(
+            [rows[512 * n + 128 * q : 512 * n + 128 * q + 128, :].T for q in range(4)], axis=1
         )
-        rows[:, pl.ds(row, 128)] = jnp.broadcast_to(part, (128, 128)).T[0:8]
-        return carry
-
-    lax.fori_loop(0, features // 128, gain_part, 0)
-    small_ref[...] = jnp.zeros_like(small_ref)
-    for n in range(3):
-        cut = slice(512 * n, 512 * (n + 1))
-        small_ref[n : n + 1, :] = rows[0:1, cut] / gain_ref[:, cut]
+        gain_sums = jnp.sum(turned_rows, axis=0, keepdims=True)
+        small_ref[n : n + 1, :] = gain_sums / gain_ref[:, 512 * n : 512 * n + 512]
         stop = min(512 * (n + 1), width)
-        small_ref[3 + n : 4 + n, 0 : stop - 512 * n] = bias_part_ref[:, 512 * n : stop]
+        small_ref[3 + n : 4 + n, 0 : stop - 512 * n] = bias_sums[:, 512 * n : stop]
     put_small(send_ref, small_ref[...])
-    for yh in range(2):
-        for step in range(4):
-            base = (place_ref[0] ^ yh) * 8 + (place_ref[1] ^ step) * 2
-            mine = pl.multiple_of((base + place_ref[2]) * 96, 96)
-            other = pl.multiple_of((base + (place_ref[2] ^ 1)) * 96, 96)
-            keep_ref[yh, step] = grad[pl.ds(mine, 96), :]
-            start = 16 + 96 * (yh * 4 + step)
-            send_ref[start : start + 96, :] = grad[pl.ds(other, 96), :].astype(BF16)
 
 
 def backward_kernel(order, before, place_ref, tokens_ref, gain_ref, full_ref, *refs):
@@ -284,13 +293,14 @@
     return rows[0:8] + rows[8:16]
 
 
-def core_kernel(keep_ref, small_ref, came_ref, own_ref, small_out_ref, *sends):
+def core_kernel(place_ref, keep_ref, small_ref, came_ref, own_ref, small_out_ref, *sends):
     small = small_ref[...] + get_small(came_ref)
     small_out_ref[...] = small
     for step in range(4):
         for yh in range(2):
-            start = 16 + 96 * (yh * 4 + step)
-            block = keep_ref[yh, step] + came_ref[start : start + 96, :].astype(F32)
+            n = (place_ref[0] ^ yh) * 4 + (place_ref[1] ^ step)
+            start = pl.multiple_of(16 + 96 * n, 16)
+            block = keep_ref[n] + came_ref[pl.ds(start, 96), :].astype(F32)
             if step == 0:
                 own_ref[96 * yh : 96 * yh + 96, :] = block
             else:
@@ -340,6 +350,37 @@
     share_ref[...] = total[0:12]
     for n in range(24):
         small_ref[n : n + 1, :] = small[n // 4 : n // 4 + 1, 128 * (n % 4) : 128 * (n % 4 + 1)]
+
+
+def middle(*operands):
+    features, outs = 1536, operands[3].shape[1]
+    padded = operands[4].shape[1]
+    return pl.pallas_call(
+        middle_kernel,
+        out_shape=(
+            jax.ShapeDtypeStruct((features, outs), BF16),
+            jax.ShapeDtypeStruct((8, 96, outs), F32),
+            jax.ShapeDtypeStruct((16 + 768, outs), BF16),
+            jax.ShapeDtypeStruct((8, 512), F32),
+        )
+        + (jax.ShapeDtypeStruct((128, outs), BF16),) * 8,
+        in_specs=[pl.BlockSpec(memory_space=pltpu.SMEM)] + vmem(len(operands) - 1),
+        out_specs=tuple(vmem(12)),
+        scratch_shapes=[
+            pltpu.VMEM((1024, features), BF16),
+            pltpu.VMEM((features, 1024), BF16),
+            pltpu.VMEM((16, 64, 256), F32),
+            pltpu.VMEM((16, 64, 256), F32),
+            pltpu.VMEM((1024, 256), BF16),
+            pltpu.VMEM((1024, 256), BF16),
+            pltpu.VMEM((1536, 256), F32),
+            pltpu.VMEM((8, padded + 128), F32),
+            pltpu.VMEM((features, 128), F32),
+        ],
+        compiler_params=params(28),
+        cost_estimate=cost(20000000000, 80000000),
+        name="middle",
+    )(*operands)
 
 
 def on_device(tokens, gain, weight, bias, target, channel_weight):
@@ -407,50 +448,14 @@
     for k in (7, 2, 5):
         normed[k] = norm_piece(arrived[k], gain_row)
 
-    full, bias_part, *dfield = pl.pallas_call(
-        pairs_kernel,
-        out_shape=(
-            jax.ShapeDtypeStruct((features, outs), BF16),
-            jax.ShapeDtypeStruct((1, padded), F32),
-        )
-        + (jax.ShapeDtypeStruct((128, outs), BF16),) * 8,
-        in_specs=[smem] + vmem(13),
-        out_specs=tuple(vmem(10)),
-        scratch_shapes=[
-            pltpu.VMEM((1024, features), BF16),
-            pltpu.VMEM((16, 64, padded), F32),
-            pltpu.VMEM((8, padded), F32),
-        ],
-        compiler_params=params(32),
-        cost_estimate=cost(20000000000, 80000000),
-        name="pairs",
-    )(place, quad, other, bias.reshape(1, outs), truth, wt, *[normed[k][0] for k in range(8)])
+    full, keep, send, small, *dfield = middle(
+        place, quad, other, bias.reshape(1, outs), truth, wt, gain_row,
+        *[normed[k][0] for k in range(8)], *[normed[k][1] for k in range(8)],
+    )
 
     returned = {0: dfield[0]}
     for k in (1, 4):
         returned[k] = swap_member(dfield[k], k)
-    keep, send, small = pl.pallas_call(
-        grad_kernel,
-        out_shape=(
-            jax.ShapeDtypeStruct((2, 4, 96, outs), F32),
-            jax.ShapeDtypeStruct((16 + 768, outs), BF16),
-            jax.ShapeDtypeStruct((8, 512), F32),
-        ),
-        in_specs=[smem] + vmem(19),
-        out_specs=tuple(vmem(3)),
-        scratch_shapes=[
-            pltpu.VMEM((features, 1024), BF16),
-            pltpu.VMEM((1024, outs), BF16),
-            pltpu.VMEM((features, outs), F32),
-            pltpu.VMEM((8, features), F32),
-        ],
-        compiler_params=params(34),
-        cost_estimate=cost(12000000000, 45000000),
-        name="weight_gradient",
-    )(
-        place, full, bias_part, gain_row,
-        *[normed[k][1] for k in range(8)], *dfield,
-    )
 
     def backward(order, *before):
         count = len(order)
@@ -488,11 +493,8 @@
             name=name,
         )(*operands)
 
-    (send,), done = after((send,), *[returned[k] for k in (1, 4)])
-    for k, piece in zip((1, 4), done):
-        returned[k] = piece
     came = swap(send, "core", 1)
-    own, small, *sends = combine(core_kernel, "core_sums", 192, 208, 3, keep, small, came)
+    own, small, *sends = combine(core_kernel, "core_sums", 192, 208, 3, place, keep, small, came)
     came = [swap(value, "z", k) for k, value in zip((1, 2, 3), sends)]
     (d3, d6), (small,) = after((dfield[3], dfield[6]), small)
     returned[3], returned[6] = swap_member(d3, 3), swap_member(d6, 6)

time: 159 us -> 151 us (0.950)
  Pallas kernels: 48.8 us -> 42 us
  waiting for transfers between devices: 34.5 us -> 29.4 us
  blocking collectives: 11.5 us -> 13.6 us
    pallas_call x2 -> x1, Pallas kernels: 27.5 us -> 20.1 us  [middle(): pl.pallas_call(middle_kernel, out_shape=(jax.ShapeDtypeStruct((features,...]
    ppermute x14, waiting for transfers between devices: 13.6 us -> 9.83 us  [swap_member(): return lax.ppermute(value, MEMBER, [(i, i ^ step) for i in range(8)])]
    all_to_all x1, blocking collectives: 11.5 us -> 13.6 us  [on_device(): came = lax.all_to_all(send, MEMBER, 0, 0)]
  transfers between devices with their start and end apart: 29 -> 29, of which waited for: 13 -> 13; matrix products, arithmetic and copies ran while one was open for 4% -> 4% of each run, Pallas kernels for 18% -> 14%
where the time goes in v5:
time: 151 us; the launch traced here: 150 us
  starting transfers between devices  48.3 us (32%)
  Pallas kernels  42 us (28%)
  waiting for transfers between devices  29.4 us (19%)
  local copies, waits for them, and re-layouts  14.7 us (10%)
  blocking collectives  13.6 us (9%)
    ppermute x14, starting transfers between devices, swap_member(): return lax.ppermute(value, MEMBER, [(i, i ^ step) for i in range(8)])  25.8 us
    pallas_call x1, Pallas kernels, middle(): pl.pallas_call(middle_kernel, out_shape=(jax.ShapeDtypeStruct((features,...  20.1 us
    ppermute x12, waiting for transfers between devices, swap(): return lax.ppermute(value, axis, [(i, i ^ step) for i in range(SIZE[axis])])  19.5 us
    ppermute x12, starting transfers between devices, swap(): return lax.ppermute(value, axis, [(i, i ^ step) for i in range(SIZE[axis])])  17.9 us
    pallas_call x2, Pallas kernels, backward(): pl.pallas_call(functools.partial(backward_kernel, order, [done for done,...  15 us
    all_to_all x1, blocking collectives, on_device(): came = lax.all_to_all(send, MEMBER, 0, 0)  13.6 us
    ppermute x14, waiting for transfers between devices, swap_member(): return lax.ppermute(value, MEMBER, [(i, i ^ step) for i in range(8)])  9.83 us
    unnamed x70, local copies, waits for them, and re-layouts  8.84 us
  transfers between devices with their start and end apart: 29, of which 13 were waited for; matrix products, arithmetic and copies ran while one was open for 4% of the time, Pallas kernels for 14%

profile of v5, /device:TPU:0, one launch (start us, length us, event | category | flops | bytes accessed | tf_op | source)
XLA Modules:
  0.0 150.3 jit_solution(7047280656495004551)
XLA Ops:
  0.6 1.7 %collective-permute-start = (bf16[12,1120]{1,0:T(8,128)(2,1)}, bf16[12,1120]{1,0:T(8,128)(2,1)S(1)}, u32[]{:S(2)}, u32[]{:S(2)}) collective-permute-start(bf16[12,1120]{1,0:T(8,128)(2,1)} %param.9), channel_id=1, source_target_pairs={{0,1},{1,0},{64,65},{65,64},{2,3},{3,2},{66,67},{67,66},{4,5},{5,4... | collective-permute-start | bytes 80648 | tf_op jit(solution)/shard_map/ppermute | solution.py:47
  2.4 2.2 %collective-permute-start.2 = (bf16[12,1120]{1,0:T(8,128)(2,1)}, bf16[12,1120]{1,0:T(8,128)(2,1)S(1)}, u32[]{:S(2)}, u32[]{:S(2)}) collective-permute-start(bf16[12,1120]{1,0:T(8,128)(2,1)} %param.9), channel_id=1, source_target_pairs={{0,65},{1,64},{64,1},{65,0},{2,67},{3,66},{66,3},{67,2},{4,69},{5,... | collective-permute-start | bytes 80648 | tf_op jit(solution)/shard_map/ppermute | solution.py:47
  5.3 3.1 %constant_dynamic-slice_fusion = (bf16[2,1,64,1536]{3,2,1,0:T(8,128)(2,1)S(1)}, bf16[2,64,1536]{2,1,0:T(8,128)(2,1)}, bf16[2,64,1536]{2,1,0:T(8,128)(2,1)}, bf16...) fusion(bf16[2,8,64,1536]{3,2,1,0:T(8,128)(2,1)} %bitcast.54, ...), kind=kLoop, calls=%fused_computation.20 | loop fusion | bytes 6291488 | tf_op jit(solution)/shard_map/jit(dynamic_index_in_dim)/dynamic_slice | solution.py:401
  8.4 3.0 %collective-permute-start.6 = (bf16[2,64,1536]{2,1,0:T(8,128)(2,1)S(1)}, bf16[2,64,1536]{2,1,0:T(8,128)(2,1)S(1)}, u32[]{:S(2)}, u32[]{:S(2)}) collective-permute-start(bf16[2,64,1536]{2,1,0:T(8,128)(2,1)S(1)} %get-tuple-element.168), channel_id=1, source_target_pairs={{0,4},{1,5},{2,6},{3,7},{4,0},{5,1},{6,2},{7,3},{8,12},{9,13},{10,... | collective-permute-start | bytes 1179656 | tf_op jit(solution)/shard_map/ppermute | solution.py:51
  11.7 1.3 truth.1.truth_ref
  16.2 1.2 collective-permute-start.5
  17.4 1.5 %collective-permute-start.4 = (bf16[4,12,1120]{2,1,0:T(8,128)(2,1)S(1)}, bf16[4,12,1120]{2,1,0:T(8,128)(2,1)S(1)}, u32[]{:S(2)}, u32[]{:S(2)}) collective-permute-start(bf16[4,12,1120]{2,1,0:T(8,128)(2,1)S(1)} %pad_maximum_fusion.3), channel_id=1, source_target_pairs={{0,4},{2,6},{4,0},{6,2},{1,5},{3,7},{5,1},{7,3},{8,12},{10,14},{12... | collective-permute-start | bytes 322568 | tf_op jit(solution)/shard_map/ppermute | solution.py:43
  18.9 1.4 collective-permute-start.3
  20.4 1.3 collective-permute-start.10
  21.6 4.9 %collective-permute-done.5 = bf16[4,12,1120]{2,1,0:T(8,128)(2,1)S(1)} collective-permute-done((bf16[4,12,1120]{2,1,0:T(8,128)(2,1)S(1)}, bf16[4,12,1120]{2,1,0:T(8,128)(2,1)S(1)}, u32[]{:S(2)}, u32[]{:S(2)}) %collective-permute-start.5) | collective-permute-done | bytes 107552 | tf_op jit(solution)/shard_map/ppermute | solution.py:43
  27.6 2.7 %collective-permute-start.11 = (bf16[2,64,1536]{2,1,0:T(8,128)(2,1)}, bf16[2,64,1536]{2,1,0:T(8,128)(2,1)S(1)}, u32[]{:S(2)}, u32[]{:S(2)}) collective-permute-start(bf16[2,64,1536]{2,1,0:T(8,128)(2,1)} %get-tuple-element.87), channel_id=1, source_target_pairs={{0,6},{1,7},{2,4},{3,5},{4,2},{5,3},{6,0},{7,1},{8,14},{9,15},{10,... | collective-permute-start | bytes 1179656 | tf_op jit(solution)/shard_map/ppermute | solution.py:51
  31.0 4.0 %collective-permute-start.8 = (bf16[2,96,1120]{2,1,0:T(8,128)(2,1)S(1)}, bf16[2,96,1120]{2,1,0:T(8,128)(2,1)S(1)}, u32[]{:S(2)}, u32[]{:S(2)}) collective-permute-start(bf16[2,96,1120]{2,1,0:T(8,128)(2,1)S(1)} %get-tuple-element.175), channel_id=1, source_target_pairs={{0,32},{16,48},{32,0},{48,16},{1,33},{17,49},{33,1},{49,17},{2,34}... | collective-permute-start | bytes 1290248 | tf_op jit(solution)/shard_map/ppermute | solution.py:43
  37.2 2.9 %collective-permute-done.11 = bf16[2,64,1536]{2,1,0:T(8,128)(2,1)S(1)} collective-permute-done((bf16[2,64,1536]{2,1,0:T(8,128)(2,1)}, bf16[2,64,1536]{2,1,0:T(8,128)(2,1)S(1)}, u32[]{:S(2)}, u32[]{:S(2)}) %collective-permute-start.11) | collective-permute-done | bytes 393248 | tf_op jit(solution)/shard_map/ppermute | solution.py:51
  40.0 3.1 %collective-permute-start.12 = (bf16[2,64,1536]{2,1,0:T(8,128)(2,1)S(1)}, bf16[2,64,1536]{2,1,0:T(8,128)(2,1)S(1)}, u32[]{:S(2)}, u32[]{:S(2)}) collective-permute-start(bf16[2,64,1536]{2,1,0:T(8,128)(2,1)S(1)} %copy-done.30), channel_id=1, source_target_pairs={{0,7},{1,6},{2,5},{3,4},{4,3},{5,2},{6,1},{7,0},{8,15},{9,14},{10,... | collective-permute-start | bytes 1179656 | tf_op jit(solution)/shard_map/ppermute | solution.py:51
  46.0 2.4 %collective-permute-start.15 = (bf16[2,64,1536]{2,1,0:T(8,128)(2,1)S(1)}, bf16[2,64,1536]{2,1,0:T(8,128)(2,1)S(1)}, u32[]{:S(2)}, u32[]{:S(2)}) collective-permute-start(bf16[2,64,1536]{2,1,0:T(8,128)(2,1)S(1)} %copy-done.28), channel_id=1, source_target_pairs={{0,5},{1,4},{2,7},{3,6},{4,1},{5,0},{6,3},{7,2},{8,13},{9,12},{10,... | collective-permute-start | bytes 1179656 | tf_op jit(solution)/shard_map/ppermute | solution.py:51
  50.4 4.5 %collective-permute-done.7 = bf16[2,96,1120]{2,1,0:T(8,128)(2,1)S(1)} collective-permute-done((bf16[2,96,1120]{2,1,0:T(8,128)(2,1)S(1)}, bf16[2,96,1120]{2,1,0:T(8,128)(2,1)S(1)}, u32[]{:S(2)}, u32[]{:S(2)}) %collective-permute-start.7) | collective-permute-done | bytes 430112 | tf_op jit(solution)/shard_map/ppermute | solution.py:43
  56.0 5.8 %collective-permute-done.15 = bf16[2,64,1536]{2,1,0:T(8,128)(2,1)S(1)} collective-permute-done((bf16[2,64,1536]{2,1,0:T(8,128)(2,1)S(1)}, bf16[2,64,1536]{2,1,0:T(8,128)(2,1)S(1)}, u32[]{:S(2)}, u32[]{:S(2)}) %collective-permute-start.15) | collective-permute-done | bytes 393248 | tf_op jit(solution)/shard_map/ppermute | solution.py:51
  67.3 20.1 %middle.1 = (bf16[1536,1120]{1,0:T(8,128)(2,1)S(1)}, f32[8,96,1120]{2,1,0:T(8,128)S(1)}, bf16[784,1120]{1,0:T(8,128)(2,1)S(1)}, f32[8,512]{1,0:T(8,128)S(1)}, bf...) custom-call(s32[6]{0:T(128)S(1)} %stack.81.place_ref, ...), custom_call_target="tpu_custom_call" | custom-call | flops 20000000000 | bytes 80000000 | tf_op jit(solution)/shard_map/middle/pallas_call | solution.py:358
  88.8 2.0 %collective-permute-start.22 = (bf16[128,1120]{1,0:T(8,128)(2,1)S(1)}, bf16[128,1120]{1,0:T(8,128)(2,1)S(1)}, u32[]{:S(2)}, u32[]{:S(2)}) collective-permute-start(bf16[128,1120]{1,0:T(8,128)(2,1)S(1)} %get-tuple-element.142), channel_id=1, source_target_pairs={{0,4},{1,5},{2,6},{3,7},{4,0},{5,1},{6,2},{7,3},{8,12},{9,13},{10,... | collective-permute-start | bytes 860168 | tf_op jit(solution)/shard_map/ppermute | solution.py:51
  92.2 2.0 %collective-permute-start.18 = (bf16[208,1120]{1,0:T(8,128)(2,1)S(1)}, bf16[208,1120]{1,0:T(8,128)(2,1)S(1)}, u32[]{:S(2)}, u32[]{:S(2)}) collective-permute-start(bf16[208,1120]{1,0:T(8,128)(2,1)S(1)} %get-tuple-element.136), channel_id=1, source_target_pairs={{0,16},{16,0},{32,48},{48,32},{1,17},{17,1},{33,49},{49,33},{2,18}... | collective-permute-start | bytes 1397768 | tf_op jit(solution)/shard_map/ppermute | solution.py:43
  94.2 3.6 %collective-permute-start.19 = (bf16[208,1120]{1,0:T(8,128)(2,1)S(1)}, bf16[208,1120]{1,0:T(8,128)(2,1)S(1)}, u32[]{:S(2)}, u32[]{:S(2)}) collective-permute-start(bf16[208,1120]{1,0:T(8,128)(2,1)S(1)} %get-tuple-element.137), channel_id=1, source_target_pairs={{0,32},{16,48},{32,0},{48,16},{1,33},{17,49},{33,1},{49,17},{2,34}... | collective-permute-start | bytes 1397768 | tf_op jit(solution)/shard_map/ppermute | solution.py:43
  97.8 1.8 %collective-permute-start.24 = (bf16[128,1120]{1,0:T(8,128)(2,1)S(1)}, bf16[128,1120]{1,0:T(8,128)(2,1)S(1)}, u32[]{:S(2)}, u32[]{:S(2)}) collective-permute-start(bf16[128,1120]{1,0:T(8,128)(2,1)S(1)} %get-tuple-element.151), channel_id=1, source_target_pairs={{0,3},{1,2},{2,1},{3,0},{4,7},{5,6},{6,5},{7,4},{8,11},{9,10},{10,... | collective-permute-start | bytes 860168 | tf_op jit(solution)/shard_map/ppermute | solution.py:51
  99.7 2.3 %collective-permute-start.25 = (bf16[128,1120]{1,0:T(8,128)(2,1)S(1)}, bf16[128,1120]{1,0:T(8,128)(2,1)S(1)}, u32[]{:S(2)}, u32[]{:S(2)}) collective-permute-start(bf16[128,1120]{1,0:T(8,128)(2,1)S(1)} %get-tuple-element.152), channel_id=1, source_target_pairs={{0,6},{1,7},{2,4},{3,5},{4,2},{5,3},{6,0},{7,1},{8,14},{9,15},{10,... | collective-permute-start | bytes 860168 | tf_op jit(solution)/shard_map/ppermute | solution.py:51
  102.0 5.4 %backward.2.refs_0_ = bf16[3,2,64,1536]{3,2,1,0:T(8,128)(2,1)S(1)} custom-call(s32[6]{0:T(128)S(1)} %stack.81.place_ref, bf16[2,8,64,1536]{3,2,1,0:T(8,128)(2,1)S(1)} %bitcast.55, f32[1,1536]{1,0:T(1,128)S(1)} %reshape.152.gain_ref, bf16[1536,1120]{1,0:T(8,128)(2,1)S(1)} %get-tuple-element.139.full_ref, bf16[128,1120]{1,0:T(8,128)(2,1)S(1)} %get-tuple-element.140.refs_0_, ...), custom_call_target="tpu_custom_call" | custom-call | flops 1000 | bytes 1000 | tf_op jit(solution)/shard_map/backward/pallas_call | solution.py:463
  107.5 1.0 collective-permute-done.25.refs_2_
  108.5 3.1 %collective-permute-start.26 = (bf16[128,1120]{1,0:T(8,128)(2,1)S(1)}, bf16[128,1120]{1,0:T(8,128)(2,1)S(1)}, u32[]{:S(2)}, u32[]{:S(2)}) collective-permute-start(bf16[128,1120]{1,0:T(8,128)(2,1)S(1)} %get-tuple-element.155), channel_id=1, source_target_pairs={{0,7},{1,6},{2,5},{3,4},{4,3},{5,2},{6,1},{7,0},{8,15},{9,14},{10,... | collective-permute-start | bytes 860168 | tf_op jit(solution)/shard_map/ppermute | solution.py:51
  111.6 2.5 %collective-permute-start.28 = (bf16[128,1120]{1,0:T(8,128)(2,1)S(1)}, bf16[128,1120]{1,0:T(8,128)(2,1)S(1)}, u32[]{:S(2)}, u32[]{:S(2)}) collective-permute-start(bf16[128,1120]{1,0:T(8,128)(2,1)S(1)} %get-tuple-element.157), channel_id=1, source_target_pairs={{0,5},{1,4},{2,7},{3,6},{4,1},{5,0},{6,3},{7,2},{8,13},{9,12},{10,... | collective-permute-start | bytes 860168 | tf_op jit(solution)/shard_map/ppermute | solution.py:51
  114.1 5.3 %collective-permute-done.19.b_ref = bf16[208,1120]{1,0:T(8,128)(2,1)S(1)} collective-permute-done((bf16[208,1120]{1,0:T(8,128)(2,1)S(1)}, bf16[208,1120]{1,0:T(8,128)(2,1)S(1)}, u32[]{:S(2)}, u32[]{:S(2)}) %collective-permute-start.19) | collective-permute-done | bytes 465952 | tf_op jit(solution)/shard_map/ppermute | solution.py:43
  119.4 2.6 %collective-permute-done.20.c_ref = bf16[208,1120]{1,0:T(8,128)(2,1)S(1)} collective-permute-done((bf16[208,1120]{1,0:T(8,128)(2,1)S(1)}, bf16[208,1120]{1,0:T(8,128)(2,1)S(1)}, u32[]{:S(2)}, u32[]{:S(2)}) %collective-permute-start.20) | collective-permute-done | bytes 465952 | tf_op jit(solution)/shard_map/ppermute | solution.py:43
  122.2 2.6 %collective-permute-start.23 = (bf16[112,1120]{1,0:T(8,128)(2,1)S(1)}, bf16[112,1120]{1,0:T(8,128)(2,1)S(1)}, u32[]{:S(2)}, u32[]{:S(2)}) collective-permute-start(bf16[112,1120]{1,0:T(8,128)(2,1)S(1)} %get-tuple-element.146), channel_id=1, source_target_pairs={{0,64},{64,0},{1,65},{65,1},{2,66},{66,2},{3,67},{67,3},{4,68},{68... | collective-permute-start | bytes 752648 | tf_op jit(solution)/shard_map/ppermute | solution.py:43
  124.9 9.6 %backward.3 = bf16[2,8,64,1536]{3,2,1,0:T(8,128)(2,1)} custom-call(s32[6]{0:T(128)S(1)} %stack.81.place_ref, bf16[2,8,64,1536]{3,2,1,0:T(8,128)(2,1)S(1)} %bitcast.56, f32[1,1536]{1,0:T(1,128)S(1)} %reshape.152.gain_ref, bf16[1536,1120]{1,0:T(8,128)(2,1)S(1)} %get-tuple-element.139.full_ref, bf16[3,2,64,1536]{3,2,1,0:T(8,128)(2,1)S(1)} %backward.2.refs_0_, ...), custom_call_target="tpu_custom_call" | custom-call | flops 1000 | bytes 1000 | tf_op jit(solution)/shard_map/backward/pallas_call | solution.py:463
  134.8 13.6 %all_to_all.5.came_ref = bf16[8,32,1120]{2,1,0:T(8,128)(2,1)S(1)} all-to-all(bf16[8,32,1120]{2,1,0:T(8,128)(2,1)S(1)} %yh_sums.1), channel_id=1, replica_groups=mesh['yh'=2,'z'=4,'core'=2,'x'=4,'yl'=2] {'x','yl'}, dimensions={0} | all-to-all | bytes 1146880 | tf_op jit(solution)/shard_map/all_to_all | solution.py:522
  (136 shorter events, 24.5 us)
Async XLA Ops:
  0.6 10.8 %copy-start = (bf16[70,8,1024]{2,1,0:T(8,128)(2,1)S(1)}, bf16[70,8,1024]{2,1,0:T(8,128)(2,1)}, u32[]{:S(2)}) copy-start(bf16[70,8,1024]{2,1,0:T(8,128)(2,1)} %param.11) | copy-start | bytes 3440644
  0.6 15.4 %collective-permute-start = (bf16[12,1120]{1,0:T(8,128)(2,1)}, bf16[12,1120]{1,0:T(8,128)(2,1)S(1)}, u32[]{:S(2)}, u32[]{:S(2)}) collective-permute-start(bf16[12,1120]{1,0:T(8,128)(2,1)} %param.9), channel_id=1, source_target_pairs={{0,1},{1,0},{64,65},{65,64},{2,3},{3,2},{66,67},{67,66},{4,5},{5,4... | collective-permute-start | bytes 80648 | tf_op jit(solution)/shard_map/ppermute | solution.py:47
  2.4 13.7 %collective-permute-start.2 = (bf16[12,1120]{1,0:T(8,128)(2,1)}, bf16[12,1120]{1,0:T(8,128)(2,1)S(1)}, u32[]{:S(2)}, u32[]{:S(2)}) collective-permute-start(bf16[12,1120]{1,0:T(8,128)(2,1)} %param.9), channel_id=1, source_target_pairs={{0,65},{1,64},{64,1},{65,0},{2,67},{3,66},{66,3},{67,2},{4,69},{5,... | collective-permute-start | bytes 80648 | tf_op jit(solution)/shard_map/ppermute | solution.py:47
  4.6 11.5 %collective-permute-start.1 = (bf16[12,1120]{1,0:T(8,128)(2,1)}, bf16[12,1120]{1,0:T(8,128)(2,1)S(1)}, u32[]{:S(2)}, u32[]{:S(2)}) collective-permute-start(bf16[12,1120]{1,0:T(8,128)(2,1)} %param.9), channel_id=1, source_target_pairs={{0,64},{1,65},{64,0},{65,1},{2,66},{3,67},{66,2},{67,3},{4,68},{5,... | collective-permute-start | bytes 80648 | tf_op jit(solution)/shard_map/ppermute | solution.py:47
  8.4 18.4 %collective-permute-start.6 = (bf16[2,64,1536]{2,1,0:T(8,128)(2,1)S(1)}, bf16[2,64,1536]{2,1,0:T(8,128)(2,1)S(1)}, u32[]{:S(2)}, u32[]{:S(2)}) collective-permute-start(bf16[2,64,1536]{2,1,0:T(8,128)(2,1)S(1)} %get-tuple-element.168), channel_id=1, source_target_pairs={{0,4},{1,5},{2,6},{3,7},{4,0},{5,1},{6,2},{7,3},{8,12},{9,13},{10,... | collective-permute-start | bytes 1179656 | tf_op jit(solution)/shard_map/ppermute | solution.py:51
  15.7 11.3 %copy-start.8 = (bf16[1536,128]{1,0:T(8,128)(2,1)}, bf16[1536,128]{1,0:T(8,128)(2,1)S(1)}, u32[]{:S(2)}) copy-start(bf16[1536,128]{1,0:T(8,128)(2,1)S(1)} %get-tuple-element.120.refs_8_) | copy-start | bytes 1179652
  16.2 10.4 %collective-permute-start.5 = (bf16[4,12,1120]{2,1,0:T(8,128)(2,1)S(1)}, bf16[4,12,1120]{2,1,0:T(8,128)(2,1)S(1)}, u32[]{:S(2)}, u32[]{:S(2)}) collective-permute-start(bf16[4,12,1120]{2,1,0:T(8,128)(2,1)S(1)} %pad_maximum_fusion.3), channel_id=1, source_target_pairs={{0,6},{2,4},{4,2},{6,0},{1,7},{3,5},{5,3},{7,1},{8,14},{10,12},{12... | collective-permute-start | bytes 322568 | tf_op jit(solution)/shard_map/ppermute | solution.py:43
  17.4 9.2 %collective-permute-start.4 = (bf16[4,12,1120]{2,1,0:T(8,128)(2,1)S(1)}, bf16[4,12,1120]{2,1,0:T(8,128)(2,1)S(1)}, u32[]{:S(2)}, u32[]{:S(2)}) collective-permute-start(bf16[4,12,1120]{2,1,0:T(8,128)(2,1)S(1)} %pad_maximum_fusion.3), channel_id=1, source_target_pairs={{0,4},{2,6},{4,0},{6,2},{1,5},{3,7},{5,1},{7,3},{8,12},{10,14},{12... | collective-permute-start | bytes 322568 | tf_op jit(solution)/shard_map/ppermute | solution.py:43
  18.9 7.8 %collective-permute-start.3 = (bf16[4,12,1120]{2,1,0:T(8,128)(2,1)S(1)}, bf16[4,12,1120]{2,1,0:T(8,128)(2,1)S(1)}, u32[]{:S(2)}, u32[]{:S(2)}) collective-permute-start(bf16[4,12,1120]{2,1,0:T(8,128)(2,1)S(1)} %pad_maximum_fusion.3), channel_id=1, source_target_pairs={{0,2},{2,0},{4,6},{6,4},{1,3},{3,1},{5,7},{7,5},{8,10},{10,8},{12,... | collective-permute-start | bytes 322568 | tf_op jit(solution)/shard_map/ppermute | solution.py:43
  20.4 16.8 %collective-permute-start.10 = (bf16[2,64,1536]{2,1,0:T(8,128)(2,1)}, bf16[2,64,1536]{2,1,0:T(8,128)(2,1)S(1)}, u32[]{:S(2)}, u32[]{:S(2)}) collective-permute-start(bf16[2,64,1536]{2,1,0:T(8,128)(2,1)} %get-tuple-element.86), channel_id=1, source_target_pairs={{0,1},{1,0},{2,3},{3,2},{4,5},{5,4},{6,7},{7,6},{8,9},{9,8},{10,11... | collective-permute-start | bytes 1179656 | tf_op jit(solution)/shard_map/ppermute | solution.py:51
  27.6 12.4 %collective-permute-start.11 = (bf16[2,64,1536]{2,1,0:T(8,128)(2,1)}, bf16[2,64,1536]{2,1,0:T(8,128)(2,1)S(1)}, u32[]{:S(2)}, u32[]{:S(2)}) collective-permute-start(bf16[2,64,1536]{2,1,0:T(8,128)(2,1)} %get-tuple-element.87), channel_id=1, source_target_pairs={{0,6},{1,7},{2,4},{3,5},{4,2},{5,3},{6,0},{7,1},{8,14},{9,15},{10,... | collective-permute-start | bytes 1179656 | tf_op jit(solution)/shard_map/ppermute | solution.py:51
  30.3 12.8 %collective-permute-start.14 = (bf16[2,64,1536]{2,1,0:T(8,128)(2,1)S(1)}, bf16[2,64,1536]{2,1,0:T(8,128)(2,1)S(1)}, u32[]{:S(2)}, u32[]{:S(2)}) collective-permute-start(bf16[2,64,1536]{2,1,0:T(8,128)(2,1)S(1)} %get-tuple-element.90), channel_id=1, source_target_pairs={{0,3},{1,2},{2,1},{3,0},{4,7},{5,6},{6,5},{7,4},{8,11},{9,10},{10,... | collective-permute-start | bytes 1179656 | tf_op jit(solution)/shard_map/ppermute | solution.py:51
  31.0 15.1 %collective-permute-start.8 = (bf16[2,96,1120]{2,1,0:T(8,128)(2,1)S(1)}, bf16[2,96,1120]{2,1,0:T(8,128)(2,1)S(1)}, u32[]{:S(2)}, u32[]{:S(2)}) collective-permute-start(bf16[2,96,1120]{2,1,0:T(8,128)(2,1)S(1)} %get-tuple-element.175), channel_id=1, source_target_pairs={{0,32},{16,48},{32,0},{48,16},{1,33},{17,49},{33,1},{49,17},{2,34}... | collective-permute-start | bytes 1290248 | tf_op jit(solution)/shard_map/ppermute | solution.py:43
  34.9 20.0 %collective-permute-start.7 = (bf16[2,96,1120]{2,1,0:T(8,128)(2,1)S(1)}, bf16[2,96,1120]{2,1,0:T(8,128)(2,1)S(1)}, u32[]{:S(2)}, u32[]{:S(2)}) collective-permute-start(bf16[2,96,1120]{2,1,0:T(8,128)(2,1)S(1)} %get-tuple-element.175), channel_id=1, source_target_pairs={{0,16},{16,0},{32,48},{48,32},{1,17},{17,1},{33,49},{49,33},{2,18}... | collective-permute-start | bytes 1290248 | tf_op jit(solution)/shard_map/ppermute | solution.py:43
  37.1 17.8 %collective-permute-start.9 = (bf16[2,96,1120]{2,1,0:T(8,128)(2,1)S(1)}, bf16[2,96,1120]{2,1,0:T(8,128)(2,1)S(1)}, u32[]{:S(2)}, u32[]{:S(2)}) collective-permute-start(bf16[2,96,1120]{2,1,0:T(8,128)(2,1)S(1)} %get-tuple-element.175), channel_id=1, source_target_pairs={{0,48},{16,32},{32,16},{48,0},{1,49},{17,33},{33,17},{49,1},{2,50}... | collective-permute-start | bytes 1290248 | tf_op jit(solution)/shard_map/ppermute | solution.py:43
  40.0 15.3 %collective-permute-start.12 = (bf16[2,64,1536]{2,1,0:T(8,128)(2,1)S(1)}, bf16[2,64,1536]{2,1,0:T(8,128)(2,1)S(1)}, u32[]{:S(2)}, u32[]{:S(2)}) collective-permute-start(bf16[2,64,1536]{2,1,0:T(8,128)(2,1)S(1)} %copy-done.30), channel_id=1, source_target_pairs={{0,7},{1,6},{2,5},{3,4},{4,3},{5,2},{6,1},{7,0},{8,15},{9,14},{10,... | collective-permute-start | bytes 1179656 | tf_op jit(solution)/shard_map/ppermute | solution.py:51
  43.1 12.2 %collective-permute-start.13 = (bf16[2,64,1536]{2,1,0:T(8,128)(2,1)S(1)}, bf16[2,64,1536]{2,1,0:T(8,128)(2,1)S(1)}, u32[]{:S(2)}, u32[]{:S(2)}) collective-permute-start(bf16[2,64,1536]{2,1,0:T(8,128)(2,1)S(1)} %copy-done.29), channel_id=1, source_target_pairs={{0,2},{1,3},{2,0},{3,1},{4,6},{5,7},{6,4},{7,5},{8,10},{9,11},{10,... | collective-permute-start | bytes 1179656 | tf_op jit(solution)/shard_map/ppermute | solution.py:51
  46.0 15.8 %collective-permute-start.15 = (bf16[2,64,1536]{2,1,0:T(8,128)(2,1)S(1)}, bf16[2,64,1536]{2,1,0:T(8,128)(2,1)S(1)}, u32[]{:S(2)}, u32[]{:S(2)}) collective-permute-start(bf16[2,64,1536]{2,1,0:T(8,128)(2,1)S(1)} %copy-done.28), channel_id=1, source_target_pairs={{0,5},{1,4},{2,7},{3,6},{4,1},{5,0},{6,3},{7,2},{8,13},{9,12},{10,... | collective-permute-start | bytes 1179656 | tf_op jit(solution)/shard_map/ppermute | solution.py:51
  62.6 3.8 %collective-permute-start.16 = (bf16[4,2,96,1120]{3,2,1,0:T(8,128)(2,1)S(1)}, bf16[4,2,96,1120]{3,2,1,0:T(8,128)(2,1)}, u32[]{:S(2)}, u32[]{:S(2)}) collective-permute-start(bf16[4,2,96,1120]{3,2,1,0:T(8,128)(2,1)S(1)} %pad_maximum_fusion.quad_ref), channel_id=1, source_target_pairs={{0,8},{8,0},{1,9},{9,1},{2,10},{10,2},{3,11},{11,3},{4,12},{12,4},... | collective-permute-start | bytes 5160968 | tf_op jit(solution)/shard_map/ppermute | solution.py:43
  87.3 4.0 %collective-permute-start.17 = (bf16[784,1120]{1,0:T(8,128)(2,1)S(1)}, bf16[784,1120]{1,0:T(8,128)(2,1)S(1)}, u32[]{:S(2)}, u32[]{:S(2)}) collective-permute-start(bf16[784,1120]{1,0:T(8,128)(2,1)S(1)} %get-tuple-element.130), channel_id=1, source_target_pairs={{0,8},{8,0},{1,9},{9,1},{2,10},{10,2},{3,11},{11,3},{4,12},{12,4},... | collective-permute-start | bytes 5268488 | tf_op jit(solution)/shard_map/ppermute | solution.py:43
  87.9 9.9 %collective-permute-start.21 = (bf16[128,1120]{1,0:T(8,128)(2,1)S(1)}, bf16[128,1120]{1,0:T(8,128)(2,1)S(1)}, u32[]{:S(2)}, u32[]{:S(2)}) collective-permute-start(bf16[128,1120]{1,0:T(8,128)(2,1)S(1)} %get-tuple-element.141), channel_id=1, source_target_pairs={{0,1},{1,0},{2,3},{3,2},{4,5},{5,4},{6,7},{7,6},{8,9},{9,8},{10,11... | collective-permute-start | bytes 860168 | tf_op jit(solution)/shard_map/ppermute | solution.py:51
  88.8 10.8 %collective-permute-start.22 = (bf16[128,1120]{1,0:T(8,128)(2,1)S(1)}, bf16[128,1120]{1,0:T(8,128)(2,1)S(1)}, u32[]{:S(2)}, u32[]{:S(2)}) collective-permute-start(bf16[128,1120]{1,0:T(8,128)(2,1)S(1)} %get-tuple-element.142), channel_id=1, source_target_pairs={{0,4},{1,5},{2,6},{3,7},{4,0},{5,1},{6,2},{7,3},{8,12},{9,13},{10,... | collective-permute-start | bytes 860168 | tf_op jit(solution)/shard_map/ppermute | solution.py:51
  91.3 10.7 %copy-start.1 = (bf16[2,2,256,1536]{3,2,1,0:T(8,128)(2,1)S(1)}, bf16[2,2,256,1536]{3,2,1,0:T(8,128)(2,1)}, u32[]{:S(2)}) copy-start(bf16[2,2,256,1536]{3,2,1,0:T(8,128)(2,1)} %param.7) | copy-start | bytes 9437188
  92.2 19.4 %collective-permute-start.18 = (bf16[208,1120]{1,0:T(8,128)(2,1)S(1)}, bf16[208,1120]{1,0:T(8,128)(2,1)S(1)}, u32[]{:S(2)}, u32[]{:S(2)}) collective-permute-start(bf16[208,1120]{1,0:T(8,128)(2,1)S(1)} %get-tuple-element.136), channel_id=1, source_target_pairs={{0,16},{16,0},{32,48},{48,32},{1,17},{17,1},{33,49},{49,33},{2,18}... | collective-permute-start | bytes 1397768 | tf_op jit(solution)/shard_map/ppermute | solution.py:43
  94.2 25.2 %collective-permute-start.19 = (bf16[208,1120]{1,0:T(8,128)(2,1)S(1)}, bf16[208,1120]{1,0:T(8,128)(2,1)S(1)}, u32[]{:S(2)}, u32[]{:S(2)}) collective-permute-start(bf16[208,1120]{1,0:T(8,128)(2,1)S(1)} %get-tuple-element.137), channel_id=1, source_target_pairs={{0,32},{16,48},{32,0},{48,16},{1,33},{17,49},{33,1},{49,17},{2,34}... | collective-permute-start | bytes 1397768 | tf_op jit(solution)/shard_map/ppermute | solution.py:43
  97.8 24.1 %collective-permute-start.20 = (bf16[208,1120]{1,0:T(8,128)(2,1)S(1)}, bf16[208,1120]{1,0:T(8,128)(2,1)S(1)}, u32[]{:S(2)}, u32[]{:S(2)}) collective-permute-start(bf16[208,1120]{1,0:T(8,128)(2,1)S(1)} %get-tuple-element.138), channel_id=1, source_target_pairs={{0,48},{16,32},{32,16},{48,0},{1,49},{17,33},{33,17},{49,1},{2,50}... | collective-permute-start | bytes 1397768 | tf_op jit(solution)/shard_map/ppermute | solution.py:43
  97.8 9.6 %collective-permute-start.24 = (bf16[128,1120]{1,0:T(8,128)(2,1)S(1)}, bf16[128,1120]{1,0:T(8,128)(2,1)S(1)}, u32[]{:S(2)}, u32[]{:S(2)}) collective-permute-start(bf16[128,1120]{1,0:T(8,128)(2,1)S(1)} %get-tuple-element.151), channel_id=1, source_target_pairs={{0,3},{1,2},{2,1},{3,0},{4,7},{5,6},{6,5},{7,4},{8,11},{9,10},{10,... | collective-permute-start | bytes 860168 | tf_op jit(solution)/shard_map/ppermute | solution.py:51
  99.7 8.8 %collective-permute-start.25 = (bf16[128,1120]{1,0:T(8,128)(2,1)S(1)}, bf16[128,1120]{1,0:T(8,128)(2,1)S(1)}, u32[]{:S(2)}, u32[]{:S(2)}) collective-permute-start(bf16[128,1120]{1,0:T(8,128)(2,1)S(1)} %get-tuple-element.152), channel_id=1, source_target_pairs={{0,6},{1,7},{2,4},{3,5},{4,2},{5,3},{6,0},{7,1},{8,14},{9,15},{10,... | collective-permute-start | bytes 860168 | tf_op jit(solution)/shard_map/ppermute | solution.py:51
  108.5 16.3 %collective-permute-start.26 = (bf16[128,1120]{1,0:T(8,128)(2,1)S(1)}, bf16[128,1120]{1,0:T(8,128)(2,1)S(1)}, u32[]{:S(2)}, u32[]{:S(2)}) collective-permute-start(bf16[128,1120]{1,0:T(8,128)(2,1)S(1)} %get-tuple-element.155), channel_id=1, source_target_pairs={{0,7},{1,6},{2,5},{3,4},{4,3},{5,2},{6,1},{7,0},{8,15},{9,14},{10,... | collective-permute-start | bytes 860168 | tf_op jit(solution)/shard_map/ppermute | solution.py:51
  111.6 13.2 %collective-permute-start.27 = (bf16[128,1120]{1,0:T(8,128)(2,1)S(1)}, bf16[128,1120]{1,0:T(8,128)(2,1)S(1)}, u32[]{:S(2)}, u32[]{:S(2)}) collective-permute-start(bf16[128,1120]{1,0:T(8,128)(2,1)S(1)} %get-tuple-element.156), channel_id=1, source_target_pairs={{0,2},{1,3},{2,0},{3,1},{4,6},{5,7},{6,4},{7,5},{8,10},{9,11},{10,... | collective-permute-start | bytes 860168 | tf_op jit(solution)/shard_map/ppermute | solution.py:51
  111.6 13.3 %collective-permute-start.28 = (bf16[128,1120]{1,0:T(8,128)(2,1)S(1)}, bf16[128,1120]{1,0:T(8,128)(2,1)S(1)}, u32[]{:S(2)}, u32[]{:S(2)}) collective-permute-start(bf16[128,1120]{1,0:T(8,128)(2,1)S(1)} %get-tuple-element.157), channel_id=1, source_target_pairs={{0,5},{1,4},{2,7},{3,6},{4,1},{5,0},{6,3},{7,2},{8,13},{9,12},{10,... | collective-permute-start | bytes 860168 | tf_op jit(solution)/shard_map/ppermute | solution.py:51
  122.2 12.3 %collective-permute-start.23 = (bf16[112,1120]{1,0:T(8,128)(2,1)S(1)}, bf16[112,1120]{1,0:T(8,128)(2,1)S(1)}, u32[]{:S(2)}, u32[]{:S(2)}) collective-permute-start(bf16[112,1120]{1,0:T(8,128)(2,1)S(1)} %get-tuple-element.146), channel_id=1, source_target_pairs={{0,64},{64,0},{1,65},{65,1},{2,66},{66,2},{3,67},{67,3},{4,68},{68... | collective-permute-start | bytes 752648 | tf_op jit(solution)/shard_map/ppermute | solution.py:43
  (32 other events, 71.4 us)

commit v6 on v5

--- a/solution.py
+++ b/solution.py
@@ -16,7 +16,7 @@
 SPACE = ("yh", "z", "core")
 MEMBER = ("x", "yl")
 BF16 = jnp.bfloat16
-FIRST, SECOND = (0, 1, 4), (3, 6, 7, 2, 5)
+FIRST, SECOND, THIRD = (0, 1, 4), (3, 6), (7, 2, 5)
 F32 = jnp.float32
 
 
@@ -341,15 +341,16 @@
         out_ref[n, 16:32, :] = picked[16 * n : 16 * n + 16]
 
 
-def member_kernel(came_ref, share_ref, small_ref):
+def member_kernel(came_ref, share_ref, gain_out_ref, bias_out_ref):
     total = came_ref[0, 16:32, :].astype(F32)
     small = get_small(came_ref.at[0])
     for n in range(1, 8):
         total = total + came_ref[n, 16:32, :].astype(F32)
         small = small + get_small(came_ref.at[n])
     share_ref[...] = total[0:12]
-    for n in range(24):
-        small_ref[n : n + 1, :] = small[n // 4 : n // 4 + 1, 128 * (n % 4) : 128 * (n % 4 + 1)]
+    for n in range(21):
+        ref, at = (gain_out_ref, n) if n < 12 else (bias_out_ref, n - 12)
+        ref[at : at + 1, :] = small[n // 4 : n // 4 + 1, 128 * (n % 4) : 128 * (n % 4 + 1)]
 
 
 def middle(*operands):
@@ -504,11 +505,11 @@
     )
     for k, piece in zip(late, held):
         returned[k] = swap_member(piece, k)
-    first = backward(FIRST)
-    came, (first,) = after(came, first)
+    first, second = backward(FIRST), backward(SECOND)
+    came, (first, second) = after(came, first, second)
     own, small, send = combine(z_kernel, "z_sums", 96, 112, 1, own, small, *came)
     came = swap(send, "yh", 1)
-    result = backward(SECOND, (FIRST, first))
+    result = backward(THIRD, (FIRST, first), (SECOND, second))
     (came,), (result,) = after((came,), result)
     send = pl.pallas_call(
         yh_kernel,
@@ -520,24 +521,24 @@
         name="yh_sums",
     )(own, small, came)
     came = lax.all_to_all(send, MEMBER, 0, 0)
-    share, small = pl.pallas_call(
+    share, gain_sums, bias_sums = pl.pallas_call(
         member_kernel,
         out_shape=(
             jax.ShapeDtypeStruct((12, outs), F32),
-            jax.ShapeDtypeStruct((24, 128), F32),
+            jax.ShapeDtypeStruct((12, 128), F32),
+            jax.ShapeDtypeStruct((9, 128), F32),
         ),
         in_specs=vmem(1),
-        out_specs=tuple(vmem(2)),
+        out_specs=tuple(vmem(3)),
         compiler_params=params(16),
         cost_estimate=cost(1000000000, 4000000),
         name="member_sums",
     )(came)
-    small = small.reshape(-1)
     return (
         result.reshape(tokens.shape),
-        small[:features],
+        gain_sums.reshape(-1),
         share,
-        small[features : features + outs],
+        bias_sums.reshape(-1)[:outs],
     )
 
 

time: 151 us -> 148 us (0.980)
  waiting for transfers between devices: 29.4 us -> 25.4 us
  Pallas kernels: 42 us -> 43.8 us
    ppermute x12, waiting for transfers between devices: 19.5 us -> 15.3 us  [swap(): return lax.ppermute(value, axis, [(i, i ^ step) for i in range(SIZE[axis])])]
    pallas_call x2 -> x3, Pallas kernels: 15 us -> 16.8 us  [backward(): pl.pallas_call(functools.partial(backward_kernel, order, [done for done,...]
  transfers between devices with their start and end apart: 29 -> 29, of which waited for: 13 -> 14; matrix products, arithmetic and copies ran while one was open for 4% -> 4% of each run, Pallas kernels for 14% -> 15%
where the time goes in v6:
time: 148 us; the launch traced here: 147 us
  starting transfers between devices  48.4 us (33%)
  Pallas kernels  43.8 us (30%)
  waiting for transfers between devices  25.4 us (17%)
  blocking collectives  14.1 us (10%)
  local copies, waits for them, and re-layouts  13.5 us (9%)
    ppermute x14, starting transfers between devices, swap_member(): return lax.ppermute(value, MEMBER, [(i, i ^ step) for i in range(8)])  25.8 us
    pallas_call x1, Pallas kernels, middle(): pl.pallas_call(middle_kernel, out_shape=(jax.ShapeDtypeStruct((features,...  20.1 us
    ppermute x12, starting transfers between devices, swap(): return lax.ppermute(value, axis, [(i, i ^ step) for i in range(SIZE[axis])])  17.9 us
    pallas_call x3, Pallas kernels, backward(): pl.pallas_call(functools.partial(backward_kernel, order, [done for done,...  16.8 us
    ppermute x12, waiting for transfers between devices, swap(): return lax.ppermute(value, axis, [(i, i ^ step) for i in range(SIZE[axis])])  15.3 us
    all_to_all x1, blocking collectives, on_device(): came = lax.all_to_all(send, MEMBER, 0, 0)  14.1 us
    ppermute x14, waiting for transfers between devices, swap_member(): return lax.ppermute(value, MEMBER, [(i, i ^ step) for i in range(8)])  10 us
    unnamed x70, local copies, waits for them, and re-layouts  8.84 us
  transfers between devices with their start and end apart: 29, of which 14 were waited for; matrix products, arithmetic and copies ran while one was open for 4% of the time, Pallas kernels for 15%

profile of v6, /device:TPU:0, one launch (start us, length us, event | category | flops | bytes accessed | tf_op | source)
XLA Modules:
  0.0 147.5 jit_solution(10823626528982302738)
XLA Ops:
  0.6 1.7 %collective-permute-start = (bf16[12,1120]{1,0:T(8,128)(2,1)}, bf16[12,1120]{1,0:T(8,128)(2,1)S(1)}, u32[]{:S(2)}, u32[]{:S(2)}) collective-permute-start(bf16[12,1120]{1,0:T(8,128)(2,1)} %param.9), channel_id=1, source_target_pairs={{0,1},{1,0},{64,65},{65,64},{2,3},{3,2},{66,67},{67,66},{4,5},{5,4... | collective-permute-start | bytes 80648 | tf_op jit(solution)/shard_map/ppermute | solution.py:47
  2.4 2.2 %collective-permute-start.2 = (bf16[12,1120]{1,0:T(8,128)(2,1)}, bf16[12,1120]{1,0:T(8,128)(2,1)S(1)}, u32[]{:S(2)}, u32[]{:S(2)}) collective-permute-start(bf16[12,1120]{1,0:T(8,128)(2,1)} %param.9), channel_id=1, source_target_pairs={{0,65},{1,64},{64,1},{65,0},{2,67},{3,66},{66,3},{67,2},{4,69},{5,... | collective-permute-start | bytes 80648 | tf_op jit(solution)/shard_map/ppermute | solution.py:47
  5.3 3.1 %constant_dynamic-slice_fusion = (bf16[2,1,64,1536]{3,2,1,0:T(8,128)(2,1)S(1)}, bf16[2,64,1536]{2,1,0:T(8,128)(2,1)}, bf16[2,64,1536]{2,1,0:T(8,128)(2,1)}, bf16...) fusion(bf16[2,8,64,1536]{3,2,1,0:T(8,128)(2,1)} %bitcast.54, ...), kind=kLoop, calls=%fused_computation.19 | loop fusion | bytes 6291488 | tf_op jit(solution)/shard_map/jit(dynamic_index_in_dim)/dynamic_slice | solution.py:402
  8.4 3.0 %collective-permute-start.6 = (bf16[2,64,1536]{2,1,0:T(8,128)(2,1)S(1)}, bf16[2,64,1536]{2,1,0:T(8,128)(2,1)S(1)}, u32[]{:S(2)}, u32[]{:S(2)}) collective-permute-start(bf16[2,64,1536]{2,1,0:T(8,128)(2,1)S(1)} %get-tuple-element.172), channel_id=1, source_target_pairs={{0,4},{1,5},{2,6},{3,7},{4,0},{5,1},{6,2},{7,3},{8,12},{9,13},{10,... | collective-permute-start | bytes 1179656 | tf_op jit(solution)/shard_map/ppermute | solution.py:51
  11.7 1.3 truth.1.truth_ref
  16.2 1.2 collective-permute-start.5
  17.4 1.5 %collective-permute-start.4 = (bf16[4,12,1120]{2,1,0:T(8,128)(2,1)S(1)}, bf16[4,12,1120]{2,1,0:T(8,128)(2,1)S(1)}, u32[]{:S(2)}, u32[]{:S(2)}) collective-permute-start(bf16[4,12,1120]{2,1,0:T(8,128)(2,1)S(1)} %pad_maximum_fusion.3), channel_id=1, source_target_pairs={{0,4},{2,6},{4,0},{6,2},{1,5},{3,7},{5,1},{7,3},{8,12},{10,14},{12... | collective-permute-start | bytes 322568 | tf_op jit(solution)/shard_map/ppermute | solution.py:43
  18.9 1.4 collective-permute-start.3
  20.4 1.3 collective-permute-start.10
  21.6 4.9 %collective-permute-done.5 = bf16[4,12,1120]{2,1,0:T(8,128)(2,1)S(1)} collective-permute-done((bf16[4,12,1120]{2,1,0:T(8,128)(2,1)S(1)}, bf16[4,12,1120]{2,1,0:T(8,128)(2,1)S(1)}, u32[]{:S(2)}, u32[]{:S(2)}) %collective-permute-start.5) | collective-permute-done | bytes 107552 | tf_op jit(solution)/shard_map/ppermute | solution.py:43
  27.6 2.7 %collective-permute-start.11 = (bf16[2,64,1536]{2,1,0:T(8,128)(2,1)}, bf16[2,64,1536]{2,1,0:T(8,128)(2,1)S(1)}, u32[]{:S(2)}, u32[]{:S(2)}) collective-permute-start(bf16[2,64,1536]{2,1,0:T(8,128)(2,1)} %get-tuple-element.89), channel_id=1, source_target_pairs={{0,6},{1,7},{2,4},{3,5},{4,2},{5,3},{6,0},{7,1},{8,14},{9,15},{10,... | collective-permute-start | bytes 1179656 | tf_op jit(solution)/shard_map/ppermute | solution.py:51
  31.0 4.0 %collective-permute-start.8 = (bf16[2,96,1120]{2,1,0:T(8,128)(2,1)S(1)}, bf16[2,96,1120]{2,1,0:T(8,128)(2,1)S(1)}, u32[]{:S(2)}, u32[]{:S(2)}) collective-permute-start(bf16[2,96,1120]{2,1,0:T(8,128)(2,1)S(1)} %get-tuple-element.179), channel_id=1, source_target_pairs={{0,32},{16,48},{32,0},{48,16},{1,33},{17,49},{33,1},{49,17},{2,34}... | collective-permute-start | bytes 1290248 | tf_op jit(solution)/shard_map/ppermute | solution.py:43
  37.2 2.9 %collective-permute-done.11 = bf16[2,64,1536]{2,1,0:T(8,128)(2,1)S(1)} collective-permute-done((bf16[2,64,1536]{2,1,0:T(8,128)(2,1)}, bf16[2,64,1536]{2,1,0:T(8,128)(2,1)S(1)}, u32[]{:S(2)}, u32[]{:S(2)}) %collective-permute-start.11) | collective-permute-done | bytes 393248 | tf_op jit(solution)/shard_map/ppermute | solution.py:51
  40.0 3.1 %collective-permute-start.12 = (bf16[2,64,1536]{2,1,0:T(8,128)(2,1)S(1)}, bf16[2,64,1536]{2,1,0:T(8,128)(2,1)S(1)}, u32[]{:S(2)}, u32[]{:S(2)}) collective-permute-start(bf16[2,64,1536]{2,1,0:T(8,128)(2,1)S(1)} %copy-done.30), channel_id=1, source_target_pairs={{0,7},{1,6},{2,5},{3,4},{4,3},{5,2},{6,1},{7,0},{8,15},{9,14},{10,... | collective-permute-start | bytes 1179656 | tf_op jit(solution)/shard_map/ppermute | solution.py:51
  46.0 2.4 %collective-permute-start.15 = (bf16[2,64,1536]{2,1,0:T(8,128)(2,1)S(1)}, bf16[2,64,1536]{2,1,0:T(8,128)(2,1)S(1)}, u32[]{:S(2)}, u32[]{:S(2)}) collective-permute-start(bf16[2,64,1536]{2,1,0:T(8,128)(2,1)S(1)} %copy-done.28), channel_id=1, source_target_pairs={{0,5},{1,4},{2,7},{3,6},{4,1},{5,0},{6,3},{7,2},{8,13},{9,12},{10,... | collective-permute-start | bytes 1179656 | tf_op jit(solution)/shard_map/ppermute | solution.py:51
  50.4 4.5 %collective-permute-done.7 = bf16[2,96,1120]{2,1,0:T(8,128)(2,1)S(1)} collective-permute-done((bf16[2,96,1120]{2,1,0:T(8,128)(2,1)S(1)}, bf16[2,96,1120]{2,1,0:T(8,128)(2,1)S(1)}, u32[]{:S(2)}, u32[]{:S(2)}) %collective-permute-start.7) | collective-permute-done | bytes 430112 | tf_op jit(solution)/shard_map/ppermute | solution.py:43
  56.0 5.8 %collective-permute-done.15 = bf16[2,64,1536]{2,1,0:T(8,128)(2,1)S(1)} collective-permute-done((bf16[2,64,1536]{2,1,0:T(8,128)(2,1)S(1)}, bf16[2,64,1536]{2,1,0:T(8,128)(2,1)S(1)}, u32[]{:S(2)}, u32[]{:S(2)}) %collective-permute-start.15) | collective-permute-done | bytes 393248 | tf_op jit(solution)/shard_map/ppermute | solution.py:51
  67.3 20.1 %middle.1 = (bf16[1536,1120]{1,0:T(8,128)(2,1)S(1)}, f32[8,96,1120]{2,1,0:T(8,128)S(1)}, bf16[784,1120]{1,0:T(8,128)(2,1)S(1)}, f32[8,512]{1,0:T(8,128)S(1)}, bf...) custom-call(s32[6]{0:T(128)S(1)} %stack.81.place_ref, ...), custom_call_target="tpu_custom_call" | custom-call | flops 20000000000 | bytes 80000000 | tf_op jit(solution)/shard_map/middle/pallas_call | solution.py:359
  88.8 2.0 %collective-permute-start.22 = (bf16[128,1120]{1,0:T(8,128)(2,1)S(1)}, bf16[128,1120]{1,0:T(8,128)(2,1)S(1)}, u32[]{:S(2)}, u32[]{:S(2)}) collective-permute-start(bf16[128,1120]{1,0:T(8,128)(2,1)S(1)} %get-tuple-element.144), channel_id=1, source_target_pairs={{0,4},{1,5},{2,6},{3,7},{4,0},{5,1},{6,2},{7,3},{8,12},{9,13},{10,... | collective-permute-start | bytes 860168 | tf_op jit(solution)/shard_map/ppermute | solution.py:51
  92.2 2.0 %collective-permute-start.18 = (bf16[208,1120]{1,0:T(8,128)(2,1)S(1)}, bf16[208,1120]{1,0:T(8,128)(2,1)S(1)}, u32[]{:S(2)}, u32[]{:S(2)}) collective-permute-start(bf16[208,1120]{1,0:T(8,128)(2,1)S(1)} %get-tuple-element.138), channel_id=1, source_target_pairs={{0,16},{16,0},{32,48},{48,32},{1,17},{17,1},{33,49},{49,33},{2,18}... | collective-permute-start | bytes 1397768 | tf_op jit(solution)/shard_map/ppermute | solution.py:43
  94.2 3.6 %collective-permute-start.19 = (bf16[208,1120]{1,0:T(8,128)(2,1)S(1)}, bf16[208,1120]{1,0:T(8,128)(2,1)S(1)}, u32[]{:S(2)}, u32[]{:S(2)}) collective-permute-start(bf16[208,1120]{1,0:T(8,128)(2,1)S(1)} %get-tuple-element.139), channel_id=1, source_target_pairs={{0,32},{16,48},{32,0},{48,16},{1,33},{17,49},{33,1},{49,17},{2,34}... | collective-permute-start | bytes 1397768 | tf_op jit(solution)/shard_map/ppermute | solution.py:43
  97.8 1.8 %collective-permute-start.23 = (bf16[128,1120]{1,0:T(8,128)(2,1)S(1)}, bf16[128,1120]{1,0:T(8,128)(2,1)S(1)}, u32[]{:S(2)}, u32[]{:S(2)}) collective-permute-start(bf16[128,1120]{1,0:T(8,128)(2,1)S(1)} %get-tuple-element.148), channel_id=1, source_target_pairs={{0,3},{1,2},{2,1},{3,0},{4,7},{5,6},{6,5},{7,4},{8,11},{9,10},{10,... | collective-permute-start | bytes 860168 | tf_op jit(solution)/shard_map/ppermute | solution.py:51
  99.7 2.3 %collective-permute-start.24 = (bf16[128,1120]{1,0:T(8,128)(2,1)S(1)}, bf16[128,1120]{1,0:T(8,128)(2,1)S(1)}, u32[]{:S(2)}, u32[]{:S(2)}) collective-permute-start(bf16[128,1120]{1,0:T(8,128)(2,1)S(1)} %get-tuple-element.149), channel_id=1, source_target_pairs={{0,6},{1,7},{2,4},{3,5},{4,2},{5,3},{6,0},{7,1},{8,14},{9,15},{10,... | collective-permute-start | bytes 860168 | tf_op jit(solution)/shard_map/ppermute | solution.py:51
  102.0 5.4 %backward.3.refs_0_ = bf16[3,2,64,1536]{3,2,1,0:T(8,128)(2,1)S(1)} custom-call(s32[6]{0:T(128)S(1)} %stack.81.place_ref, bf16[2,8,64,1536]{3,2,1,0:T(8,128)(2,1)S(1)} %bitcast.55, f32[1,1536]{1,0:T(1,128)S(1)} %reshape.154.gain_ref, bf16[1536,1120]{1,0:T(8,128)(2,1)S(1)} %get-tuple-element.141.full_ref, bf16[128,1120]{1,0:T(8,128)(2,1)S(1)} %get-tuple-element.142.refs_0_, ...), custom_call_target="tpu_custom_call" | custom-call | flops 1000 | bytes 1000 | tf_op jit(solution)/shard_map/backward/pallas_call | solution.py:464
  108.5 3.1 %collective-permute-start.26 = (bf16[128,1120]{1,0:T(8,128)(2,1)S(1)}, bf16[128,1120]{1,0:T(8,128)(2,1)S(1)}, u32[]{:S(2)}, u32[]{:S(2)}) collective-permute-start(bf16[128,1120]{1,0:T(8,128)(2,1)S(1)} %get-tuple-element.158), channel_id=1, source_target_pairs={{0,7},{1,6},{2,5},{3,4},{4,3},{5,2},{6,1},{7,0},{8,15},{9,14},{10,... | collective-permute-start | bytes 860168 | tf_op jit(solution)/shard_map/ppermute | solution.py:51
  111.6 4.2 %backward.4.refs_1_ = bf16[2,2,64,1536]{3,2,1,0:T(8,128)(2,1)S(1)} custom-call(s32[6]{0:T(128)S(1)} %stack.81.place_ref, bf16[2,8,64,1536]{3,2,1,0:T(8,128)(2,1)S(1)} %bitcast.56, f32[1,1536]{1,0:T(1,128)S(1)} %reshape.154.gain_ref, bf16[1536,1120]{1,0:T(8,128)(2,1)S(1)} %get-tuple-element.141.full_ref, ...), custom_call_target="tpu_custom_call" | custom-call | flops 1000 | bytes 1000 | tf_op jit(solution)/shard_map/backward/pallas_call | solution.py:464
  115.8 2.6 %collective-permute-start.28 = (bf16[128,1120]{1,0:T(8,128)(2,1)S(1)}, bf16[128,1120]{1,0:T(8,128)(2,1)S(1)}, u32[]{:S(2)}, u32[]{:S(2)}) collective-permute-start(bf16[128,1120]{1,0:T(8,128)(2,1)S(1)} %get-tuple-element.160), channel_id=1, source_target_pairs={{0,5},{1,4},{2,7},{3,6},{4,1},{5,0},{6,3},{7,2},{8,13},{9,12},{10,... | collective-permute-start | bytes 860168 | tf_op jit(solution)/shard_map/ppermute | solution.py:51
  118.3 1.0 collective-permute-done.19.b_ref
  119.4 2.6 %collective-permute-done.20.c_ref = bf16[208,1120]{1,0:T(8,128)(2,1)S(1)} collective-permute-done((bf16[208,1120]{1,0:T(8,128)(2,1)S(1)}, bf16[208,1120]{1,0:T(8,128)(2,1)S(1)}, u32[]{:S(2)}, u32[]{:S(2)}) %collective-permute-start.20) | collective-permute-done | bytes 465952 | tf_op jit(solution)/shard_map/ppermute | solution.py:43
  122.2 2.6 %collective-permute-start.25 = (bf16[112,1120]{1,0:T(8,128)(2,1)S(1)}, bf16[112,1120]{1,0:T(8,128)(2,1)S(1)}, u32[]{:S(2)}, u32[]{:S(2)}) collective-permute-start(bf16[112,1120]{1,0:T(8,128)(2,1)S(1)} %get-tuple-element.155), channel_id=1, source_target_pairs={{0,64},{64,0},{1,65},{65,1},{2,66},{66,2},{3,67},{67,3},{4,68},{68... | collective-permute-start | bytes 752648 | tf_op jit(solution)/shard_map/ppermute | solution.py:43
  125.1 7.2 %backward.5 = bf16[2,8,64,1536]{3,2,1,0:T(8,128)(2,1)} custom-call(s32[6]{0:T(128)S(1)} %stack.81.place_ref, bf16[2,8,64,1536]{3,2,1,0:T(8,128)(2,1)S(1)} %bitcast.57, f32[1,1536]{1,0:T(1,128)S(1)} %reshape.154.gain_ref, bf16[1536,1120]{1,0:T(8,128)(2,1)S(1)} %get-tuple-element.141.full_ref, bf16[3,2,64,1536]{3,2,1,0:T(8,128)(2,1)S(1)} %backward.3.refs_0_, ...), custom_call_target="tpu_custom_call" | custom-call | flops 1000 | bytes 1000 | tf_op jit(solution)/shard_map/backward/pallas_call | solution.py:464
  132.7 14.1 %all_to_all.5.came_ref = bf16[8,32,1120]{2,1,0:T(8,128)(2,1)S(1)} all-to-all(bf16[8,32,1120]{2,1,0:T(8,128)(2,1)S(1)} %yh_sums.1), channel_id=1, replica_groups=mesh['yh'=2,'z'=4,'core'=2,'x'=4,'yl'=2] {'x','yl'}, dimensions={0} | all-to-all | bytes 1146880 | tf_op jit(solution)/shard_map/all_to_all | solution.py:523
  (135 shorter events, 24.6 us)
Async XLA Ops:
  0.6 10.8 %copy-start = (bf16[70,8,1024]{2,1,0:T(8,128)(2,1)S(1)}, bf16[70,8,1024]{2,1,0:T(8,128)(2,1)}, u32[]{:S(2)}) copy-start(bf16[70,8,1024]{2,1,0:T(8,128)(2,1)} %param.11) | copy-start | bytes 3440644
  0.6 15.4 %collective-permute-start = (bf16[12,1120]{1,0:T(8,128)(2,1)}, bf16[12,1120]{1,0:T(8,128)(2,1)S(1)}, u32[]{:S(2)}, u32[]{:S(2)}) collective-permute-start(bf16[12,1120]{1,0:T(8,128)(2,1)} %param.9), channel_id=1, source_target_pairs={{0,1},{1,0},{64,65},{65,64},{2,3},{3,2},{66,67},{67,66},{4,5},{5,4... | collective-permute-start | bytes 80648 | tf_op jit(solution)/shard_map/ppermute | solution.py:47
  2.4 13.7 %collective-permute-start.2 = (bf16[12,1120]{1,0:T(8,128)(2,1)}, bf16[12,1120]{1,0:T(8,128)(2,1)S(1)}, u32[]{:S(2)}, u32[]{:S(2)}) collective-permute-start(bf16[12,1120]{1,0:T(8,128)(2,1)} %param.9), channel_id=1, source_target_pairs={{0,65},{1,64},{64,1},{65,0},{2,67},{3,66},{66,3},{67,2},{4,69},{5,... | collective-permute-start | bytes 80648 | tf_op jit(solution)/shard_map/ppermute | solution.py:47
  4.6 11.5 %collective-permute-start.1 = (bf16[12,1120]{1,0:T(8,128)(2,1)}, bf16[12,1120]{1,0:T(8,128)(2,1)S(1)}, u32[]{:S(2)}, u32[]{:S(2)}) collective-permute-start(bf16[12,1120]{1,0:T(8,128)(2,1)} %param.9), channel_id=1, source_target_pairs={{0,64},{1,65},{64,0},{65,1},{2,66},{3,67},{66,2},{67,3},{4,68},{5,... | collective-permute-start | bytes 80648 | tf_op jit(solution)/shard_map/ppermute | solution.py:47
  8.4 18.4 %collective-permute-start.6 = (bf16[2,64,1536]{2,1,0:T(8,128)(2,1)S(1)}, bf16[2,64,1536]{2,1,0:T(8,128)(2,1)S(1)}, u32[]{:S(2)}, u32[]{:S(2)}) collective-permute-start(bf16[2,64,1536]{2,1,0:T(8,128)(2,1)S(1)} %get-tuple-element.172), channel_id=1, source_target_pairs={{0,4},{1,5},{2,6},{3,7},{4,0},{5,1},{6,2},{7,3},{8,12},{9,13},{10,... | collective-permute-start | bytes 1179656 | tf_op jit(solution)/shard_map/ppermute | solution.py:51
  15.7 11.3 %copy-start.8 = (bf16[1536,128]{1,0:T(8,128)(2,1)}, bf16[1536,128]{1,0:T(8,128)(2,1)S(1)}, u32[]{:S(2)}) copy-start(bf16[1536,128]{1,0:T(8,128)(2,1)S(1)} %get-tuple-element.122.refs_8_) | copy-start | bytes 1179652
  16.2 10.4 %collective-permute-start.5 = (bf16[4,12,1120]{2,1,0:T(8,128)(2,1)S(1)}, bf16[4,12,1120]{2,1,0:T(8,128)(2,1)S(1)}, u32[]{:S(2)}, u32[]{:S(2)}) collective-permute-start(bf16[4,12,1120]{2,1,0:T(8,128)(2,1)S(1)} %pad_maximum_fusion.3), channel_id=1, source_target_pairs={{0,6},{2,4},{4,2},{6,0},{1,7},{3,5},{5,3},{7,1},{8,14},{10,12},{12... | collective-permute-start | bytes 322568 | tf_op jit(solution)/shard_map/ppermute | solution.py:43
  17.4 9.2 %collective-permute-start.4 = (bf16[4,12,1120]{2,1,0:T(8,128)(2,1)S(1)}, bf16[4,12,1120]{2,1,0:T(8,128)(2,1)S(1)}, u32[]{:S(2)}, u32[]{:S(2)}) collective-permute-start(bf16[4,12,1120]{2,1,0:T(8,128)(2,1)S(1)} %pad_maximum_fusion.3), channel_id=1, source_target_pairs={{0,4},{2,6},{4,0},{6,2},{1,5},{3,7},{5,1},{7,3},{8,12},{10,14},{12... | collective-permute-start | bytes 322568 | tf_op jit(solution)/shard_map/ppermute | solution.py:43
  18.9 7.8 %collective-permute-start.3 = (bf16[4,12,1120]{2,1,0:T(8,128)(2,1)S(1)}, bf16[4,12,1120]{2,1,0:T(8,128)(2,1)S(1)}, u32[]{:S(2)}, u32[]{:S(2)}) collective-permute-start(bf16[4,12,1120]{2,1,0:T(8,128)(2,1)S(1)} %pad_maximum_fusion.3), channel_id=1, source_target_pairs={{0,2},{2,0},{4,6},{6,4},{1,3},{3,1},{5,7},{7,5},{8,10},{10,8},{12,... | collective-permute-start | bytes 322568 | tf_op jit(solution)/shard_map/ppermute | solution.py:43
  20.4 16.8 %collective-permute-start.10 = (bf16[2,64,1536]{2,1,0:T(8,128)(2,1)}, bf16[2,64,1536]{2,1,0:T(8,128)(2,1)S(1)}, u32[]{:S(2)}, u32[]{:S(2)}) collective-permute-start(bf16[2,64,1536]{2,1,0:T(8,128)(2,1)} %get-tuple-element.88), channel_id=1, source_target_pairs={{0,1},{1,0},{2,3},{3,2},{4,5},{5,4},{6,7},{7,6},{8,9},{9,8},{10,11... | collective-permute-start | bytes 1179656 | tf_op jit(solution)/shard_map/ppermute | solution.py:51
  27.6 12.4 %collective-permute-start.11 = (bf16[2,64,1536]{2,1,0:T(8,128)(2,1)}, bf16[2,64,1536]{2,1,0:T(8,128)(2,1)S(1)}, u32[]{:S(2)}, u32[]{:S(2)}) collective-permute-start(bf16[2,64,1536]{2,1,0:T(8,128)(2,1)} %get-tuple-element.89), channel_id=1, source_target_pairs={{0,6},{1,7},{2,4},{3,5},{4,2},{5,3},{6,0},{7,1},{8,14},{9,15},{10,... | collective-permute-start | bytes 1179656 | tf_op jit(solution)/shard_map/ppermute | solution.py:51
  30.3 12.8 %collective-permute-start.14 = (bf16[2,64,1536]{2,1,0:T(8,128)(2,1)S(1)}, bf16[2,64,1536]{2,1,0:T(8,128)(2,1)S(1)}, u32[]{:S(2)}, u32[]{:S(2)}) collective-permute-start(bf16[2,64,1536]{2,1,0:T(8,128)(2,1)S(1)} %get-tuple-element.92), channel_id=1, source_target_pairs={{0,3},{1,2},{2,1},{3,0},{4,7},{5,6},{6,5},{7,4},{8,11},{9,10},{10,... | collective-permute-start | bytes 1179656 | tf_op jit(solution)/shard_map/ppermute | solution.py:51
  31.0 15.1 %collective-permute-start.8 = (bf16[2,96,1120]{2,1,0:T(8,128)(2,1)S(1)}, bf16[2,96,1120]{2,1,0:T(8,128)(2,1)S(1)}, u32[]{:S(2)}, u32[]{:S(2)}) collective-permute-start(bf16[2,96,1120]{2,1,0:T(8,128)(2,1)S(1)} %get-tuple-element.179), channel_id=1, source_target_pairs={{0,32},{16,48},{32,0},{48,16},{1,33},{17,49},{33,1},{49,17},{2,34}... | collective-permute-start | bytes 1290248 | tf_op jit(solution)/shard_map/ppermute | solution.py:43
  34.9 20.0 %collective-permute-start.7 = (bf16[2,96,1120]{2,1,0:T(8,128)(2,1)S(1)}, bf16[2,96,1120]{2,1,0:T(8,128)(2,1)S(1)}, u32[]{:S(2)}, u32[]{:S(2)}) collective-permute-start(bf16[2,96,1120]{2,1,0:T(8,128)(2,1)S(1)} %get-tuple-element.179), channel_id=1, source_target_pairs={{0,16},{16,0},{32,48},{48,32},{1,17},{17,1},{33,49},{49,33},{2,18}... | collective-permute-start | bytes 1290248 | tf_op jit(solution)/shard_map/ppermute | solution.py:43
  37.1 17.8 %collective-permute-start.9 = (bf16[2,96,1120]{2,1,0:T(8,128)(2,1)S(1)}, bf16[2,96,1120]{2,1,0:T(8,128)(2,1)S(1)}, u32[]{:S(2)}, u32[]{:S(2)}) collective-permute-start(bf16[2,96,1120]{2,1,0:T(8,128)(2,1)S(1)} %get-tuple-element.179), channel_id=1, source_target_pairs={{0,48},{16,32},{32,16},{48,0},{1,49},{17,33},{33,17},{49,1},{2,50}... | collective-permute-start | bytes 1290248 | tf_op jit(solution)/shard_map/ppermute | solution.py:43
  40.0 15.3 %collective-permute-start.12 = (bf16[2,64,1536]{2,1,0:T(8,128)(2,1)S(1)}, bf16[2,64,1536]{2,1,0:T(8,128)(2,1)S(1)}, u32[]{:S(2)}, u32[]{:S(2)}) collective-permute-start(bf16[2,64,1536]{2,1,0:T(8,128)(2,1)S(1)} %copy-done.30), channel_id=1, source_target_pairs={{0,7},{1,6},{2,5},{3,4},{4,3},{5,2},{6,1},{7,0},{8,15},{9,14},{10,... | collective-permute-start | bytes 1179656 | tf_op jit(solution)/shard_map/ppermute | solution.py:51
  43.1 12.2 %collective-permute-start.13 = (bf16[2,64,1536]{2,1,0:T(8,128)(2,1)S(1)}, bf16[2,64,1536]{2,1,0:T(8,128)(2,1)S(1)}, u32[]{:S(2)}, u32[]{:S(2)}) collective-permute-start(bf16[2,64,1536]{2,1,0:T(8,128)(2,1)S(1)} %copy-done.29), channel_id=1, source_target_pairs={{0,2},{1,3},{2,0},{3,1},{4,6},{5,7},{6,4},{7,5},{8,10},{9,11},{10,... | collective-permute-start | bytes 1179656 | tf_op jit(solution)/shard_map/ppermute | solution.py:51
  46.0 15.8 %collective-permute-start.15 = (bf16[2,64,1536]{2,1,0:T(8,128)(2,1)S(1)}, bf16[2,64,1536]{2,1,0:T(8,128)(2,1)S(1)}, u32[]{:S(2)}, u32[]{:S(2)}) collective-permute-start(bf16[2,64,1536]{2,1,0:T(8,128)(2,1)S(1)} %copy-done.28), channel_id=1, source_target_pairs={{0,5},{1,4},{2,7},{3,6},{4,1},{5,0},{6,3},{7,2},{8,13},{9,12},{10,... | collective-permute-start | bytes 1179656 | tf_op jit(solution)/shard_map/ppermute | solution.py:51
  62.6 3.8 %collective-permute-start.16 = (bf16[4,2,96,1120]{3,2,1,0:T(8,128)(2,1)S(1)}, bf16[4,2,96,1120]{3,2,1,0:T(8,128)(2,1)}, u32[]{:S(2)}, u32[]{:S(2)}) collective-permute-start(bf16[4,2,96,1120]{3,2,1,0:T(8,128)(2,1)S(1)} %pad_maximum_fusion.quad_ref), channel_id=1, source_target_pairs={{0,8},{8,0},{1,9},{9,1},{2,10},{10,2},{3,11},{11,3},{4,12},{12,4},... | collective-permute-start | bytes 5160968 | tf_op jit(solution)/shard_map/ppermute | solution.py:43
  87.3 4.0 %collective-permute-start.17 = (bf16[784,1120]{1,0:T(8,128)(2,1)S(1)}, bf16[784,1120]{1,0:T(8,128)(2,1)S(1)}, u32[]{:S(2)}, u32[]{:S(2)}) collective-permute-start(bf16[784,1120]{1,0:T(8,128)(2,1)S(1)} %get-tuple-element.132), channel_id=1, source_target_pairs={{0,8},{8,0},{1,9},{9,1},{2,10},{10,2},{3,11},{11,3},{4,12},{12,4},... | collective-permute-start | bytes 5268488 | tf_op jit(solution)/shard_map/ppermute | solution.py:43
  87.9 9.9 %collective-permute-start.21 = (bf16[128,1120]{1,0:T(8,128)(2,1)S(1)}, bf16[128,1120]{1,0:T(8,128)(2,1)S(1)}, u32[]{:S(2)}, u32[]{:S(2)}) collective-permute-start(bf16[128,1120]{1,0:T(8,128)(2,1)S(1)} %get-tuple-element.143), channel_id=1, source_target_pairs={{0,1},{1,0},{2,3},{3,2},{4,5},{5,4},{6,7},{7,6},{8,9},{9,8},{10,11... | collective-permute-start | bytes 860168 | tf_op jit(solution)/shard_map/ppermute | solution.py:51
  88.8 10.8 %collective-permute-start.22 = (bf16[128,1120]{1,0:T(8,128)(2,1)S(1)}, bf16[128,1120]{1,0:T(8,128)(2,1)S(1)}, u32[]{:S(2)}, u32[]{:S(2)}) collective-permute-start(bf16[128,1120]{1,0:T(8,128)(2,1)S(1)} %get-tuple-element.144), channel_id=1, source_target_pairs={{0,4},{1,5},{2,6},{3,7},{4,0},{5,1},{6,2},{7,3},{8,12},{9,13},{10,... | collective-permute-start | bytes 860168 | tf_op jit(solution)/shard_map/ppermute | solution.py:51
  91.3 10.7 %copy-start.1 = (bf16[2,2,256,1536]{3,2,1,0:T(8,128)(2,1)S(1)}, bf16[2,2,256,1536]{3,2,1,0:T(8,128)(2,1)}, u32[]{:S(2)}) copy-start(bf16[2,2,256,1536]{3,2,1,0:T(8,128)(2,1)} %param.7) | copy-start | bytes 9437188
  92.2 23.6 %collective-permute-start.18 = (bf16[208,1120]{1,0:T(8,128)(2,1)S(1)}, bf16[208,1120]{1,0:T(8,128)(2,1)S(1)}, u32[]{:S(2)}, u32[]{:S(2)}) collective-permute-start(bf16[208,1120]{1,0:T(8,128)(2,1)S(1)} %get-tuple-element.138), channel_id=1, source_target_pairs={{0,16},{16,0},{32,48},{48,32},{1,17},{17,1},{33,49},{49,33},{2,18}... | collective-permute-start | bytes 1397768 | tf_op jit(solution)/shard_map/ppermute | solution.py:43
  94.2 25.2 %collective-permute-start.19 = (bf16[208,1120]{1,0:T(8,128)(2,1)S(1)}, bf16[208,1120]{1,0:T(8,128)(2,1)S(1)}, u32[]{:S(2)}, u32[]{:S(2)}) collective-permute-start(bf16[208,1120]{1,0:T(8,128)(2,1)S(1)} %get-tuple-element.139), channel_id=1, source_target_pairs={{0,32},{16,48},{32,0},{48,16},{1,33},{17,49},{33,1},{49,17},{2,34}... | collective-permute-start | bytes 1397768 | tf_op jit(solution)/shard_map/ppermute | solution.py:43
  97.8 24.1 %collective-permute-start.20 = (bf16[208,1120]{1,0:T(8,128)(2,1)S(1)}, bf16[208,1120]{1,0:T(8,128)(2,1)S(1)}, u32[]{:S(2)}, u32[]{:S(2)}) collective-permute-start(bf16[208,1120]{1,0:T(8,128)(2,1)S(1)} %get-tuple-element.140), channel_id=1, source_target_pairs={{0,48},{16,32},{32,16},{48,0},{1,49},{17,33},{33,17},{49,1},{2,50}... | collective-permute-start | bytes 1397768 | tf_op jit(solution)/shard_map/ppermute | solution.py:43
  97.8 9.6 %collective-permute-start.23 = (bf16[128,1120]{1,0:T(8,128)(2,1)S(1)}, bf16[128,1120]{1,0:T(8,128)(2,1)S(1)}, u32[]{:S(2)}, u32[]{:S(2)}) collective-permute-start(bf16[128,1120]{1,0:T(8,128)(2,1)S(1)} %get-tuple-element.148), channel_id=1, source_target_pairs={{0,3},{1,2},{2,1},{3,0},{4,7},{5,6},{6,5},{7,4},{8,11},{9,10},{10,... | collective-permute-start | bytes 860168 | tf_op jit(solution)/shard_map/ppermute | solution.py:51
  99.7 8.8 %collective-permute-start.24 = (bf16[128,1120]{1,0:T(8,128)(2,1)S(1)}, bf16[128,1120]{1,0:T(8,128)(2,1)S(1)}, u32[]{:S(2)}, u32[]{:S(2)}) collective-permute-start(bf16[128,1120]{1,0:T(8,128)(2,1)S(1)} %get-tuple-element.149), channel_id=1, source_target_pairs={{0,6},{1,7},{2,4},{3,5},{4,2},{5,3},{6,0},{7,1},{8,14},{9,15},{10,... | collective-permute-start | bytes 860168 | tf_op jit(solution)/shard_map/ppermute | solution.py:51
  108.5 16.3 %collective-permute-start.26 = (bf16[128,1120]{1,0:T(8,128)(2,1)S(1)}, bf16[128,1120]{1,0:T(8,128)(2,1)S(1)}, u32[]{:S(2)}, u32[]{:S(2)}) collective-permute-start(bf16[128,1120]{1,0:T(8,128)(2,1)S(1)} %get-tuple-element.158), channel_id=1, source_target_pairs={{0,7},{1,6},{2,5},{3,4},{4,3},{5,2},{6,1},{7,0},{8,15},{9,14},{10,... | collective-permute-start | bytes 860168 | tf_op jit(solution)/shard_map/ppermute | solution.py:51
  111.6 13.2 %collective-permute-start.27 = (bf16[128,1120]{1,0:T(8,128)(2,1)S(1)}, bf16[128,1120]{1,0:T(8,128)(2,1)S(1)}, u32[]{:S(2)}, u32[]{:S(2)}) collective-permute-start(bf16[128,1120]{1,0:T(8,128)(2,1)S(1)} %get-tuple-element.159), channel_id=1, source_target_pairs={{0,2},{1,3},{2,0},{3,1},{4,6},{5,7},{6,4},{7,5},{8,10},{9,11},{10,... | collective-permute-start | bytes 860168 | tf_op jit(solution)/shard_map/ppermute | solution.py:51
  115.8 9.3 %collective-permute-start.28 = (bf16[128,1120]{1,0:T(8,128)(2,1)S(1)}, bf16[128,1120]{1,0:T(8,128)(2,1)S(1)}, u32[]{:S(2)}, u32[]{:S(2)}) collective-permute-start(bf16[128,1120]{1,0:T(8,128)(2,1)S(1)} %get-tuple-element.160), channel_id=1, source_target_pairs={{0,5},{1,4},{2,7},{3,6},{4,1},{5,0},{6,3},{7,2},{8,13},{9,12},{10,... | collective-permute-start | bytes 860168 | tf_op jit(solution)/shard_map/ppermute | solution.py:51
  122.2 10.2 %collective-permute-start.25 = (bf16[112,1120]{1,0:T(8,128)(2,1)S(1)}, bf16[112,1120]{1,0:T(8,128)(2,1)S(1)}, u32[]{:S(2)}, u32[]{:S(2)}) collective-permute-start(bf16[112,1120]{1,0:T(8,128)(2,1)S(1)} %get-tuple-element.155), channel_id=1, source_target_pairs={{0,64},{64,0},{1,65},{65,1},{2,66},{66,2},{3,67},{67,3},{4,68},{68... | collective-permute-start | bytes 752648 | tf_op jit(solution)/shard_map/ppermute | solution.py:43
  (32 other events, 71.4 us)

commit v7 on v6

--- a/solution.py
+++ b/solution.py
@@ -441,10 +441,10 @@
     early = (0, 4, 1, 3, 6)
     normed = {k: norm_piece(arrived[k], gain_row) for k in early}
     held = [n for k in early for n in normed[k]]
-    (quad,), done = after((quad,), arrived[7], arrived[2], arrived[5], *held)
-    arrived[7], arrived[2], arrived[5] = done[:3]
+    (quad,), done = after((quad,), arrived[7], arrived[2], *held)
+    arrived[7], arrived[2] = done[:2]
     for n, k in enumerate(early):
-        normed[k] = done[3 + 2 * n : 5 + 2 * n]
+        normed[k] = done[2 + 2 * n : 4 + 2 * n]
     other = swap(quad, "core", 1)
     for k in (7, 2, 5):
         normed[k] = norm_piece(arrived[k], gain_row)

time: 148 us -> 155 us (1.047)
  waiting for transfers between devices: 25.4 us -> 34.9 us
  starting transfers between devices: 48.4 us -> 46.7 us
    ppermute x14, waiting for transfers between devices: 10 us -> 19.9 us  [swap_member(): return lax.ppermute(value, MEMBER, [(i, i ^ step) for i in range(8)])]
    dynamic_slice x1 -> x0, local copies, waits for them, and re-layouts: 3.13 us -> none  [on_device(): lax.dynamic_index_in_dim(pieces, member ^ k, 1, keepdims=False)]
    squeeze x0 -> x1, local copies, waits for them, and re-layouts: none -> 3.13 us  [on_device(): lax.dynamic_index_in_dim(pieces, member ^ k, 1, keepdims=False)]
    unnamed x70 -> x64, local copies, waits for them, and re-layouts: 8.84 us -> 7.65 us
  transfers between devices with their start and end apart: 29 -> 29, of which waited for: 14 -> 10; matrix products, arithmetic and copies ran while one was open for 4% -> 4% of each run, Pallas kernels for 15% -> 15%
where the time goes in v7:
time: 155 us
  starting transfers between devices  46.7 us (30%)
  Pallas kernels  44.7 us (29%)
  waiting for transfers between devices  34.9 us (23%)
  blocking collectives  13.7 us (9%)
  local copies, waits for them, and re-layouts  12.3 us (8%)
    ppermute x14, starting transfers between devices, swap_member(): return lax.ppermute(value, MEMBER, [(i, i ^ step) for i in range(8)])  25.1 us
    pallas_call x1, Pallas kernels, middle(): pl.pallas_call(middle_kernel, out_shape=(jax.ShapeDtypeStruct((features,...  20 us
    ppermute x14, waiting for transfers between devices, swap_member(): return lax.ppermute(value, MEMBER, [(i, i ^ step) for i in range(8)])  19.9 us
    ppermute x12, starting transfers between devices, swap(): return lax.ppermute(value, axis, [(i, i ^ step) for i in range(SIZE[axis])])  17 us
    pallas_call x3, Pallas kernels, backward(): pl.pallas_call(functools.partial(backward_kernel, order, [done for done,...  16.8 us
    ppermute x12, waiting for transfers between devices, swap(): return lax.ppermute(value, axis, [(i, i ^ step) for i in range(SIZE[axis])])  15 us
    all_to_all x1, blocking collectives, on_device(): came = lax.all_to_all(send, MEMBER, 0, 0)  13.7 us
    unnamed x64, local copies, waits for them, and re-layouts  7.65 us
  transfers between devices with their start and end apart: 29, of which 10 were waited for; matrix products, arithmetic and copies ran while one was open for 4% of the time, Pallas kernels for 15%

profile of v7, /device:TPU:0, one launch (start us, length us, event | category | flops | bytes accessed | tf_op | source)
XLA Modules:
  0.0 154.7 jit_solution(15622173393868402944)
XLA Ops:
  0.6 1.7 %collective-permute-start = (bf16[12,1120]{1,0:T(8,128)(2,1)}, bf16[12,1120]{1,0:T(8,128)(2,1)S(1)}, u32[]{:S(2)}, u32[]{:S(2)}) collective-permute-start(bf16[12,1120]{1,0:T(8,128)(2,1)} %param.9), channel_id=1, source_target_pairs={{0,1},{1,0},{64,65},{65,64},{2,3},{3,2},{66,67},{67,66},{4,5},{5,4... | collective-permute-start | bytes 80648 | tf_op jit(solution)/shard_map/ppermute | solution.py:47
  2.4 2.2 %collective-permute-start.2 = (bf16[12,1120]{1,0:T(8,128)(2,1)}, bf16[12,1120]{1,0:T(8,128)(2,1)S(1)}, u32[]{:S(2)}, u32[]{:S(2)}) collective-permute-start(bf16[12,1120]{1,0:T(8,128)(2,1)} %param.9), channel_id=1, source_target_pairs={{0,65},{1,64},{64,1},{65,0},{2,67},{3,66},{66,3},{67,2},{4,69},{5,... | collective-permute-start | bytes 80648 | tf_op jit(solution)/shard_map/ppermute | solution.py:47
  5.3 3.1 %dynamic-slice_bitcast_fusion = (bf16[2,64,1536]{2,1,0:T(8,128)(2,1)}, bf16[2,1,64,1536]{3,2,1,0:T(8,128)(2,1)S(1)}, bf16[2,64,1536]{2,1,0:T(8,128)(2,1)}, bf16[...) fusion(bf16[2,8,64,1536]{3,2,1,0:T(8,128)(2,1)} %bitcast.54, ...), kind=kLoop, calls=%fused_computation.7 | loop fusion | bytes 6291488 | tf_op jit(solution)/shard_map/jit(dynamic_index_in_dim)/squeeze | solution.py:402
  8.4 3.0 %collective-permute-start.6 = (bf16[2,64,1536]{2,1,0:T(8,128)(2,1)S(1)}, bf16[2,64,1536]{2,1,0:T(8,128)(2,1)S(1)}, u32[]{:S(2)}, u32[]{:S(2)}) collective-permute-start(bf16[2,64,1536]{2,1,0:T(8,128)(2,1)S(1)} %get-tuple-element.170), channel_id=1, source_target_pairs={{0,4},{1,5},{2,6},{3,7},{4,0},{5,1},{6,2},{7,3},{8,12},{9,13},{10,... | collective-permute-start | bytes 1179656 | tf_op jit(solution)/shard_map/ppermute | solution.py:51
  11.7 1.3 truth.1.truth_ref
  16.1 1.2 collective-permute-start.5
  17.3 1.5 collective-permute-start.4
  18.8 1.4 collective-permute-start.3
  20.3 1.3 collective-permute-start.10
  21.6 5.0 %collective-permute-done.5 = bf16[4,12,1120]{2,1,0:T(8,128)(2,1)S(1)} collective-permute-done((bf16[4,12,1120]{2,1,0:T(8,128)(2,1)S(1)}, bf16[4,12,1120]{2,1,0:T(8,128)(2,1)S(1)}, u32[]{:S(2)}, u32[]{:S(2)}) %collective-permute-start.5) | collective-permute-done | bytes 107552 | tf_op jit(solution)/shard_map/ppermute | solution.py:43
  27.6 2.7 %collective-permute-start.11 = (bf16[2,64,1536]{2,1,0:T(8,128)(2,1)}, bf16[2,64,1536]{2,1,0:T(8,128)(2,1)S(1)}, u32[]{:S(2)}, u32[]{:S(2)}) collective-permute-start(bf16[2,64,1536]{2,1,0:T(8,128)(2,1)} %get-tuple-element.88), channel_id=1, source_target_pairs={{0,6},{1,7},{2,4},{3,5},{4,2},{5,3},{6,0},{7,1},{8,14},{9,15},{10,... | collective-permute-start | bytes 1179656 | tf_op jit(solution)/shard_map/ppermute | solution.py:51
  31.0 4.0 %collective-permute-start.8 = (bf16[2,96,1120]{2,1,0:T(8,128)(2,1)S(1)}, bf16[2,96,1120]{2,1,0:T(8,128)(2,1)S(1)}, u32[]{:S(2)}, u32[]{:S(2)}) collective-permute-start(bf16[2,96,1120]{2,1,0:T(8,128)(2,1)S(1)} %get-tuple-element.177), channel_id=1, source_target_pairs={{0,32},{16,48},{32,0},{48,16},{1,33},{17,49},{33,1},{49,17},{2,34}... | collective-permute-start | bytes 1290248 | tf_op jit(solution)/shard_map/ppermute | solution.py:43
  37.2 2.8 %collective-permute-done.11 = bf16[2,64,1536]{2,1,0:T(8,128)(2,1)S(1)} collective-permute-done((bf16[2,64,1536]{2,1,0:T(8,128)(2,1)}, bf16[2,64,1536]{2,1,0:T(8,128)(2,1)S(1)}, u32[]{:S(2)}, u32[]{:S(2)}) %collective-permute-start.11) | collective-permute-done | bytes 393248 | tf_op jit(solution)/shard_map/ppermute | solution.py:51
  40.0 3.1 %collective-permute-start.12 = (bf16[2,64,1536]{2,1,0:T(8,128)(2,1)S(1)}, bf16[2,64,1536]{2,1,0:T(8,128)(2,1)S(1)}, u32[]{:S(2)}, u32[]{:S(2)}) collective-permute-start(bf16[2,64,1536]{2,1,0:T(8,128)(2,1)S(1)} %copy-done.27), channel_id=1, source_target_pairs={{0,7},{1,6},{2,5},{3,4},{4,3},{5,2},{6,1},{7,0},{8,15},{9,14},{10,... | collective-permute-start | bytes 1179656 | tf_op jit(solution)/shard_map/ppermute | solution.py:51
  47.5 7.4 %collective-permute-done.7 = bf16[2,96,1120]{2,1,0:T(8,128)(2,1)S(1)} collective-permute-done((bf16[2,96,1120]{2,1,0:T(8,128)(2,1)S(1)}, bf16[2,96,1120]{2,1,0:T(8,128)(2,1)S(1)}, u32[]{:S(2)}, u32[]{:S(2)}) %collective-permute-start.7) | collective-permute-done | bytes 430112 | tf_op jit(solution)/shard_map/ppermute | solution.py:43
  56.1 2.3 %collective-permute-start.16 = (bf16[2,64,1536]{2,1,0:T(8,128)(2,1)}, bf16[2,64,1536]{2,1,0:T(8,128)(2,1)}, u32[]{:S(2)}, u32[]{:S(2)}) collective-permute-start(bf16[2,64,1536]{2,1,0:T(8,128)(2,1)} %get-tuple-element.115), channel_id=1, source_target_pairs={{0,5},{1,4},{2,7},{3,6},{4,1},{5,0},{6,3},{7,2},{8,13},{9,12},{10,... | collective-permute-start | bytes 1179656 | tf_op jit(solution)/shard_map/ppermute | solution.py:51
  58.4 11.9 %collective-permute-done.16 = bf16[2,64,1536]{2,1,0:T(8,128)(2,1)} collective-permute-done((bf16[2,64,1536]{2,1,0:T(8,128)(2,1)}, bf16[2,64,1536]{2,1,0:T(8,128)(2,1)}, u32[]{:S(2)}, u32[]{:S(2)}) %collective-permute-start.16) | collective-permute-done | bytes 393248 | tf_op jit(solution)/shard_map/ppermute | solution.py:51
  70.3 1.5 norm.14
  74.4 20.0 %middle.1 = (bf16[1536,1120]{1,0:T(8,128)(2,1)S(1)}, f32[8,96,1120]{2,1,0:T(8,128)S(1)}, bf16[784,1120]{1,0:T(8,128)(2,1)S(1)}, f32[8,512]{1,0:T(8,128)S(1)}, bf...) custom-call(s32[6]{0:T(128)S(1)} %stack.81.place_ref, ...), custom_call_target="tpu_custom_call" | custom-call | flops 20000000000 | bytes 80000000 | tf_op jit(solution)/shard_map/middle/pallas_call | solution.py:359
  95.8 1.7 %collective-permute-start.22 = (bf16[128,1120]{1,0:T(8,128)(2,1)S(1)}, bf16[128,1120]{1,0:T(8,128)(2,1)S(1)}, u32[]{:S(2)}, u32[]{:S(2)}) collective-permute-start(bf16[128,1120]{1,0:T(8,128)(2,1)S(1)} %get-tuple-element.142), channel_id=1, source_target_pairs={{0,4},{1,5},{2,6},{3,7},{4,0},{5,1},{6,2},{7,3},{8,12},{9,13},{10,... | collective-permute-start | bytes 860168 | tf_op jit(solution)/shard_map/ppermute | solution.py:51
  100.3 3.1 %collective-permute-start.19 = (bf16[208,1120]{1,0:T(8,128)(2,1)S(1)}, bf16[208,1120]{1,0:T(8,128)(2,1)S(1)}, u32[]{:S(2)}, u32[]{:S(2)}) collective-permute-start(bf16[208,1120]{1,0:T(8,128)(2,1)S(1)} %get-tuple-element.137), channel_id=1, source_target_pairs={{0,32},{16,48},{32,0},{48,16},{1,33},{17,49},{33,1},{49,17},{2,34}... | collective-permute-start | bytes 1397768 | tf_op jit(solution)/shard_map/ppermute | solution.py:43
  104.0 2.4 %collective-permute-start.23 = (bf16[128,1120]{1,0:T(8,128)(2,1)S(1)}, bf16[128,1120]{1,0:T(8,128)(2,1)S(1)}, u32[]{:S(2)}, u32[]{:S(2)}) collective-permute-start(bf16[128,1120]{1,0:T(8,128)(2,1)S(1)} %get-tuple-element.146), channel_id=1, source_target_pairs={{0,3},{1,2},{2,1},{3,0},{4,7},{5,6},{6,5},{7,4},{8,11},{9,10},{10,... | collective-permute-start | bytes 860168 | tf_op jit(solution)/shard_map/ppermute | solution.py:51
  107.5 5.4 %backward.3.refs_0_ = bf16[3,2,64,1536]{3,2,1,0:T(8,128)(2,1)S(1)} custom-call(s32[6]{0:T(128)S(1)} %stack.81.place_ref, bf16[2,8,64,1536]{3,2,1,0:T(8,128)(2,1)S(1)} %bitcast.55, f32[1,1536]{1,0:T(1,128)S(1)} %reshape.154.gain_ref, bf16[1536,1120]{1,0:T(8,128)(2,1)S(1)} %get-tuple-element.139.full_ref, bf16[128,1120]{1,0:T(8,128)(2,1)S(1)} %get-tuple-element.140.refs_0_, ...), custom_call_target="tpu_custom_call" | custom-call | flops 1000 | bytes 1000 | tf_op jit(solution)/shard_map/backward/pallas_call | solution.py:464
  113.4 2.4 %collective-permute-done.24.refs_1_ = bf16[128,1120]{1,0:T(8,128)(2,1)S(1)} collective-permute-done((bf16[128,1120]{1,0:T(8,128)(2,1)S(1)}, bf16[128,1120]{1,0:T(8,128)(2,1)S(1)}, u32[]{:S(2)}, u32[]{:S(2)}) %collective-permute-start.24) | collective-permute-done | bytes 286752 | tf_op jit(solution)/shard_map/ppermute | solution.py:51
  115.8 1.6 %collective-permute-start.26 = (bf16[128,1120]{1,0:T(8,128)(2,1)S(1)}, bf16[128,1120]{1,0:T(8,128)(2,1)S(1)}, u32[]{:S(2)}, u32[]{:S(2)}) collective-permute-start(bf16[128,1120]{1,0:T(8,128)(2,1)S(1)} %get-tuple-element.156), channel_id=1, source_target_pairs={{0,7},{1,6},{2,5},{3,4},{4,3},{5,2},{6,1},{7,0},{8,15},{9,14},{10,... | collective-permute-start | bytes 860168 | tf_op jit(solution)/shard_map/ppermute | solution.py:51
  117.4 4.2 %backward.4.refs_1_ = bf16[2,2,64,1536]{3,2,1,0:T(8,128)(2,1)S(1)} custom-call(s32[6]{0:T(128)S(1)} %stack.81.place_ref, bf16[2,8,64,1536]{3,2,1,0:T(8,128)(2,1)S(1)} %bitcast.56, f32[1,1536]{1,0:T(1,128)S(1)} %reshape.154.gain_ref, bf16[1536,1120]{1,0:T(8,128)(2,1)S(1)} %get-tuple-element.139.full_ref, ...), custom_call_target="tpu_custom_call" | custom-call | flops 1000 | bytes 1000 | tf_op jit(solution)/shard_map/backward/pallas_call | solution.py:464
  121.6 4.1 %collective-permute-start.28 = (bf16[128,1120]{1,0:T(8,128)(2,1)S(1)}, bf16[128,1120]{1,0:T(8,128)(2,1)S(1)}, u32[]{:S(2)}, u32[]{:S(2)}) collective-permute-start(bf16[128,1120]{1,0:T(8,128)(2,1)S(1)} %get-tuple-element.158), channel_id=1, source_target_pairs={{0,5},{1,4},{2,7},{3,6},{4,1},{5,0},{6,3},{7,2},{8,13},{9,12},{10,... | collective-permute-start | bytes 860168 | tf_op jit(solution)/shard_map/ppermute | solution.py:51
  125.7 1.6 %collective-permute-done.20.c_ref = bf16[208,1120]{1,0:T(8,128)(2,1)S(1)} collective-permute-done((bf16[208,1120]{1,0:T(8,128)(2,1)S(1)}, bf16[208,1120]{1,0:T(8,128)(2,1)S(1)}, u32[]{:S(2)}, u32[]{:S(2)}) %collective-permute-start.20) | collective-permute-done | bytes 465952 | tf_op jit(solution)/shard_map/ppermute | solution.py:43
  127.5 3.0 %collective-permute-start.25 = (bf16[112,1120]{1,0:T(8,128)(2,1)S(1)}, bf16[112,1120]{1,0:T(8,128)(2,1)S(1)}, u32[]{:S(2)}, u32[]{:S(2)}) collective-permute-start(bf16[112,1120]{1,0:T(8,128)(2,1)S(1)} %get-tuple-element.153), channel_id=1, source_target_pairs={{0,64},{64,0},{1,65},{65,1},{2,66},{66,2},{3,67},{67,3},{4,68},{68... | collective-permute-start | bytes 752648 | tf_op jit(solution)/shard_map/ppermute | solution.py:43
  130.5 2.3 %collective-permute-done.28.refs_4_ = bf16[128,1120]{1,0:T(8,128)(2,1)S(1)} collective-permute-done((bf16[128,1120]{1,0:T(8,128)(2,1)S(1)}, bf16[128,1120]{1,0:T(8,128)(2,1)S(1)}, u32[]{:S(2)}, u32[]{:S(2)}) %collective-permute-start.28) | collective-permute-done | bytes 286752 | tf_op jit(solution)/shard_map/ppermute | solution.py:51
  132.8 7.2 %backward.5 = bf16[2,8,64,1536]{3,2,1,0:T(8,128)(2,1)} custom-call(s32[6]{0:T(128)S(1)} %stack.81.place_ref, bf16[2,8,64,1536]{3,2,1,0:T(8,128)(2,1)S(1)} %bitcast.57, f32[1,1536]{1,0:T(1,128)S(1)} %reshape.154.gain_ref, bf16[1536,1120]{1,0:T(8,128)(2,1)S(1)} %get-tuple-element.139.full_ref, bf16[3,2,64,1536]{3,2,1,0:T(8,128)(2,1)S(1)} %backward.3.refs_0_, ...), custom_call_target="tpu_custom_call" | custom-call | flops 1000 | bytes 1000 | tf_op jit(solution)/shard_map/backward/pallas_call | solution.py:464
  140.3 13.7 %all_to_all.5.came_ref = bf16[8,32,1120]{2,1,0:T(8,128)(2,1)S(1)} all-to-all(bf16[8,32,1120]{2,1,0:T(8,128)(2,1)S(1)} %yh_sums.1), channel_id=1, replica_groups=mesh['yh'=2,'z'=4,'core'=2,'x'=4,'yl'=2] {'x','yl'}, dimensions={0} | all-to-all | bytes 1146880 | tf_op jit(solution)/shard_map/all_to_all | solution.py:523
  (129 shorter events, 23.5 us)
Async XLA Ops:
  0.6 10.8 %copy-start = (bf16[70,8,1024]{2,1,0:T(8,128)(2,1)S(1)}, bf16[70,8,1024]{2,1,0:T(8,128)(2,1)}, u32[]{:S(2)}) copy-start(bf16[70,8,1024]{2,1,0:T(8,128)(2,1)} %param.11) | copy-start | bytes 3440644
  0.6 15.4 %collective-permute-start = (bf16[12,1120]{1,0:T(8,128)(2,1)}, bf16[12,1120]{1,0:T(8,128)(2,1)S(1)}, u32[]{:S(2)}, u32[]{:S(2)}) collective-permute-start(bf16[12,1120]{1,0:T(8,128)(2,1)} %param.9), channel_id=1, source_target_pairs={{0,1},{1,0},{64,65},{65,64},{2,3},{3,2},{66,67},{67,66},{4,5},{5,4... | collective-permute-start | bytes 80648 | tf_op jit(solution)/shard_map/ppermute | solution.py:47
  2.4 13.6 %collective-permute-start.2 = (bf16[12,1120]{1,0:T(8,128)(2,1)}, bf16[12,1120]{1,0:T(8,128)(2,1)S(1)}, u32[]{:S(2)}, u32[]{:S(2)}) collective-permute-start(bf16[12,1120]{1,0:T(8,128)(2,1)} %param.9), channel_id=1, source_target_pairs={{0,65},{1,64},{64,1},{65,0},{2,67},{3,66},{66,3},{67,2},{4,69},{5,... | collective-permute-start | bytes 80648 | tf_op jit(solution)/shard_map/ppermute | solution.py:47
  4.6 11.5 %collective-permute-start.1 = (bf16[12,1120]{1,0:T(8,128)(2,1)}, bf16[12,1120]{1,0:T(8,128)(2,1)S(1)}, u32[]{:S(2)}, u32[]{:S(2)}) collective-permute-start(bf16[12,1120]{1,0:T(8,128)(2,1)} %param.9), channel_id=1, source_target_pairs={{0,64},{1,65},{64,0},{65,1},{2,66},{3,67},{66,2},{67,3},{4,68},{5,... | collective-permute-start | bytes 80648 | tf_op jit(solution)/shard_map/ppermute | solution.py:47
  8.4 18.4 %collective-permute-start.6 = (bf16[2,64,1536]{2,1,0:T(8,128)(2,1)S(1)}, bf16[2,64,1536]{2,1,0:T(8,128)(2,1)S(1)}, u32[]{:S(2)}, u32[]{:S(2)}) collective-permute-start(bf16[2,64,1536]{2,1,0:T(8,128)(2,1)S(1)} %get-tuple-element.170), channel_id=1, source_target_pairs={{0,4},{1,5},{2,6},{3,7},{4,0},{5,1},{6,2},{7,3},{8,12},{9,13},{10,... | collective-permute-start | bytes 1179656 | tf_op jit(solution)/shard_map/ppermute | solution.py:51
  15.7 11.4 %copy-start.6 = (bf16[1536,128]{1,0:T(8,128)(2,1)}, bf16[1536,128]{1,0:T(8,128)(2,1)S(1)}, u32[]{:S(2)}) copy-start(bf16[1536,128]{1,0:T(8,128)(2,1)S(1)} %get-tuple-element.120.refs_8_) | copy-start | bytes 1179652
  16.1 10.4 %collective-permute-start.5 = (bf16[4,12,1120]{2,1,0:T(8,128)(2,1)S(1)}, bf16[4,12,1120]{2,1,0:T(8,128)(2,1)S(1)}, u32[]{:S(2)}, u32[]{:S(2)}) collective-permute-start(bf16[4,12,1120]{2,1,0:T(8,128)(2,1)S(1)} %pad_maximum_fusion.3), channel_id=1, source_target_pairs={{0,6},{2,4},{4,2},{6,0},{1,7},{3,5},{5,3},{7,1},{8,14},{10,12},{12... | collective-permute-start | bytes 322568 | tf_op jit(solution)/shard_map/ppermute | solution.py:43
  17.3 9.2 %collective-permute-start.4 = (bf16[4,12,1120]{2,1,0:T(8,128)(2,1)S(1)}, bf16[4,12,1120]{2,1,0:T(8,128)(2,1)S(1)}, u32[]{:S(2)}, u32[]{:S(2)}) collective-permute-start(bf16[4,12,1120]{2,1,0:T(8,128)(2,1)S(1)} %pad_maximum_fusion.3), channel_id=1, source_target_pairs={{0,4},{2,6},{4,0},{6,2},{1,5},{3,7},{5,1},{7,3},{8,12},{10,14},{12... | collective-permute-start | bytes 322568 | tf_op jit(solution)/shard_map/ppermute | solution.py:43
  18.8 7.8 %collective-permute-start.3 = (bf16[4,12,1120]{2,1,0:T(8,128)(2,1)S(1)}, bf16[4,12,1120]{2,1,0:T(8,128)(2,1)S(1)}, u32[]{:S(2)}, u32[]{:S(2)}) collective-permute-start(bf16[4,12,1120]{2,1,0:T(8,128)(2,1)S(1)} %pad_maximum_fusion.3), channel_id=1, source_target_pairs={{0,2},{2,0},{4,6},{6,4},{1,3},{3,1},{5,7},{7,5},{8,10},{10,8},{12,... | collective-permute-start | bytes 322568 | tf_op jit(solution)/shard_map/ppermute | solution.py:43
  20.3 16.9 %collective-permute-start.10 = (bf16[2,64,1536]{2,1,0:T(8,128)(2,1)}, bf16[2,64,1536]{2,1,0:T(8,128)(2,1)S(1)}, u32[]{:S(2)}, u32[]{:S(2)}) collective-permute-start(bf16[2,64,1536]{2,1,0:T(8,128)(2,1)} %get-tuple-element.87), channel_id=1, source_target_pairs={{0,1},{1,0},{2,3},{3,2},{4,5},{5,4},{6,7},{7,6},{8,9},{9,8},{10,11... | collective-permute-start | bytes 1179656 | tf_op jit(solution)/shard_map/ppermute | solution.py:51
  27.6 12.4 %collective-permute-start.11 = (bf16[2,64,1536]{2,1,0:T(8,128)(2,1)}, bf16[2,64,1536]{2,1,0:T(8,128)(2,1)S(1)}, u32[]{:S(2)}, u32[]{:S(2)}) collective-permute-start(bf16[2,64,1536]{2,1,0:T(8,128)(2,1)} %get-tuple-element.88), channel_id=1, source_target_pairs={{0,6},{1,7},{2,4},{3,5},{4,2},{5,3},{6,0},{7,1},{8,14},{9,15},{10,... | collective-permute-start | bytes 1179656 | tf_op jit(solution)/shard_map/ppermute | solution.py:51
  30.3 12.8 %collective-permute-start.14 = (bf16[2,64,1536]{2,1,0:T(8,128)(2,1)S(1)}, bf16[2,64,1536]{2,1,0:T(8,128)(2,1)S(1)}, u32[]{:S(2)}, u32[]{:S(2)}) collective-permute-start(bf16[2,64,1536]{2,1,0:T(8,128)(2,1)S(1)} %get-tuple-element.99), channel_id=1, source_target_pairs={{0,3},{1,2},{2,1},{3,0},{4,7},{5,6},{6,5},{7,4},{8,11},{9,10},{10,... | collective-permute-start | bytes 1179656 | tf_op jit(solution)/shard_map/ppermute | solution.py:51
  31.0 16.6 %collective-permute-start.8 = (bf16[2,96,1120]{2,1,0:T(8,128)(2,1)S(1)}, bf16[2,96,1120]{2,1,0:T(8,128)(2,1)S(1)}, u32[]{:S(2)}, u32[]{:S(2)}) collective-permute-start(bf16[2,96,1120]{2,1,0:T(8,128)(2,1)S(1)} %get-tuple-element.177), channel_id=1, source_target_pairs={{0,32},{16,48},{32,0},{48,16},{1,33},{17,49},{33,1},{49,17},{2,34}... | collective-permute-start | bytes 1290248 | tf_op jit(solution)/shard_map/ppermute | solution.py:43
  34.9 20.0 %collective-permute-start.7 = (bf16[2,96,1120]{2,1,0:T(8,128)(2,1)S(1)}, bf16[2,96,1120]{2,1,0:T(8,128)(2,1)S(1)}, u32[]{:S(2)}, u32[]{:S(2)}) collective-permute-start(bf16[2,96,1120]{2,1,0:T(8,128)(2,1)S(1)} %get-tuple-element.177), channel_id=1, source_target_pairs={{0,16},{16,0},{32,48},{48,32},{1,17},{17,1},{33,49},{49,33},{2,18}... | collective-permute-start | bytes 1290248 | tf_op jit(solution)/shard_map/ppermute | solution.py:43
  37.2 17.8 %collective-permute-start.9 = (bf16[2,96,1120]{2,1,0:T(8,128)(2,1)S(1)}, bf16[2,96,1120]{2,1,0:T(8,128)(2,1)S(1)}, u32[]{:S(2)}, u32[]{:S(2)}) collective-permute-start(bf16[2,96,1120]{2,1,0:T(8,128)(2,1)S(1)} %get-tuple-element.177), channel_id=1, source_target_pairs={{0,48},{16,32},{32,16},{48,0},{1,49},{17,33},{33,17},{49,1},{2,50}... | collective-permute-start | bytes 1290248 | tf_op jit(solution)/shard_map/ppermute | solution.py:43
  40.0 15.3 %collective-permute-start.12 = (bf16[2,64,1536]{2,1,0:T(8,128)(2,1)S(1)}, bf16[2,64,1536]{2,1,0:T(8,128)(2,1)S(1)}, u32[]{:S(2)}, u32[]{:S(2)}) collective-permute-start(bf16[2,64,1536]{2,1,0:T(8,128)(2,1)S(1)} %copy-done.27), channel_id=1, source_target_pairs={{0,7},{1,6},{2,5},{3,4},{4,3},{5,2},{6,1},{7,0},{8,15},{9,14},{10,... | collective-permute-start | bytes 1179656 | tf_op jit(solution)/shard_map/ppermute | solution.py:51
  43.1 12.2 %collective-permute-start.13 = (bf16[2,64,1536]{2,1,0:T(8,128)(2,1)S(1)}, bf16[2,64,1536]{2,1,0:T(8,128)(2,1)S(1)}, u32[]{:S(2)}, u32[]{:S(2)}) collective-permute-start(bf16[2,64,1536]{2,1,0:T(8,128)(2,1)S(1)} %copy-done.26), channel_id=1, source_target_pairs={{0,2},{1,3},{2,0},{3,1},{4,6},{5,7},{6,4},{7,5},{8,10},{9,11},{10,... | collective-permute-start | bytes 1179656 | tf_op jit(solution)/shard_map/ppermute | solution.py:51
  56.0 16.7 %collective-permute-start.15 = (bf16[4,2,96,1120]{3,2,1,0:T(8,128)(2,1)S(1)}, bf16[4,2,96,1120]{3,2,1,0:T(8,128)(2,1)}, u32[]{:S(2)}, u32[]{:S(2)}) collective-permute-start(bf16[4,2,96,1120]{3,2,1,0:T(8,128)(2,1)S(1)} %pad_maximum_fusion.quad_ref), channel_id=1, source_target_pairs={{0,8},{8,0},{1,9},{9,1},{2,10},{10,2},{3,11},{11,3},{4,12},{12,4},... | collective-permute-start | bytes 5160968 | tf_op jit(solution)/shard_map/ppermute | solution.py:43
  56.1 14.2 %collective-permute-start.16 = (bf16[2,64,1536]{2,1,0:T(8,128)(2,1)}, bf16[2,64,1536]{2,1,0:T(8,128)(2,1)}, u32[]{:S(2)}, u32[]{:S(2)}) collective-permute-start(bf16[2,64,1536]{2,1,0:T(8,128)(2,1)} %get-tuple-element.115), channel_id=1, source_target_pairs={{0,5},{1,4},{2,7},{3,6},{4,1},{5,0},{6,3},{7,2},{8,13},{9,12},{10,... | collective-permute-start | bytes 1179656 | tf_op jit(solution)/shard_map/ppermute | solution.py:51
  94.5 3.8 %collective-permute-start.17 = (bf16[784,1120]{1,0:T(8,128)(2,1)S(1)}, bf16[784,1120]{1,0:T(8,128)(2,1)S(1)}, u32[]{:S(2)}, u32[]{:S(2)}) collective-permute-start(bf16[784,1120]{1,0:T(8,128)(2,1)S(1)} %get-tuple-element.130), channel_id=1, source_target_pairs={{0,8},{8,0},{1,9},{9,1},{2,10},{10,2},{3,11},{11,3},{4,12},{12,4},... | collective-permute-start | bytes 5268488 | tf_op jit(solution)/shard_map/ppermute | solution.py:43
  94.5 9.4 %collective-permute-start.21 = (bf16[128,1120]{1,0:T(8,128)(2,1)S(1)}, bf16[128,1120]{1,0:T(8,128)(2,1)S(1)}, u32[]{:S(2)}, u32[]{:S(2)}) collective-permute-start(bf16[128,1120]{1,0:T(8,128)(2,1)S(1)} %get-tuple-element.141), channel_id=1, source_target_pairs={{0,1},{1,0},{2,3},{3,2},{4,5},{5,4},{6,7},{7,6},{8,9},{9,8},{10,11... | collective-permute-start | bytes 860168 | tf_op jit(solution)/shard_map/ppermute | solution.py:51
  95.8 10.6 %collective-permute-start.22 = (bf16[128,1120]{1,0:T(8,128)(2,1)S(1)}, bf16[128,1120]{1,0:T(8,128)(2,1)S(1)}, u32[]{:S(2)}, u32[]{:S(2)}) collective-permute-start(bf16[128,1120]{1,0:T(8,128)(2,1)S(1)} %get-tuple-element.142), channel_id=1, source_target_pairs={{0,4},{1,5},{2,6},{3,7},{4,0},{5,1},{6,2},{7,3},{8,12},{9,13},{10,... | collective-permute-start | bytes 860168 | tf_op jit(solution)/shard_map/ppermute | solution.py:51
  98.3 9.3 %copy-start.1 = (bf16[2,2,256,1536]{3,2,1,0:T(8,128)(2,1)S(1)}, bf16[2,2,256,1536]{3,2,1,0:T(8,128)(2,1)}, u32[]{:S(2)}) copy-start(bf16[2,2,256,1536]{3,2,1,0:T(8,128)(2,1)} %param.7) | copy-start | bytes 9437188
  99.2 22.4 %collective-permute-start.18 = (bf16[208,1120]{1,0:T(8,128)(2,1)S(1)}, bf16[208,1120]{1,0:T(8,128)(2,1)S(1)}, u32[]{:S(2)}, u32[]{:S(2)}) collective-permute-start(bf16[208,1120]{1,0:T(8,128)(2,1)S(1)} %get-tuple-element.136), channel_id=1, source_target_pairs={{0,16},{16,0},{32,48},{48,32},{1,17},{17,1},{33,49},{49,33},{2,18}... | collective-permute-start | bytes 1397768 | tf_op jit(solution)/shard_map/ppermute | solution.py:43
  100.3 25.4 %collective-permute-start.19 = (bf16[208,1120]{1,0:T(8,128)(2,1)S(1)}, bf16[208,1120]{1,0:T(8,128)(2,1)S(1)}, u32[]{:S(2)}, u32[]{:S(2)}) collective-permute-start(bf16[208,1120]{1,0:T(8,128)(2,1)S(1)} %get-tuple-element.137), channel_id=1, source_target_pairs={{0,32},{16,48},{32,0},{48,16},{1,33},{17,49},{33,1},{49,17},{2,34}... | collective-permute-start | bytes 1397768 | tf_op jit(solution)/shard_map/ppermute | solution.py:43
  103.4 23.9 %collective-permute-start.20 = (bf16[208,1120]{1,0:T(8,128)(2,1)S(1)}, bf16[208,1120]{1,0:T(8,128)(2,1)S(1)}, u32[]{:S(2)}, u32[]{:S(2)}) collective-permute-start(bf16[208,1120]{1,0:T(8,128)(2,1)S(1)} %get-tuple-element.138), channel_id=1, source_target_pairs={{0,48},{16,32},{32,16},{48,0},{1,49},{17,33},{33,17},{49,1},{2,50}... | collective-permute-start | bytes 1397768 | tf_op jit(solution)/shard_map/ppermute | solution.py:43
  104.0 9.4 %collective-permute-start.23 = (bf16[128,1120]{1,0:T(8,128)(2,1)S(1)}, bf16[128,1120]{1,0:T(8,128)(2,1)S(1)}, u32[]{:S(2)}, u32[]{:S(2)}) collective-permute-start(bf16[128,1120]{1,0:T(8,128)(2,1)S(1)} %get-tuple-element.146), channel_id=1, source_target_pairs={{0,3},{1,2},{2,1},{3,0},{4,7},{5,6},{6,5},{7,4},{8,11},{9,10},{10,... | collective-permute-start | bytes 860168 | tf_op jit(solution)/shard_map/ppermute | solution.py:51
  106.3 9.5 %collective-permute-start.24 = (bf16[128,1120]{1,0:T(8,128)(2,1)S(1)}, bf16[128,1120]{1,0:T(8,128)(2,1)S(1)}, u32[]{:S(2)}, u32[]{:S(2)}) collective-permute-start(bf16[128,1120]{1,0:T(8,128)(2,1)S(1)} %get-tuple-element.147), channel_id=1, source_target_pairs={{0,6},{1,7},{2,4},{3,5},{4,2},{5,3},{6,0},{7,1},{8,14},{9,15},{10,... | collective-permute-start | bytes 860168 | tf_op jit(solution)/shard_map/ppermute | solution.py:51
  115.8 14.7 %collective-permute-start.26 = (bf16[128,1120]{1,0:T(8,128)(2,1)S(1)}, bf16[128,1120]{1,0:T(8,128)(2,1)S(1)}, u32[]{:S(2)}, u32[]{:S(2)}) collective-permute-start(bf16[128,1120]{1,0:T(8,128)(2,1)S(1)} %get-tuple-element.156), channel_id=1, source_target_pairs={{0,7},{1,6},{2,5},{3,4},{4,3},{5,2},{6,1},{7,0},{8,15},{9,14},{10,... | collective-permute-start | bytes 860168 | tf_op jit(solution)/shard_map/ppermute | solution.py:51
  117.4 13.1 %collective-permute-start.27 = (bf16[128,1120]{1,0:T(8,128)(2,1)S(1)}, bf16[128,1120]{1,0:T(8,128)(2,1)S(1)}, u32[]{:S(2)}, u32[]{:S(2)}) collective-permute-start(bf16[128,1120]{1,0:T(8,128)(2,1)S(1)} %get-tuple-element.157), channel_id=1, source_target_pairs={{0,2},{1,3},{2,0},{3,1},{4,6},{5,7},{6,4},{7,5},{8,10},{9,11},{10,... | collective-permute-start | bytes 860168 | tf_op jit(solution)/shard_map/ppermute | solution.py:51
  121.6 11.2 %collective-permute-start.28 = (bf16[128,1120]{1,0:T(8,128)(2,1)S(1)}, bf16[128,1120]{1,0:T(8,128)(2,1)S(1)}, u32[]{:S(2)}, u32[]{:S(2)}) collective-permute-start(bf16[128,1120]{1,0:T(8,128)(2,1)S(1)} %get-tuple-element.158), channel_id=1, source_target_pairs={{0,5},{1,4},{2,7},{3,6},{4,1},{5,0},{6,3},{7,2},{8,13},{9,12},{10,... | collective-permute-start | bytes 860168 | tf_op jit(solution)/shard_map/ppermute | solution.py:51
  127.5 12.5 %collective-permute-start.25 = (bf16[112,1120]{1,0:T(8,128)(2,1)S(1)}, bf16[112,1120]{1,0:T(8,128)(2,1)S(1)}, u32[]{:S(2)}, u32[]{:S(2)}) collective-permute-start(bf16[112,1120]{1,0:T(8,128)(2,1)S(1)} %get-tuple-element.153), channel_id=1, source_target_pairs={{0,64},{64,0},{1,65},{65,1},{2,66},{66,2},{3,67},{67,3},{4,68},{68... | collective-permute-start | bytes 752648 | tf_op jit(solution)/shard_map/ppermute | solution.py:43
  (29 other events, 57.6 us)
